TPU v7x, 128 devices: a whole 4x4x4 slice. The times are simulated.
128 devices in a mesh: gx: 8 (over z, core), gy: 16 (over x, y).
Axes of the slice: x: 4, y: 4, z: 4, core: 2. Of those that a mesh axis runs over, the one named last changes fastest.
Arguments:
- sensitivity: float32 [3, 1048576], P(None, ('gx', 'gy')), may hold values from -24 to 24
- node_weight: float32 [1048576], P(('gx', 'gy')), may hold values from 0.05 to 0.5
- dest_device: int32 [1048576, 1], P(('gx', 'gy')), may hold values from 0 to 127; in each aligned block of 8192 rows (0 to 8191, 8192 to 16383, ...) at most 128 rows name the same one
- dest_cell: int32 [1048576], P(('gx', 'gy')), may hold values from 0 to 131071
- box_owner: int32 [1048576, 1], P(('gx', 'gy')), may hold values from 0 to 127; in each aligned block of 8192 rows (0 to 8191, 8192 to 16383, ...) at most 128 rows name the same one
- box_slot: int32 [1048576], P(('gx', 'gy')), may hold values from 0 to 63
- stiffness: float32 [128, 512, 256], P('gx', 'gy'), may hold values from 0.5 to 2
- anchor: float32 [3, 128, 512, 256], P(None, 'gx', 'gy'), may hold values from 3 to 6
- coupling: float32 [9, 128, 512, 256], P(None, 'gx', 'gy'), may hold values from -1 to 1
Outputs:
- adjoint: float32 [3, 128, 512, 256], P(None, 'gx', 'gy')
- box_gradient: float32 [3, 8192], P(None, ('gx', 'gy'))
Inputs may be any that keep to these rules, and one draw needn't show every extreme that they name: `dest_device`: among the rows of one device, no deformation device is named more than 128 times, and in some device's rows one is named exactly 128 times. `box_owner`: among the rows of one device, no owner is named more than 128 times, and in some device's rows one is named exactly 128 times.
All inputs are finite; a program needn't handle non-finite values.
Results may differ from a plain program's by a relative error of at most 0.0003.
Values sent between devices are 32-bit elements; how exact they have to be, the bound alone decides.
No kernel may reach another device: no remote copies, remote signals or barrier semaphores. Data moves between devices by JAX's collectives and lax.ppermute only.
A program may use at most 192 MiB of HBM per device.

v0:
```python
import jax
import jax.numpy as jnp
from jax import lax
from jax.sharding import PartitionSpec as P

BOX_DEV = 64
SWEEPS = 4


def extended(cells, sides, width):
    for axis, dim in sides:
        count = lax.axis_size(axis)
        ends = count - 1
        head = lax.slice_in_dim(cells, 0, width, axis=dim)
        tail = lax.slice_in_dim(cells, cells.shape[dim] - width, cells.shape[dim], axis=dim)
        cells = jnp.concatenate(
            [
                lax.ppermute(tail, axis, [(i, (i + 1) % count) for i in range(ends)]),
                cells,
                lax.ppermute(head, axis, [((i + 1) % count, i) for i in range(ends)]),
            ],
            axis=dim,
        )
    return cells


def neighbour_sum(padded):
    z_padded = jnp.pad(padded, ((0, 0), (0, 0), (0, 0), (1, 1)))
    middle = z_padded[:, 1:-1, 1:-1, :]
    total = z_padded[:, 2:, 1:-1, 1:-1] + z_padded[:, :-2, 1:-1, 1:-1]
    total = total + z_padded[:, 1:-1, 2:, 1:-1] + z_padded[:, 1:-1, :-2, 1:-1]
    return total + middle[..., 2:] + middle[..., :-2]


def apply_transposed(field, weighted_pad, stiff, anchor, coupling):
    blocks = coupling.reshape((3, 3) + coupling.shape[1:])
    mixing = jnp.sum(blocks * field[:, None], axis=0)
    return 6.0 * stiff[None] * field - neighbour_sum(weighted_pad) + mixing + anchor * field


def slot_ranks(target, num_targets):
    row_count = target.shape[0]
    block = 128
    num_blocks = row_count // block
    one_hot = (target[:, None] == jnp.arange(num_targets, dtype=jnp.int32)[None, :]).astype(
        jnp.float32
    )
    one_hot = one_hot.reshape(num_blocks, block, num_targets)
    lower = (
        jnp.arange(block, dtype=jnp.int32)[:, None] > jnp.arange(block, dtype=jnp.int32)[None, :]
    ).astype(jnp.float32)
    within = jnp.einsum(
        "ij,bjt->bit",
        lower,
        one_hot,
        precision=lax.Precision.HIGHEST,
        preferred_element_type=jnp.float32,
    )
    totals = jnp.sum(one_hot, axis=1)
    before = jnp.cumsum(totals, axis=0) - totals
    ranks = jnp.sum((within + before[:, None, :]) * one_hot, axis=2)
    return ranks.reshape(row_count).astype(jnp.int32)


def pack_rows(payload, send_slot, total_slots):
    return jnp.zeros((payload.shape[0], total_slots), jnp.float32).at[:, send_slot].set(payload)


def solve_sweeps(load, stiffness, anchor, coupling):
    diagonal = 6.0 * stiffness[None] + anchor + jnp.stack([coupling[0], coupling[4], coupling[8]])
    stiff_pad = extended(stiffness, (("gx", 0), ("gy", 1)), 1)
    adjoint = load / diagonal
    for sweep_idx in range(1, SWEEPS):
        field_pad = extended(adjoint, (("gx", 1), ("gy", 2)), 1)
        weighted = stiff_pad[None] * field_pad
        applied = apply_transposed(adjoint, weighted, stiffness, anchor, coupling)
        adjoint = adjoint + (load - applied) / diagonal
    return adjoint


def body(
    sensitivity,
    node_weight,
    dest_device,
    dest_cell,
    box_owner,
    box_slot,
    stiffness,
    anchor,
    coupling,
):
    devices = lax.axis_size("gx") * lax.axis_size("gy")
    row_count = sensitivity.shape[1]
    capacity = 2 * row_count // devices
    total_slots = devices * capacity
    size_x, size_y, size_z = stiffness.shape
    cells = size_x * size_y * size_z
    target = dest_device[:, 0]
    send_slot = target * capacity + slot_ranks(target, devices)
    cell_float = dest_cell.astype(jnp.float32)
    payload = jnp.concatenate([sensitivity, node_weight[None], cell_float[None]], axis=0)
    arrived = lax.all_to_all(
        pack_rows(payload, send_slot, total_slots),
        ("gx", "gy"),
        split_axis=1,
        concat_axis=1,
        tiled=True,
    )
    cell_ids = arrived[4].astype(jnp.int32)
    load = jnp.zeros((3, cells), jnp.float32).at[:, cell_ids].add(arrived[0:3])
    load = load.reshape(3, size_x, size_y, size_z)
    adjoint = solve_sweeps(load, stiffness, anchor, coupling)
    flat_field = adjoint.reshape(3, cells)
    slot_gradient = arrived[3][None] * flat_field[:, cell_ids]
    returned = lax.all_to_all(slot_gradient, ("gx", "gy"), split_axis=1, concat_axis=1, tiled=True)
    row_gradient = returned[:, send_slot]
    owner_ids = box_owner[:, 0]
    owner_slot = owner_ids * capacity + slot_ranks(owner_ids, devices)
    owner_payload = jnp.concatenate([row_gradient, box_slot.astype(jnp.float32)[None]], axis=0)
    at_owner = lax.all_to_all(
        pack_rows(owner_payload, owner_slot, total_slots),
        ("gx", "gy"),
        split_axis=1,
        concat_axis=1,
        tiled=True,
    )
    box_match = (
        at_owner[3].astype(jnp.int32)[:, None] == jnp.arange(BOX_DEV, dtype=jnp.int32)[None, :]
    ).astype(jnp.float32)
    box_gradient = jnp.dot(
        at_owner[0:3],
        box_match,
        precision=lax.Precision.HIGHEST,
        preferred_element_type=jnp.float32,
    )
    return (adjoint, box_gradient)


def solution(mesh):
    placed = (
        P(None, ("gx", "gy")),
        P(("gx", "gy")),
        P(("gx", "gy"), None),
        P(("gx", "gy")),
        P(("gx", "gy"), None),
        P(("gx", "gy")),
        P("gx", "gy", None),
        P(None, "gx", "gy", None),
        P(None, "gx", "gy", None),
    )
    return jax.shard_map(
        body,
        mesh=mesh,
        in_specs=placed,
        out_specs=(P(None, "gx", "gy", None), P(None, ("gx", "gy"))),
        check_vma=False,
    )
```

profile of v0, /device:TPU:1, one launch (start us, length us, event | category | flops | bytes accessed | tf_op | source)
XLA Modules:
  0.0 1213.5 jit_solution(12051178650008898883)
XLA Ops:
  7.6 24.5 %scatter_custom_fusion = f32[5,16384]{0,1:T(8,128)} fusion(s32[8192]{0:T(1024)S(1)} %bitcast.72, f32[8192,5]{1,0:T(8,128)} %copy.58, f32[]{:T(128)} %constant.6.clone.1), kind=kCustom, calls=%fused_computation.25 | custom fusion | bytes 328192 | tf_op jit(solution)/shard_map/scatter | solution.py:66
  32.1 6.1 copy.59
  38.2 11.5 all-to-all-start
  66.2 7.1 sort
  73.4 8.9 copy.61
  82.3 222.3 %scatter_custom_fusion.1 = f32[3,131072]{0,1:T(8,128)} fusion(s32[16384]{0:T(1024)S(1)} %get-tuple-element.2, f32[]{:T(128)} %constant.6.clone.1, f32[16384,3]{1,0:T(8,128)} %copy.61, s32[16384]{0:T(1024)S(1)} %broadcast_clamp_fusion.1), kind=kCustom, calls=%fused_computation.6 | custom fusion | flops 49152 | bytes 1573376 | tf_op jit(solution)/shard_map/scatter-add | solution.py:110
  304.6 38.4 %copy.62 = f32[3,16,32,256]{3,2,1,0:T(8,128)S(1)} copy(f32[3,16,32,256]{0,3,2,1:T(8,128)} %bitcast.13) | data formatting | bytes 3145728 | tf_op jit(solution)/shard_map/reshape | solution.py:111
  345.3 9.3 collective-permute-start.4
  356.7 3.9 collective-permute-done.5
  360.7 5.4 collective-permute-start.6
  373.9 4.0 collective-permute-start.8
  379.9 4.3 collective-permute-done.9
  401.5 4.0 collective-permute-done.13
  405.6 4.3 collective-permute-start.14
  419.1 33.2 %copy.67 = f32[3,16,32,256]{0,3,2,1:T(8,128)} copy(f32[3,16,32,256]{3,2,1,0:T(8,128)} %fusion.41) | data formatting | bytes 3145728 | tf_op jit(solution)/shard_map/add | solution.py:77
  452.3 456.2 %gather_fusion = f32[16384,3]{1,0:T(8,128)} fusion(f32[3,131072]{0,1:T(8,128)} %bitcast.20, s32[16384]{0:T(1024)S(1)} %broadcast_clamp_fusion), kind=kCustom, calls=%fused_computation | custom fusion | bytes 458752 | tf_op jit(solution)/shard_map/gather | solution.py:114
  908.5 5.5 copy.68
  914.8 197.7 %all-to-all-start.1 = ((f32[3,128,128]{2,0,1:T(4,128)}), f32[3,128,128]{2,0,1:T(4,128)S(1)}, u32[]{:S(2)}, u32[]{:S(2)}) async-start(f32[3,128,128]{2,0,1:T(4,128)} %broadcast_multiply_fusion.1), calls=%async_computation.1 | async-start | bytes 524288 | tf_op jit(solution)/shard_map/all_to_all | solution.py:115
  1112.6 11.0 all-to-all-done.1
  1123.6 4.8 copy.69
  1128.4 31.3 %gather_fusion.1 = f32[8192,3]{1,0:T(8,128)} fusion(f32[3,16384]{0,1:T(8,128)} %bitcast.58, s32[8192]{0:T(1024)S(1)} %broadcast_clamp_fusion.2), kind=kCustom, calls=%fused_computation.1 | custom fusion | bytes 229376 | tf_op jit(solution)/shard_map/gather | solution.py:116
  1165.3 24.5 %scatter_custom_fusion.2 = f32[4,16384]{0,1:T(8,128)} fusion(s32[8192]{0:T(1024)S(1)} %bitcast.78, f32[8192,4]{1,0:T(8,128)} %copy.71, f32[]{:T(128)} %constant.6.clone.1), kind=kCustom, calls=%fused_computation.20 | custom fusion | bytes 262656 | tf_op jit(solution)/shard_map/scatter | solution.py:66
  1189.8 5.5 copy.72
  1195.3 15.2 %all_to_all.27 = f32[4,128,128]{2,0,1:T(4,128)S(1)} all-to-all(f32[4,128,128]{2,0,1:T(4,128)S(1)} %copy.72), channel_id=1, replica_groups=mesh['gx'=8,'gy'=16] {'gx','gy'}, dimensions={1} | all-to-all | bytes 524288 | tf_op jit(solution)/shard_map/all_to_all | solution.py:120
  (113 shorter events, 72.8 us)
Async XLA Ops:
  32.1 17.6 %copy-start.7 = (f32[16,32,256]{2,1,0:T(8,128)S(1)}, f32[16,32,256]{2,1,0:T(8,128)}, u32[]{:S(2)}) copy-start(f32[16,32,256]{2,1,0:T(8,128)} %param.15) | copy-start | bytes 1572868
  38.2 27.8 %all-to-all-start = ((f32[5,128,128]{2,0,1:T(8,128)}), f32[5,128,128]{2,0,1:T(8,128)S(1)}, u32[]{:S(2)}, u32[]{:S(2)}) async-start(f32[5,128,128]{2,0,1:T(8,128)} %copy.59), calls=%async_computation | async-start | bytes 1048576 | tf_op jit(solution)/shard_map/all_to_all | solution.py:102
  49.7 10.6 collective-permute-start
  53.4 7.8 collective-permute-start.1
  61.3 295.3 %collective-permute-start.2 = (f32[18,1,256]{2,1,0:T(1,128)S(1)}, f32[18,1,256]{2,1,0:T(1,128)S(1)}, u32[]{:S(2)}, u32[]{:S(2)}) collective-permute-start(f32[18,1,256]{2,1,0:T(1,128)S(1)} %get-tuple-element.19), channel_id=1, source_target_pairs={{0,1},{1,2},{2,3},{3,4},{4,5},{5,6},{6,7},{7,8},{8,9},{9,10},{10,1... | collective-permute-start | bytes 55304 | tf_op jit(solution)/shard_map/ppermute | solution.py:18
  64.4 292.2 %collective-permute-start.3 = (f32[18,1,256]{2,1,0:T(1,128)S(1)}, f32[18,1,256]{2,1,0:T(1,128)S(1)}, u32[]{:S(2)}, u32[]{:S(2)}) collective-permute-start(f32[18,1,256]{2,1,0:T(1,128)S(1)} %get-tuple-element.20), channel_id=1, source_target_pairs={{1,0},{2,1},{3,2},{4,3},{5,4},{6,5},{7,6},{8,7},{9,8},{10,9},{11,1... | collective-permute-start | bytes 55304 | tf_op jit(solution)/shard_map/ppermute | solution.py:20
  304.6 38.5 %copy-start = (f32[3,16,32,256]{3,2,1,0:T(8,128)S(1)}, f32[3,16,32,256]{3,2,1,0:T(8,128)}, u32[]{:S(2)}) copy-start(f32[3,16,32,256]{3,2,1,0:T(8,128)} %param.16) | copy-start | bytes 4718596
  343.0 24.4 %slice-start = ((s8[4718592]{0:T(1024)(128)(4,1)}), s8[4194304]{0:T(1024)(128)(4,1)S(1)}, s32[]{:S(2)}) async-start(s8[4718592]{0:T(1024)(128)(4,1)} %bitcast.51), calls=%async_computation.3 | async-start | bytes 8388608
  343.0 13.6 %copy-start.6 = (f32[18,32,256]{2,1,0:T(8,128)S(1)}, f32[18,32,256]{2,1,0:T(8,128)}, u32[]{:S(2)}) copy-start(f32[18,32,256]{2,1,0:T(8,128)} %copy-done.5) | copy-start | bytes 1769476
  343.0 24.3 %slice-start.1 = ((s8[4718592]{0:T(1024)(128)(4,1)}), s8[524288]{0:T(1024)(128)(4,1)S(1)}, s32[]{:S(2)}) async-start(s8[4718592]{0:T(1024)(128)(4,1)} %bitcast.51), calls=%async_computation.4 | async-start | bytes 1048576
  345.3 11.4 collective-permute-start.4
  354.7 5.9 collective-permute-start.5
  360.7 7.6 collective-permute-start.6
  366.1 4.9 collective-permute-start.7
  371.4 8.5 copy-start.13
  373.9 6.0 collective-permute-start.8
  377.9 6.3 collective-permute-start.9
  384.3 5.8 collective-permute-start.10
  387.8 5.7 collective-permute-start.11
  396.6 4.9 collective-permute-start.12
  399.6 5.9 collective-permute-start.13
  405.6 6.5 collective-permute-start.14
  409.9 5.3 collective-permute-start.15
  914.8 208.8 %all-to-all-start.1 = ((f32[3,128,128]{2,0,1:T(4,128)}), f32[3,128,128]{2,0,1:T(4,128)S(1)}, u32[]{:S(2)}, u32[]{:S(2)}) async-start(f32[3,128,128]{2,0,1:T(4,128)} %broadcast_multiply_fusion.1), calls=%async_computation.1 | async-start | bytes 524288 | tf_op jit(solution)/shard_map/all_to_all | solution.py:115
  (10 other events, 30.3 us)
where the time goes:
time: 1220 us; the launch traced here: 1210 us
  local copies, waits for them, and re-layouts  650 us (53%)
  starting transfers between devices  259 us (21%)
  other arithmetic  249 us (20%)
  waiting for transfers between devices  32.4 us (3%)
  blocking collectives  15.2 us (1%)
    gather x2, local copies, waits for them, and re-layouts, body(): slot_gradient = arrived[3][None] * flat_field[:, cell_ids]  462 us
    scatter-add x3, other arithmetic, body(): load = jnp.zeros((3, cells), jnp.float32).at[:, cell_ids].add(arrived[0:3])  229 us
    all_to_all x1, starting transfers between devices, body(): lax.all_to_all(slot_gradient, ('gx', 'gy'), split_axis=1, concat_axis=1,...  198 us
    scatter x2, local copies, waits for them, and re-layouts, pack_rows(): jnp.zeros((payload.shape[0], total_slots), jnp.float32).at[:, send_slot]  49.1 us
    reshape x1, local copies, waits for them, and re-layouts, body(): load = load.reshape(3, size_x, size_y, size_z)  38.4 us
    ppermute x8, starting transfers between devices, extended(): lax.ppermute(tail, axis, [(i, (i + 1) % count) for i in range(ends)])  36.3 us
    gather x2, local copies, waits for them, and re-layouts, body(): row_gradient = returned[:, send_slot]  34.1 us
    add x1, local copies, waits for them, and re-layouts, solve_sweeps(): adjoint = adjoint + (load - applied) / diagonal  33.2 us
  transfers between devices with their start and end apart: 18, of which 7 were waited for; matrix products, arithmetic and copies ran while one was open for 24% of the time, Pallas kernels for 0%

commit v1 on v0

v1 whole, which is shorter than its diff:
```python
import jax
import jax.numpy as jnp
from jax import lax
from jax.experimental import pallas as pl
from jax.experimental.pallas import tpu as pltpu
from jax.sharding import PartitionSpec as P

BOX_DEV = 64
SWEEPS = 4
AXES = ("gx", "gy")
STEP_ROWS = 512
MIB = 1024 * 1024


def dot_last(left, right):
    return lax.dot_general(
        left, right, (((1,), (1,)), ((), ())), preferred_element_type=jnp.float32
    )


def halves(values):
    high = values.astype(jnp.bfloat16).astype(jnp.float32)
    return high, values - high


def places(height, width):
    return lax.broadcasted_iota(jnp.int32, (height, width), 0)


def marked(mask, row):
    return jnp.where(mask, row, 0.0).astype(jnp.bfloat16)


def pack_kernel(sens, weight, device, cell, owner, slot, rows, tags, upper, left, right, total):
    devices, _, capacity = rows.shape
    step = upper.shape[0]
    half_cells = float(2**16)
    before = lax.broadcasted_iota(jnp.int32, (step, step), 0)
    after = lax.broadcasted_iota(jnp.int32, (step, step), 1)
    upper[...] = marked(before < after, 1.0)
    total[...] = jnp.zeros_like(total)

    def chunk(i, base):
        at = pl.ds(pl.multiple_of(i * step, step), step)
        named = places(devices, step) == device[:, at]
        ones = jnp.where(named, 1.0, 0.0)
        left[:, :step] = ones.astype(jnp.bfloat16)
        left[:, step:] = ones.astype(jnp.bfloat16)
        within = jnp.dot(left[:, :step], upper[...], preferred_element_type=jnp.float32)
        rank = jnp.sum(jnp.where(named, within + base, 0.0), axis=0, keepdims=True)
        here = places(capacity, step) == rank.astype(jnp.int32)
        own_cell = cell[:, at]
        pairs = [halves(sens[k : k + 1, at]) for k in range(3)]
        pairs.append(
            (
                ((own_cell >> 8) << 8).astype(jnp.float32) - half_cells,
                (own_cell & 255).astype(jnp.float32),
            )
        )
        pairs.append(halves(weight[:, at]))
        pairs.append(((owner[:, at] * BOX_DEV).astype(jnp.float32), slot[:, at].astype(jnp.float32)))
        for p, (high, low) in enumerate(pairs):
            band = slice(p * capacity, (p + 1) * capacity)
            right[band, :step] = marked(here, high)
            right[band, step:] = marked(here, low)
        total[...] += dot_last(left[...], right[...])
        return base + jnp.sum(ones, axis=1, keepdims=True)

    lax.fori_loop(0, sens.shape[1] // step, chunk, jnp.zeros((devices, 1), jnp.float32))
    for p in range(4):
        rows[:, p, :] = total[:, p * capacity : (p + 1) * capacity]
    for p in range(2):
        tags[:, p, :] = total[:, (4 + p) * capacity : (5 + p) * capacity]


def pack(sensitivity, weight, device, cell, owner, slot, devices):
    count = sensitivity.shape[1]
    capacity = 2 * count // devices
    return pl.pallas_call(
        pack_kernel,
        out_shape=(
            jax.ShapeDtypeStruct((devices, 4, capacity), jnp.float32),
            jax.ShapeDtypeStruct((devices, 2, capacity), jnp.float32),
        ),
        scratch_shapes=[
            pltpu.VMEM((STEP_ROWS, STEP_ROWS), jnp.bfloat16),
            pltpu.VMEM((devices, 2 * STEP_ROWS), jnp.bfloat16),
            pltpu.VMEM((6 * capacity, 2 * STEP_ROWS), jnp.bfloat16),
            pltpu.VMEM((devices, 6 * capacity), jnp.float32),
        ],
        compiler_params=pltpu.CompilerParams(vmem_limit_bytes=16 * MIB),
        name="pack_rows",
    )(sensitivity, weight, device, cell, owner, slot)


def cell_parts(row):
    cell = row.astype(jnp.int32) + 2**16
    return cell >> 8, cell & 255


def scatter_kernel(rows, load, left, right):
    height, depth = load.shape[1:]
    sources, _, width = rows.shape
    group = left.shape[1] // 2 // width
    step = group * width
    load[...] = jnp.zeros_like(load)

    def chunk(i, _):
        for q in range(group):
            source = i * group + q
            at = slice(q * width, (q + 1) * width)
            low_at = slice(step + q * width, step + (q + 1) * width)
            line, place = cell_parts(rows[source, 3:4, :])
            hot = marked(places(height, width) == line, 1.0)
            left[:, at] = hot
            left[:, low_at] = hot
            there = places(depth, width) == place
            for k in range(3):
                high, low = halves(rows[source, k : k + 1, :])
                band = slice(k * depth, (k + 1) * depth)
                right[band, at] = marked(there, high)
                right[band, low_at] = marked(there, low)
        for k in range(3):
            load[k] += dot_last(left[...], right[k * depth : (k + 1) * depth, :])
        return 0

    lax.fori_loop(0, sources // group, chunk, 0)


def scatter(rows, height, depth):
    return pl.pallas_call(
        scatter_kernel,
        out_shape=jax.ShapeDtypeStruct((3, height, depth), jnp.float32),
        scratch_shapes=[
            pltpu.VMEM((height, 2 * STEP_ROWS), jnp.bfloat16),
            pltpu.VMEM((3 * depth, 2 * STEP_ROWS), jnp.bfloat16),
        ],
        compiler_params=pltpu.CompilerParams(vmem_limit_bytes=24 * MIB),
        name="scatter_rows",
    )(rows)


def sweep_kernel(last, field, load, inverse, stiff, coupling, west, east, south, north, *outs):
    _, size_x, size_y, size_z = field.shape
    padded = outs[-1]
    result = outs[0]
    padded[:, 0] = west[...]
    padded[:, size_x + 1] = east[...]
    for x in range(size_x):
        for k in range(3):
            padded[k, x + 1] = stiff[x] * field[k, x]
    row = lax.broadcasted_iota(jnp.int32, (size_y, size_z), 0)
    column = lax.broadcasted_iota(jnp.int32, (size_y, size_z), 1)
    for x in range(size_x):
        own = [field[k, x] for k in range(3)]
        for k in range(3):
            middle = padded[k, x + 1]
            total = load[k, x] + padded[k, x] + padded[k, x + 2]
            total = total + jnp.where(row == 0, south[k, x : x + 1], pltpu.roll(middle, 1, 0))
            total = total + jnp.where(
                row == size_y - 1, north[k, x : x + 1], pltpu.roll(middle, size_y - 1, 0)
            )
            total = total + jnp.where(column == 0, 0.0, pltpu.roll(middle, 1, 1))
            total = total + jnp.where(
                column == size_z - 1, 0.0, pltpu.roll(middle, size_z - 1, 1)
            )
            for j in range(3):
                if j != k:
                    total = total - coupling[3 * j + k, x] * own[j]
            fresh = total * inverse[k, x]
            result[k, x] = fresh
            if not last:
                head_x, tail_x, head_y, tail_y = outs[1:5]
                moved = stiff[x] * fresh
                if x == 0:
                    head_x[k] = moved
                if x == size_x - 1:
                    tail_x[k] = moved
                head_y[k, x : x + 1] = moved[:1]
                tail_y[k, x : x + 1] = moved[size_y - 1 :]


def sweep(last, field, load, inverse, stiff, coupling, halo):
    _, size_x, size_y, size_z = field.shape
    shapes = [field.shape]
    if not last:
        shapes += [(3, size_y, size_z)] * 2 + [(3, size_x, size_z)] * 2

    def kernel(*refs):
        sweep_kernel(last, *refs)

    return pl.pallas_call(
        kernel,
        out_shape=[jax.ShapeDtypeStruct(shape, jnp.float32) for shape in shapes],
        scratch_shapes=[pltpu.VMEM((3, size_x + 2, size_y, size_z), jnp.float32)],
        compiler_params=pltpu.CompilerParams(vmem_limit_bytes=24 * MIB),
        name="sweep_cells",
    )(field, load, inverse, stiff, coupling, *halo)


def exchange(head_x, tail_x, head_y, tail_y):
    def shifted(face, axis, up):
        pairs = [(i, i + 1) if up else (i + 1, i) for i in range(lax.axis_size(axis) - 1)]
        return lax.ppermute(face, axis, pairs)

    return (
        shifted(tail_x, "gx", True),
        shifted(head_x, "gx", False),
        shifted(tail_y, "gy", True),
        shifted(head_y, "gy", False),
    )


def gather_kernel(field, rows, tags, boxes, turned, hot, left, right, total):
    height, depth = field.shape[1:]
    sources, _, width = rows.shape
    group = hot.shape[1] // width
    step = group * width
    for k in range(3):
        high, low = halves(field[k].T)
        turned[k * depth : (k + 1) * depth, :height] = high.astype(jnp.bfloat16)
        turned[k * depth : (k + 1) * depth, height:] = low.astype(jnp.bfloat16)
    total[...] = jnp.zeros_like(total)
    right[...] = jnp.zeros_like(right)

    def chunk(i, _):
        for q in range(group):
            line, _ = cell_parts(rows[i * group + q, 3:4, :])
            ones = marked(places(height, width) == line, 1.0)
            hot[:height, q * width : (q + 1) * width] = ones
            hot[height:, q * width : (q + 1) * width] = ones
        parts = [
            jnp.dot(
                turned[k * depth : (k + 1) * depth, :], hot[...], preferred_element_type=jnp.float32
            )
            for k in range(3)
        ]
        for q in range(group):
            source = i * group + q
            at = slice(q * width, (q + 1) * width)
            low_at = slice(step + q * width, step + (q + 1) * width)
            _, place = cell_parts(rows[source, 3:4, :])
            there = places(depth, width) == place
            weight = tags[source, 0:1, :]
            box = tags[source, 1:2, :].astype(jnp.int32)
            owned = marked(places(left.shape[0], width) == box // BOX_DEV, 1.0)
            left[:, at] = owned
            left[:, low_at] = owned
            inside = places(BOX_DEV, width) == box % BOX_DEV
            for k in range(3):
                picked = jnp.sum(jnp.where(there, parts[k][:, at], 0.0), axis=0, keepdims=True)
                high, low = halves(picked * weight)
                band = slice(k * BOX_DEV, (k + 1) * BOX_DEV)
                right[band, at] = marked(inside, high)
                right[band, low_at] = marked(inside, low)
        total[...] += dot_last(left[...], right[...])
        return 0

    lax.fori_loop(0, sources // group, chunk, 0)
    for p in range(2):
        boxes[:, p, :] = total[:, p * 128 : (p + 1) * 128]


def gather(field, rows, tags):
    height, depth = field.shape[1:]
    devices = rows.shape[0]
    return pl.pallas_call(
        gather_kernel,
        out_shape=jax.ShapeDtypeStruct((devices, 2, 128), jnp.float32),
        scratch_shapes=[
            pltpu.VMEM((3 * depth, 2 * height), jnp.bfloat16),
            pltpu.VMEM((2 * height, STEP_ROWS), jnp.bfloat16),
            pltpu.VMEM((devices, 2 * STEP_ROWS), jnp.bfloat16),
            pltpu.VMEM((4 * BOX_DEV, 2 * STEP_ROWS), jnp.bfloat16),
            pltpu.VMEM((devices, 4 * BOX_DEV), jnp.float32),
        ],
        compiler_params=pltpu.CompilerParams(vmem_limit_bytes=24 * MIB),
        name="gather_rows",
    )(field, rows, tags)


def swapped(blocks):
    return lax.all_to_all(blocks, AXES, split_axis=0, concat_axis=0, tiled=True)


def body(
    sensitivity,
    node_weight,
    dest_device,
    dest_cell,
    box_owner,
    box_slot,
    stiffness,
    anchor,
    coupling,
):
    devices = lax.axis_size("gx") * lax.axis_size("gy")
    count = sensitivity.shape[1]
    size_x, size_y, size_z = stiffness.shape
    lane = lambda values: values.reshape(1, count)
    rows, tags = pack(
        sensitivity,
        lane(node_weight),
        lane(dest_device),
        lane(dest_cell),
        lane(box_owner),
        lane(box_slot),
        devices,
    )
    rows = swapped(rows)
    tags = swapped(tags)
    diagonal = 6.0 * stiffness[None] + anchor + jnp.stack([coupling[0], coupling[4], coupling[8]])
    inverse = 1.0 / diagonal
    load = scatter(rows, size_x * size_y, size_z).reshape(3, size_x, size_y, size_z)
    field = load * inverse
    moved = stiffness[None] * field
    faces = (moved[:, 0], moved[:, -1], moved[:, :, 0], moved[:, :, -1])
    for turn in range(1, SWEEPS):
        last = turn == SWEEPS - 1
        field, *faces = sweep(
            last, field, load, inverse, stiffness, coupling, exchange(*faces)
        )
    partial = gather(field.reshape(3, size_x * size_y, size_z), rows, tags)
    summed = jnp.sum(swapped(partial), axis=0).reshape(4, BOX_DEV)
    return (field, summed[:3])


def solution(mesh):
    placed = (
        P(None, AXES),
        P(AXES),
        P(AXES, None),
        P(AXES),
        P(AXES, None),
        P(AXES),
        P("gx", "gy", None),
        P(None, "gx", "gy", None),
        P(None, "gx", "gy", None),
    )
    return jax.shard_map(
        body,
        mesh=mesh,
        in_specs=placed,
        out_specs=(P(None, "gx", "gy", None), P(None, AXES)),
        check_vma=False,
    )
```

time: 1220 us -> 219 us (0.18)
  local copies, waits for them, and re-layouts: 650 us -> 16.1 us
  other arithmetic: 249 us -> 3.5 us
  starting transfers between devices: 259 us -> 50.9 us
  Pallas kernels: 0 us -> 109 us
  waiting for transfers between devices: 32.4 us -> 15.3 us
    gather x4 -> x0, local copies, waits for them, and re-layouts: 496 us -> none  [the longest x2 462 us: body(): slot_gradient = arrived[3][None] * flat_field[:, cell_ids]]
    scatter-add x3 -> x0, other arithmetic: 229 us -> none  [body(): load = jnp.zeros((3, cells), jnp.float32).at[:, cell_ids].add(arrived[0:3])]
    all_to_all x2, starting transfers between devices: 209 us -> 22.7 us  [swapped(): return lax.all_to_all(blocks, AXES, split_axis=0, concat_axis=0, tiled=True)]
    pallas_call x0 -> x6, Pallas kernels: none -> 109 us  [the longest x1 49 us: gather(): pl.pallas_call(gather_kernel, out_shape=jax.ShapeDtypeStruct((devices, 2,...]
    scatter x2 -> x0, local copies, waits for them, and re-layouts: 49.1 us -> none  [pack_rows(): jnp.zeros((payload.shape[0], total_slots), jnp.float32).at[:, send_slot]]
    reshape x1, local copies, waits for them, and re-layouts: 38.4 us -> 0.66 us  [body(): summed = jnp.sum(swapped(partial), axis=0).reshape(4, BOX_DEV)]
    add x1 -> x0, local copies, waits for them, and re-layouts: 33.2 us -> none  [solve_sweeps(): adjoint = adjoint + (load - applied) / diagonal]
    ppermute x16 -> x12, starting transfers between devices: 49.4 us -> 28.2 us  [shifted(): return lax.ppermute(face, axis, pairs)]
  transfers between devices with their start and end apart: 18 -> 14, of which waited for: 7 -> 4; matrix products, arithmetic and copies ran while one was open for 24% -> 2% of each run, Pallas kernels for 0% -> 2%
where the time goes in v1:
time: 219 us; the launch traced here: 218 us
  Pallas kernels  109 us (50%)
  starting transfers between devices  50.9 us (23%)
  blocking collectives  22.5 us (10%)
  local copies, waits for them, and re-layouts  16.1 us (7%)
  waiting for transfers between devices  15.3 us (7%)
  other arithmetic  3.5 us (2%)
    pallas_call x1, Pallas kernels, gather(): pl.pallas_call(gather_kernel, out_shape=jax.ShapeDtypeStruct((devices, 2,...  49 us
    pallas_call x1, Pallas kernels, scatter(): pl.pallas_call(scatter_kernel, out_shape=jax.ShapeDtypeStruct((3, height,...  38.2 us
    ppermute x12, starting transfers between devices, shifted(): return lax.ppermute(face, axis, pairs)  28.2 us
    all_to_all x2, starting transfers between devices, swapped(): return lax.all_to_all(blocks, AXES, split_axis=0, concat_axis=0, tiled=True)  22.7 us
    all_to_all x1, blocking collectives, swapped(): return lax.all_to_all(blocks, AXES, split_axis=0, concat_axis=0, tiled=True)  22.5 us
    pallas_call x1, Pallas kernels, pack(): pl.pallas_call(pack_kernel, out_shape=(jax.ShapeDtypeStruct((devices, 4,...  15.1 us
    unnamed x40, local copies, waits for them, and re-layouts  12.7 us
    all_to_all x2, waiting for transfers between devices, swapped(): return lax.all_to_all(blocks, AXES, split_axis=0, concat_axis=0, tiled=True)  7.69 us
  transfers between devices with their start and end apart: 14, of which 4 were waited for; matrix products, arithmetic and copies ran while one was open for 2% of the time, Pallas kernels for 2%

profile of v1, /device:TPU:1, one launch (start us, length us, event | category | flops | bytes accessed | tf_op | source)
XLA Modules:
  0.0 217.8 jit_solution(4941962215227540070)
XLA Ops:
  5.3 15.1 %pack_rows.1 = (f32[128,4,128]{2,1,0:T(4,128)}, f32[128,2,128]{2,1,0:T(2,128)S(1)}) custom-call(f32[3,8192]{1,0:T(4,128)S(1)} %copy-done.7, f32[1,8192]{1,0:T(1,128)S(1)} %bitcast.25, s32[1,8192]{1,0:T(1,128)S(1)} %bitcast.26, s32[1,8192]{1,0:T(1,128)S(1)} %bitcast.27, s32[1,8192]{1,0:T(1,128)S(1)} %bitcast.28, s32[1,8192]{1,0:T(1,128)S(1)} %bitcast.29), custom_call_target="tpu_custom_call" | custom-call | tf_op jit(solution)/shard_map/pack_rows/pallas_call | solution.py:79
  21.1 11.5 %all-to-all-start = ((f32[128,4,128]{2,1,0:T(4,128)}), f32[128,4,128]{2,1,0:T(4,128)S(1)}, u32[]{:S(2)}, u32[]{:S(2)}) async-start(f32[128,4,128]{2,1,0:T(4,128)} %get-tuple-element.14), calls=%async_computation | async-start | bytes 524288 | tf_op jit(solution)/shard_map/all_to_all | solution.py:283
  32.6 2.6 %fusion.2 = (f32[1,16,32,256]{3,2,1,0:T(8,128)}, f32[1,16,32,256]{3,2,1,0:T(8,128)}, f32[1,16,32,256]{3,2,1,0:T(8,128)}) fusion(f32[9,16,32,256]{3,2,1,0:T(8,128)} %refs_4_.5), kind=kLoop, calls=%fused_computation.8 | loop fusion | bytes 3145728 | tf_op jit(solution)/shard_map/slice | solution.py:312
  36.0 7.7 %all-to-all-done.rows = f32[128,4,128]{2,1,0:T(4,128)S(1)} async-done(((f32[128,4,128]{2,1,0:T(4,128)}), f32[128,4,128]{2,1,0:T(4,128)S(1)}, u32[]{:S(2)}, u32[]{:S(2)}) %all-to-all-start) | async-done | bytes 262176 | tf_op jit(solution)/shard_map/all_to_all | solution.py:283
  43.7 38.2 %scatter_rows.1 = f32[3,512,256]{2,1,0:T(8,128)S(1)} custom-call(f32[128,4,128]{2,1,0:T(4,128)S(1)} %all-to-all-done.rows), custom_call_target="tpu_custom_call" | custom-call | tf_op jit(solution)/shard_map/scatter_rows/pallas_call | solution.py:131
  82.0 2.5 %broadcast_multiply_fusion = (f32[3,16,32,256]{3,2,1,0:T(8,128)S(1)}, f32[3,16,32,256]{3,2,1,0:T(8,128)S(1)}, f32[3,16,32,256]{3,2,1,0:T(8,128)S(1)}) fusion(f32[16,32,256]{2,1,0:T(8,128)} %refs_3_.5, f32[3,16,32,256]{3,2,1,0:T(8,128)S(1)} %bitcast.20, f32[1,16,32,256]{3,2,1,0:T(8,128)S(1)} %copy-done.16, f32[1,16,32,256]{3,2,1,0:T(8,128)} %get-tuple-element.31, ...), kind=kLoop, calls=%fused_computation.2 | loop fusion | flops 2752512 | bytes 10485760 | tf_op jit(solution)/shard_map/mul | solution.py:316
  84.5 2.7 %collective-permute-start.1 = (f32[3,32,256]{2,1,0:T(8,128)S(1)}, f32[3,32,256]{2,1,0:T(8,128)S(1)}, u32[]{:S(2)}, u32[]{:S(2)}) collective-permute-start(f32[3,32,256]{2,1,0:T(8,128)S(1)} %get-tuple-element.34), channel_id=1, source_target_pairs={{16,0},{32,16},{48,32},{64,48},{80,64},{96,80},{112,96},{17,1},{33... | collective-permute-start | bytes 294920 | tf_op jit(solution)/shard_map/ppermute | solution.py:204
  87.2 2.9 %collective-permute-start = (f32[3,32,256]{2,1,0:T(8,128)S(1)}, f32[3,32,256]{2,1,0:T(8,128)S(1)}, u32[]{:S(2)}, u32[]{:S(2)}) collective-permute-start(f32[3,32,256]{2,1,0:T(8,128)S(1)} %get-tuple-element.35), channel_id=1, source_target_pairs={{0,16},{16,32},{32,48},{48,64},{64,80},{80,96},{96,112},{1,17},{17... | collective-permute-start | bytes 294920 | tf_op jit(solution)/shard_map/ppermute | solution.py:204
  90.2 2.3 %collective-permute-start.2 = (f32[3,16,256]{2,1,0:T(8,128)S(1)}, f32[3,16,256]{2,1,0:T(8,128)S(1)}, u32[]{:S(2)}, u32[]{:S(2)}) collective-permute-start(f32[3,16,256]{2,1,0:T(8,128)S(1)} %bitcast.31), channel_id=1, source_target_pairs={{0,1},{1,2},{2,3},{3,4},{4,5},{5,6},{6,7},{7,8},{8,9},{9,10},{10,1... | collective-permute-start | bytes 147464 | tf_op jit(solution)/shard_map/ppermute | solution.py:204
  94.0 3.8 %collective-permute-done.3.refs_8_ = f32[3,16,256]{2,1,0:T(8,128)S(1)} collective-permute-done((f32[3,16,256]{2,1,0:T(8,128)S(1)}, f32[3,16,256]{2,1,0:T(8,128)S(1)}, u32[]{:S(2)}, u32[]{:S(2)}) %collective-permute-start.3) | collective-permute-done | bytes 49184 | tf_op jit(solution)/shard_map/ppermute | solution.py:204
  97.9 2.0 sweep_cells.3
  101.0 2.8 %collective-permute-start.4 = (f32[3,32,256]{2,1,0:T(8,128)}, f32[3,32,256]{2,1,0:T(8,128)}, u32[]{:S(2)}, u32[]{:S(2)}) collective-permute-start(f32[3,32,256]{2,1,0:T(8,128)} %get-tuple-element.16), channel_id=1, source_target_pairs={{0,16},{16,32},{32,48},{48,64},{64,80},{80,96},{96,112},{1,17},{17... | collective-permute-start | bytes 294920 | tf_op jit(solution)/shard_map/ppermute | solution.py:204
  103.9 2.1 collective-permute-start.5
  106.0 2.8 %collective-permute-start.6 = (f32[3,16,256]{2,1,0:T(8,128)}, f32[3,16,256]{2,1,0:T(8,128)}, u32[]{:S(2)}, u32[]{:S(2)}) collective-permute-start(f32[3,16,256]{2,1,0:T(8,128)} %get-tuple-element.18), channel_id=1, source_target_pairs={{0,1},{1,2},{2,3},{3,4},{4,5},{5,6},{6,7},{7,8},{8,9},{9,10},{10,1... | collective-permute-start | bytes 147464 | tf_op jit(solution)/shard_map/ppermute | solution.py:204
  110.1 11.2 %all-to-all-start.1 = ((f32[128,2,128]{2,1,0:T(2,128)}), f32[128,2,128]{2,1,0:T(2,128)S(1)}, u32[]{:S(2)}, u32[]{:S(2)}) async-start(f32[128,2,128]{2,1,0:T(2,128)} %copy-done.8), calls=%async_computation.1 | async-start | bytes 262144 | tf_op jit(solution)/shard_map/all_to_all | solution.py:283
  121.3 2.3 %copy-done = f32[9,16,32,256]{3,2,1,0:T(8,128)S(1)} copy-done((f32[9,16,32,256]{3,2,1,0:T(8,128)S(1)}, f32[9,16,32,256]{3,2,1,0:T(8,128)}, u32[]{:S(2)}) %copy-start) | copy-done | bytes 4718616
  126.1 2.1 sweep_cells.4
  128.3 3.7 %collective-permute-start.8 = (f32[3,32,256]{2,1,0:T(8,128)S(1)}, f32[3,32,256]{2,1,0:T(8,128)S(1)}, u32[]{:S(2)}, u32[]{:S(2)}) collective-permute-start(f32[3,32,256]{2,1,0:T(8,128)S(1)} %get-tuple-element.21), channel_id=1, source_target_pairs={{0,16},{16,32},{32,48},{48,64},{64,80},{80,96},{96,112},{1,17},{17... | collective-permute-start | bytes 294920 | tf_op jit(solution)/shard_map/ppermute | solution.py:204
  131.9 1.9 collective-permute-start.9
  133.9 3.2 %collective-permute-start.10 = (f32[3,16,256]{2,1,0:T(8,128)S(1)}, f32[3,16,256]{2,1,0:T(8,128)S(1)}, u32[]{:S(2)}, u32[]{:S(2)}) collective-permute-start(f32[3,16,256]{2,1,0:T(8,128)S(1)} %get-tuple-element.23), channel_id=1, source_target_pairs={{0,1},{1,2},{2,3},{3,4},{4,5},{5,6},{6,7},{7,8},{8,9},{9,10},{10,1... | collective-permute-start | bytes 147464 | tf_op jit(solution)/shard_map/ppermute | solution.py:204
  138.3 3.5 %collective-permute-done.11.refs_8_ = f32[3,16,256]{2,1,0:T(8,128)S(1)} collective-permute-done((f32[3,16,256]{2,1,0:T(8,128)S(1)}, f32[3,16,256]{2,1,0:T(8,128)S(1)}, u32[]{:S(2)}, u32[]{:S(2)}) %collective-permute-start.11) | collective-permute-done | bytes 49184 | tf_op jit(solution)/shard_map/ppermute | solution.py:204
  141.9 2.3 %sweep_cells.5 = f32[3,16,32,256]{3,2,1,0:T(8,128)} custom-call(f32[3,16,32,256]{3,2,1,0:T(8,128)S(1)} %get-tuple-element.20.refs_0_, f32[3,16,32,256]{3,2,1,0:T(8,128)S(1)} %bitcast.23, f32[3,16,32,256]{3,2,1,0:T(8,128)S(1)} %get-tuple-element.28.refs_2_, f32[16,32,256]{2,1,0:T(8,128)S(1)} %copy-done.3, f32[9,16,32,256]{3,2,1,0:T(8,128)S(1)} %copy-done, ...), custom_call_target="tpu_custom_call" | custom-call | tf_op jit(solution)/shard_map/sweep_cells/pallas_call | solution.py:192
  145.5 49.0 %gather_rows.1 = f32[128,2,128]{2,1,0:T(2,128)S(1)} custom-call(f32[3,512,256]{2,1,0:T(8,128)S(1)} %bitcast.24, f32[128,4,128]{2,1,0:T(4,128)S(1)} %all-to-all-done.rows, f32[128,2,128]{2,1,0:T(2,128)S(1)} %all-to-all-done.1.tags), custom_call_target="tpu_custom_call" | custom-call | tf_op jit(solution)/shard_map/gather_rows/pallas_call | solution.py:267
  194.5 22.5 %all_to_all.15 = f32[128,2,128]{2,1,0:T(2,128)S(1)} all-to-all(f32[128,2,128]{2,1,0:T(2,128)S(1)} %gather_rows.1), channel_id=1, replica_groups=mesh['gx'=8,'gy'=16] {'gx','gy'}, dimensions={0} | all-to-all | bytes 262144 | tf_op jit(solution)/shard_map/all_to_all | solution.py:283
  (59 shorter events, 16.2 us)
Async XLA Ops:
  21.1 22.7 %all-to-all-start = ((f32[128,4,128]{2,1,0:T(4,128)}), f32[128,4,128]{2,1,0:T(4,128)S(1)}, u32[]{:S(2)}, u32[]{:S(2)}) async-start(f32[128,4,128]{2,1,0:T(4,128)} %get-tuple-element.14), calls=%async_computation | async-start | bytes 524288 | tf_op jit(solution)/shard_map/all_to_all | solution.py:283
  32.6 2.6 %copy-start.1 = (f32[16,32,256]{2,1,0:T(8,128)S(1)}, f32[16,32,256]{2,1,0:T(8,128)}, u32[]{:S(2)}) copy-start(f32[16,32,256]{2,1,0:T(8,128)} %refs_3_.5) | copy-start | bytes 1572868
  43.7 38.2 %copy-start.14 = (f32[16,32,256]{2,1,0:T(8,128)S(1)}, f32[16,32,256]{2,1,0:T(8,128)}, u32[]{:S(2)}) copy-start(f32[16,32,256]{2,1,0:T(8,128)} %broadcast_multiply_fusion.1) | copy-start | bytes 1572868
  43.7 38.2 %copy-start.15 = (f32[1,16,32,256]{3,2,1,0:T(8,128)S(1)}, f32[1,16,32,256]{3,2,1,0:T(8,128)}, u32[]{:S(2)}) copy-start(f32[1,16,32,256]{3,2,1,0:T(8,128)} %get-tuple-element.29) | copy-start | bytes 1572868
  43.7 38.2 %copy-start.16 = (f32[1,16,32,256]{3,2,1,0:T(8,128)S(1)}, f32[1,16,32,256]{3,2,1,0:T(8,128)}, u32[]{:S(2)}) copy-start(f32[1,16,32,256]{3,2,1,0:T(8,128)} %get-tuple-element.30) | copy-start | bytes 1572868
  81.9 15.9 %slice-start = ((s8[4718592]{0:T(1024)(128)(4,1)}), s8[4194304]{0:T(1024)(128)(4,1)S(1)}, s32[]{:S(2)}) async-start(s8[4718592]{0:T(1024)(128)(4,1)} %bitcast.18), calls=%async_computation.3 | async-start | bytes 8388608
  81.9 15.9 %slice-start.1 = ((s8[4718592]{0:T(1024)(128)(4,1)}), s8[524288]{0:T(1024)(128)(4,1)S(1)}, s32[]{:S(2)}) async-start(s8[4718592]{0:T(1024)(128)(4,1)} %bitcast.18), calls=%async_computation.4 | async-start | bytes 1048576
  82.0 15.9 %copy-start.2 = (f32[16,32,256]{2,1,0:T(8,128)S(1)}, f32[16,32,256]{2,1,0:T(8,128)}, u32[]{:S(2)}) copy-start(f32[16,32,256]{2,1,0:T(8,128)} %refs_3_.5) | copy-start | bytes 1572868
  84.5 13.3 %collective-permute-start.1 = (f32[3,32,256]{2,1,0:T(8,128)S(1)}, f32[3,32,256]{2,1,0:T(8,128)S(1)}, u32[]{:S(2)}, u32[]{:S(2)}) collective-permute-start(f32[3,32,256]{2,1,0:T(8,128)S(1)} %get-tuple-element.34), channel_id=1, source_target_pairs={{16,0},{32,16},{48,32},{64,48},{80,64},{96,80},{112,96},{17,1},{33... | collective-permute-start | bytes 294920 | tf_op jit(solution)/shard_map/ppermute | solution.py:204
  87.2 10.6 %collective-permute-start = (f32[3,32,256]{2,1,0:T(8,128)S(1)}, f32[3,32,256]{2,1,0:T(8,128)S(1)}, u32[]{:S(2)}, u32[]{:S(2)}) collective-permute-start(f32[3,32,256]{2,1,0:T(8,128)S(1)} %get-tuple-element.35), channel_id=1, source_target_pairs={{0,16},{16,32},{32,48},{48,64},{64,80},{80,96},{96,112},{1,17},{17... | collective-permute-start | bytes 294920 | tf_op jit(solution)/shard_map/ppermute | solution.py:204
  90.2 3.8 %collective-permute-start.2 = (f32[3,16,256]{2,1,0:T(8,128)S(1)}, f32[3,16,256]{2,1,0:T(8,128)S(1)}, u32[]{:S(2)}, u32[]{:S(2)}) collective-permute-start(f32[3,16,256]{2,1,0:T(8,128)S(1)} %bitcast.31), channel_id=1, source_target_pairs={{0,1},{1,2},{2,3},{3,4},{4,5},{5,6},{6,7},{7,8},{8,9},{9,10},{10,1... | collective-permute-start | bytes 147464 | tf_op jit(solution)/shard_map/ppermute | solution.py:204
  92.5 5.4 %collective-permute-start.3 = (f32[3,16,256]{2,1,0:T(8,128)S(1)}, f32[3,16,256]{2,1,0:T(8,128)S(1)}, u32[]{:S(2)}, u32[]{:S(2)}) collective-permute-start(f32[3,16,256]{2,1,0:T(8,128)S(1)} %bitcast.30), channel_id=1, source_target_pairs={{1,0},{2,1},{3,2},{4,3},{5,4},{6,5},{7,6},{8,7},{9,8},{10,9},{11,1... | collective-permute-start | bytes 147464 | tf_op jit(solution)/shard_map/ppermute | solution.py:204
  101.0 20.3 %collective-permute-start.4 = (f32[3,32,256]{2,1,0:T(8,128)}, f32[3,32,256]{2,1,0:T(8,128)}, u32[]{:S(2)}, u32[]{:S(2)}) collective-permute-start(f32[3,32,256]{2,1,0:T(8,128)} %get-tuple-element.16), channel_id=1, source_target_pairs={{0,16},{16,32},{32,48},{48,64},{64,80},{80,96},{96,112},{1,17},{17... | collective-permute-start | bytes 294920 | tf_op jit(solution)/shard_map/ppermute | solution.py:204
  103.9 17.4 %collective-permute-start.5 = (f32[3,32,256]{2,1,0:T(8,128)}, f32[3,32,256]{2,1,0:T(8,128)}, u32[]{:S(2)}, u32[]{:S(2)}) collective-permute-start(f32[3,32,256]{2,1,0:T(8,128)} %get-tuple-element.17), channel_id=1, source_target_pairs={{16,0},{32,16},{48,32},{64,48},{80,64},{96,80},{112,96},{17,1},{33... | collective-permute-start | bytes 294920 | tf_op jit(solution)/shard_map/ppermute | solution.py:204
  106.0 15.3 %collective-permute-start.6 = (f32[3,16,256]{2,1,0:T(8,128)}, f32[3,16,256]{2,1,0:T(8,128)}, u32[]{:S(2)}, u32[]{:S(2)}) collective-permute-start(f32[3,16,256]{2,1,0:T(8,128)} %get-tuple-element.18), channel_id=1, source_target_pairs={{0,1},{1,2},{2,3},{3,4},{4,5},{5,6},{6,7},{7,8},{8,9},{9,10},{10,1... | collective-permute-start | bytes 147464 | tf_op jit(solution)/shard_map/ppermute | solution.py:204
  108.8 12.5 %collective-permute-start.7 = (f32[3,16,256]{2,1,0:T(8,128)}, f32[3,16,256]{2,1,0:T(8,128)}, u32[]{:S(2)}, u32[]{:S(2)}) collective-permute-start(f32[3,16,256]{2,1,0:T(8,128)} %get-tuple-element.19), channel_id=1, source_target_pairs={{1,0},{2,1},{3,2},{4,3},{5,4},{6,5},{7,6},{8,7},{9,8},{10,9},{11,1... | collective-permute-start | bytes 147464 | tf_op jit(solution)/shard_map/ppermute | solution.py:204
  110.1 34.0 %all-to-all-start.1 = ((f32[128,2,128]{2,1,0:T(2,128)}), f32[128,2,128]{2,1,0:T(2,128)S(1)}, u32[]{:S(2)}, u32[]{:S(2)}) async-start(f32[128,2,128]{2,1,0:T(2,128)} %copy-done.8), calls=%async_computation.1 | async-start | bytes 262144 | tf_op jit(solution)/shard_map/all_to_all | solution.py:283
  121.3 2.3 %copy-start = (f32[9,16,32,256]{3,2,1,0:T(8,128)S(1)}, f32[9,16,32,256]{3,2,1,0:T(8,128)}, u32[]{:S(2)}) copy-start(f32[9,16,32,256]{3,2,1,0:T(8,128)} %refs_4_.5) | copy-start | bytes 14155780
  124.7 1.4 copy-start.6
  128.3 13.6 %collective-permute-start.8 = (f32[3,32,256]{2,1,0:T(8,128)S(1)}, f32[3,32,256]{2,1,0:T(8,128)S(1)}, u32[]{:S(2)}, u32[]{:S(2)}) collective-permute-start(f32[3,32,256]{2,1,0:T(8,128)S(1)} %get-tuple-element.21), channel_id=1, source_target_pairs={{0,16},{16,32},{32,48},{48,64},{64,80},{80,96},{96,112},{1,17},{17... | collective-permute-start | bytes 294920 | tf_op jit(solution)/shard_map/ppermute | solution.py:204
  131.9 9.9 %collective-permute-start.9 = (f32[3,32,256]{2,1,0:T(8,128)S(1)}, f32[3,32,256]{2,1,0:T(8,128)S(1)}, u32[]{:S(2)}, u32[]{:S(2)}) collective-permute-start(f32[3,32,256]{2,1,0:T(8,128)S(1)} %get-tuple-element.22), channel_id=1, source_target_pairs={{16,0},{32,16},{48,32},{64,48},{80,64},{96,80},{112,96},{17,1},{33... | collective-permute-start | bytes 294920 | tf_op jit(solution)/shard_map/ppermute | solution.py:204
  133.9 4.5 %collective-permute-start.10 = (f32[3,16,256]{2,1,0:T(8,128)S(1)}, f32[3,16,256]{2,1,0:T(8,128)S(1)}, u32[]{:S(2)}, u32[]{:S(2)}) collective-permute-start(f32[3,16,256]{2,1,0:T(8,128)S(1)} %get-tuple-element.23), channel_id=1, source_target_pairs={{0,1},{1,2},{2,3},{3,4},{4,5},{5,6},{6,7},{7,8},{8,9},{9,10},{10,1... | collective-permute-start | bytes 147464 | tf_op jit(solution)/shard_map/ppermute | solution.py:204
  137.0 4.8 %collective-permute-start.11 = (f32[3,16,256]{2,1,0:T(8,128)S(1)}, f32[3,16,256]{2,1,0:T(8,128)S(1)}, u32[]{:S(2)}, u32[]{:S(2)}) collective-permute-start(f32[3,16,256]{2,1,0:T(8,128)S(1)} %get-tuple-element.24), channel_id=1, source_target_pairs={{1,0},{2,1},{3,2},{4,3},{5,4},{6,5},{7,6},{8,7},{9,8},{10,9},{11,1... | collective-permute-start | bytes 147464 | tf_op jit(solution)/shard_map/ppermute | solution.py:204
  144.1 1.4 copy-start.4
  (9 other events, 7.5 us)

commit v2 on v1

--- a/solution.py
+++ b/solution.py
@@ -9,6 +9,8 @@
 SWEEPS = 4
 AXES = ("gx", "gy")
 STEP_ROWS = 512
+WINDOW = 32
+CELL_SHIFT = 257
 MIB = 1024 * 1024
 
 
@@ -31,10 +33,9 @@
     return jnp.where(mask, row, 0.0).astype(jnp.bfloat16)
 
 
-def pack_kernel(sens, weight, device, cell, owner, slot, rows, tags, upper, left, right, total):
+def pack_kernel(sens, weight, device, cell, owner, slot, rows, upper, left, right, total):
     devices, _, capacity = rows.shape
     step = upper.shape[0]
-    half_cells = float(2**16)
     before = lax.broadcasted_iota(jnp.int32, (step, step), 0)
     after = lax.broadcasted_iota(jnp.int32, (step, step), 1)
     upper[...] = marked(before < after, 1.0)
@@ -53,8 +54,8 @@
         pairs = [halves(sens[k : k + 1, at]) for k in range(3)]
         pairs.append(
             (
-                ((own_cell >> 8) << 8).astype(jnp.float32) - half_cells,
-                (own_cell & 255).astype(jnp.float32),
+                (((own_cell >> 9) + 1) << 9).astype(jnp.float32),
+                ((own_cell & 511) + (CELL_SHIFT - 512)).astype(jnp.float32),
             )
         )
         pairs.append(halves(weight[:, at]))
@@ -67,10 +68,10 @@
         return base + jnp.sum(ones, axis=1, keepdims=True)
 
     lax.fori_loop(0, sens.shape[1] // step, chunk, jnp.zeros((devices, 1), jnp.float32))
-    for p in range(4):
+    for p in range(6):
         rows[:, p, :] = total[:, p * capacity : (p + 1) * capacity]
-    for p in range(2):
-        tags[:, p, :] = total[:, (4 + p) * capacity : (5 + p) * capacity]
+    for p in range(6, 8):
+        rows[:, p, :] = jnp.zeros((devices, capacity), jnp.float32)
 
 
 def pack(sensitivity, weight, device, cell, owner, slot, devices):
@@ -78,10 +79,7 @@
     capacity = 2 * count // devices
     return pl.pallas_call(
         pack_kernel,
-        out_shape=(
-            jax.ShapeDtypeStruct((devices, 4, capacity), jnp.float32),
-            jax.ShapeDtypeStruct((devices, 2, capacity), jnp.float32),
-        ),
+        out_shape=jax.ShapeDtypeStruct((devices, 8, capacity), jnp.float32),
         scratch_shapes=[
             pltpu.VMEM((STEP_ROWS, STEP_ROWS), jnp.bfloat16),
             pltpu.VMEM((devices, 2 * STEP_ROWS), jnp.bfloat16),
@@ -93,51 +91,76 @@
     )(sensitivity, weight, device, cell, owner, slot)
 
 
-def cell_parts(row):
-    cell = row.astype(jnp.int32) + 2**16
-    return cell >> 8, cell & 255
-
-
-def scatter_kernel(rows, load, left, right):
+def windows(ends, i):
+    first = jnp.maximum(ends[0, i] >> 8, 0)
+    start = first & ~7
+    return start, (jnp.maximum((ends[1, i] >> 8) + WINDOW - start, 0)) // WINDOW
+
+
+def scatter_kernel(ends, cells, one, two, three, load, left, right):
     height, depth = load.shape[1:]
-    sources, _, width = rows.shape
-    group = left.shape[1] // 2 // width
-    step = group * width
+    lines, width = cells.shape
+    half = depth // 2
+    group = STEP_ROWS // width
+    step = STEP_ROWS
     load[...] = jnp.zeros_like(load)
 
     def chunk(i, _):
         for q in range(group):
-            source = i * group + q
-            at = slice(q * width, (q + 1) * width)
-            low_at = slice(step + q * width, step + (q + 1) * width)
-            line, place = cell_parts(rows[source, 3:4, :])
-            hot = marked(places(height, width) == line, 1.0)
-            left[:, at] = hot
-            left[:, low_at] = hot
-            there = places(depth, width) == place
+            row = pl.ds(i * group + q, 1)
+            place = cells[row, :] & (half - 1)
+            there = places(half, width) == place
+            for k, sens in enumerate((one, two, three)):
+                high, low = halves(sens[row, :])
+                band = slice(k * half, (k + 1) * half)
+                right[band, q * width : (q + 1) * width] = marked(there, high)
+                right[band, step + q * width : step + (q + 1) * width] = marked(there, low)
+        start, count = windows(ends, i)
+
+        def window(w, _):
+            least = start + w * WINDOW
+            base = pl.multiple_of(jnp.minimum(least, height - WINDOW), 8)
+            for q in range(group):
+                cell = cells[pl.ds(i * group + q, 1), :]
+                hot = marked(places(2 * WINDOW, width) == window_place(cell, least, base), 1.0)
+                left[:, q * width : (q + 1) * width] = hot
+                left[:, step + q * width : step + (q + 1) * width] = hot
+            sums = dot_last(left[...], right[...])
             for k in range(3):
-                high, low = halves(rows[source, k : k + 1, :])
-                band = slice(k * depth, (k + 1) * depth)
-                right[band, at] = marked(there, high)
-                right[band, low_at] = marked(there, low)
-        for k in range(3):
-            load[k] += dot_last(left[...], right[k * depth : (k + 1) * depth, :])
+                for side in range(2):
+                    at = (k, pl.ds(base, WINDOW), slice(side * half, (side + 1) * half))
+                    load[at] += sums[
+                        side * WINDOW : (side + 1) * WINDOW, k * half : (k + 1) * half
+                    ]
+            return 0
+
+        lax.fori_loop(0, count, window, 0)
         return 0
 
-    lax.fori_loop(0, sources // group, chunk, 0)
-
-
-def scatter(rows, height, depth):
+    lax.fori_loop(0, lines // group, chunk, 0)
+
+
+def window_place(cell, least, base):
+    line = cell >> 8
+    place = ((cell >> 7) & 1) * WINDOW + line - base
+    inside = (line >= least) & (line < base + WINDOW)
+    return jnp.where(inside, place, -1)
+
+
+def scatter(ends, cells, values, height, depth):
+    vmem = pl.BlockSpec(memory_space=pltpu.VMEM)
     return pl.pallas_call(
         scatter_kernel,
+        in_specs=[pl.BlockSpec(memory_space=pltpu.SMEM)] + [vmem] * 4,
+        out_specs=vmem,
         out_shape=jax.ShapeDtypeStruct((3, height, depth), jnp.float32),
         scratch_shapes=[
-            pltpu.VMEM((height, 2 * STEP_ROWS), jnp.bfloat16),
-            pltpu.VMEM((3 * depth, 2 * STEP_ROWS), jnp.bfloat16),
+            pltpu.VMEM((2 * WINDOW, 2 * STEP_ROWS), jnp.bfloat16),
+            pltpu.VMEM((3 * depth // 2, 2 * STEP_ROWS), jnp.bfloat16),
         ],
-        compiler_params=pltpu.CompilerParams(vmem_limit_bytes=24 * MIB),
+        compiler_params=pltpu.CompilerParams(vmem_limit_bytes=16 * MIB),
         name="scatter_rows",
-    )(rows)
+    )(ends, cells, *values)
 
 
 def sweep_kernel(last, field, load, inverse, stiff, coupling, west, east, south, north, *outs):
@@ -211,72 +234,83 @@
     )
 
 
-def gather_kernel(field, rows, tags, boxes, turned, hot, left, right, total):
+def gather_kernel(ends, field, cells, weights, boxes, sums, hot, left, right, total):
     height, depth = field.shape[1:]
-    sources, _, width = rows.shape
-    group = hot.shape[1] // width
-    step = group * width
-    for k in range(3):
-        high, low = halves(field[k].T)
-        turned[k * depth : (k + 1) * depth, :height] = high.astype(jnp.bfloat16)
-        turned[k * depth : (k + 1) * depth, height:] = low.astype(jnp.bfloat16)
+    lines, width = cells.shape
+    half = depth // 2
+    group = STEP_ROWS // width
+    step = STEP_ROWS
     total[...] = jnp.zeros_like(total)
     right[...] = jnp.zeros_like(right)
 
     def chunk(i, _):
+        rows = [pl.ds(i * group + q, 1) for q in range(group)]
+        there = jnp.concatenate(
+            [places(half, width) == (cells[row, :] & (half - 1)) for row in rows], axis=1
+        )
+        start, count = windows(ends, i)
+
+        def window(w, picked):
+            least = start + w * WINDOW
+            base = pl.multiple_of(jnp.minimum(least, height - WINDOW), 8)
+            for q in range(group):
+                place = window_place(cells[rows[q], :], least, base)
+                ones = marked(places(2 * WINDOW, width) == place, 1.0)
+                hot[: 2 * WINDOW, q * width : (q + 1) * width] = ones
+                hot[2 * WINDOW :, q * width : (q + 1) * width] = ones
+            fresh = []
+            for k in range(3):
+                block = field[k, pl.ds(base, WINDOW), :]
+                block = jnp.concatenate([block[:, :half], block[:, half:]], axis=0)
+                high, low = halves(block)
+                both = jnp.concatenate([high, low], axis=0).T.astype(jnp.bfloat16)
+                part = jnp.dot(both, hot[...], preferred_element_type=jnp.float32)
+                fresh.append(
+                    picked[k] + jnp.sum(jnp.where(there, part, 0.0), axis=0, keepdims=True)
+                )
+            return tuple(fresh)
+
+        picked = lax.fori_loop(
+            0, count, window, tuple(jnp.zeros((1, step), jnp.float32) for k in range(3))
+        )
         for q in range(group):
-            line, _ = cell_parts(rows[i * group + q, 3:4, :])
-            ones = marked(places(height, width) == line, 1.0)
-            hot[:height, q * width : (q + 1) * width] = ones
-            hot[height:, q * width : (q + 1) * width] = ones
-        parts = [
-            jnp.dot(
-                turned[k * depth : (k + 1) * depth, :], hot[...], preferred_element_type=jnp.float32
-            )
-            for k in range(3)
-        ]
-        for q in range(group):
-            source = i * group + q
             at = slice(q * width, (q + 1) * width)
             low_at = slice(step + q * width, step + (q + 1) * width)
-            _, place = cell_parts(rows[source, 3:4, :])
-            there = places(depth, width) == place
-            weight = tags[source, 0:1, :]
-            box = tags[source, 1:2, :].astype(jnp.int32)
+            weight = weights[rows[q], :]
+            box = boxes[rows[q], :].astype(jnp.int32)
             owned = marked(places(left.shape[0], width) == box // BOX_DEV, 1.0)
             left[:, at] = owned
             left[:, low_at] = owned
             inside = places(BOX_DEV, width) == box % BOX_DEV
             for k in range(3):
-                picked = jnp.sum(jnp.where(there, parts[k][:, at], 0.0), axis=0, keepdims=True)
-                high, low = halves(picked * weight)
+                high, low = halves(picked[k][:, at] * weight)
                 band = slice(k * BOX_DEV, (k + 1) * BOX_DEV)
                 right[band, at] = marked(inside, high)
                 right[band, low_at] = marked(inside, low)
         total[...] += dot_last(left[...], right[...])
         return 0
 
-    lax.fori_loop(0, sources // group, chunk, 0)
+    lax.fori_loop(0, lines // group, chunk, 0)
     for p in range(2):
-        boxes[:, p, :] = total[:, p * 128 : (p + 1) * 128]
-
-
-def gather(field, rows, tags):
-    height, depth = field.shape[1:]
-    devices = rows.shape[0]
+        sums[:, p, :] = total[:, p * 128 : (p + 1) * 128]
+
+
+def gather(ends, field, cells, weights, boxes, devices):
+    vmem = pl.BlockSpec(memory_space=pltpu.VMEM)
     return pl.pallas_call(
         gather_kernel,
+        in_specs=[pl.BlockSpec(memory_space=pltpu.SMEM)] + [vmem] * 4,
+        out_specs=vmem,
         out_shape=jax.ShapeDtypeStruct((devices, 2, 128), jnp.float32),
         scratch_shapes=[
-            pltpu.VMEM((3 * depth, 2 * height), jnp.bfloat16),
-            pltpu.VMEM((2 * height, STEP_ROWS), jnp.bfloat16),
+            pltpu.VMEM((4 * WINDOW, STEP_ROWS), jnp.bfloat16),
             pltpu.VMEM((devices, 2 * STEP_ROWS), jnp.bfloat16),
             pltpu.VMEM((4 * BOX_DEV, 2 * STEP_ROWS), jnp.bfloat16),
             pltpu.VMEM((devices, 4 * BOX_DEV), jnp.float32),
         ],
-        compiler_params=pltpu.CompilerParams(vmem_limit_bytes=24 * MIB),
+        compiler_params=pltpu.CompilerParams(vmem_limit_bytes=16 * MIB),
         name="gather_rows",
-    )(field, rows, tags)
+    )(ends, field, cells, weights, boxes)
 
 
 def swapped(blocks):
@@ -298,7 +332,7 @@
     count = sensitivity.shape[1]
     size_x, size_y, size_z = stiffness.shape
     lane = lambda values: values.reshape(1, count)
-    rows, tags = pack(
+    rows = pack(
         sensitivity,
         lane(node_weight),
         lane(dest_device),
@@ -308,10 +342,15 @@
         devices,
     )
     rows = swapped(rows)
-    tags = swapped(tags)
+    planes = [rows[:, p].reshape(-1) for p in range(6)]
+    keys = jnp.maximum(planes[3].astype(jnp.int32) - CELL_SHIFT, -1)
+    ordered = lax.sort((keys, *planes[:3], *planes[4:]), num_keys=1, is_stable=False)
+    cells, *values, weights, boxes = [part.reshape(-1, 128) for part in ordered]
+    blocks = cells.reshape(-1, STEP_ROWS // 128, 128)
+    ends = jnp.stack([blocks[:, 0, 0], blocks[:, -1, -1]])
     diagonal = 6.0 * stiffness[None] + anchor + jnp.stack([coupling[0], coupling[4], coupling[8]])
     inverse = 1.0 / diagonal
-    load = scatter(rows, size_x * size_y, size_z).reshape(3, size_x, size_y, size_z)
+    load = scatter(ends, cells, values, size_x * size_y, size_z).reshape(3, size_x, size_y, size_z)
     field = load * inverse
     moved = stiffness[None] * field
     faces = (moved[:, 0], moved[:, -1], moved[:, :, 0], moved[:, :, -1])
@@ -320,7 +359,8 @@
         field, *faces = sweep(
             last, field, load, inverse, stiffness, coupling, exchange(*faces)
         )
-    partial = gather(field.reshape(3, size_x * size_y, size_z), rows, tags)
+    flat = field.reshape(3, size_x * size_y, size_z)
+    partial = gather(ends, flat, cells, weights, boxes, devices)
     summed = jnp.sum(swapped(partial), axis=0).reshape(4, BOX_DEV)
     return (field, summed[:3])
 

time: 219 us -> 173 us (0.79)
  Pallas kernels: 109 us -> 54.7 us
  other arithmetic: 3.5 us -> 14.1 us
  waiting for transfers between devices: 15.3 us -> 22.8 us
  starting transfers between devices: 50.9 us -> 44.8 us
  local copies, waits for them, and re-layouts: 16.1 us -> 10.6 us
    pallas_call x3, Pallas kernels: 102 us -> 49.7 us  [the longest x1 20 us: gather(): pl.pallas_call(gather_kernel, in_specs=[pl.BlockSpec(memory_space=pltpu.S...]
    sort x0 -> x1, other arithmetic: none -> 12.6 us  [body(): lax.sort((keys, *planes[:3], *planes[4:]), num_keys=1, is_stable=False)]
    all_to_all x2 -> x1, starting transfers between devices: 22.7 us -> 11.5 us  [swapped(): return lax.all_to_all(blocks, AXES, split_axis=0, concat_axis=0, tiled=True)]
    unnamed x40 -> x24, local copies, waits for them, and re-layouts: 12.7 us -> 6.18 us
    ppermute x12, starting transfers between devices: 28.2 us -> 33.3 us  [shifted(): return lax.ppermute(face, axis, pairs)]
    all_to_all x2 -> x1, waiting for transfers between devices: 7.69 us -> 11.8 us  [swapped(): return lax.all_to_all(blocks, AXES, split_axis=0, concat_axis=0, tiled=True)]
    ppermute x12, waiting for transfers between devices: 7.6 us -> 11 us  [shifted(): return lax.ppermute(face, axis, pairs)]
  transfers between devices with their start and end apart: 14 -> 13, of which waited for: 4 -> 4; matrix products, arithmetic and copies ran while one was open for 2% -> 1% of each run, Pallas kernels for 2% -> 0%
where the time goes in v2:
time: 173 us; the launch traced here: 172 us
  Pallas kernels  54.7 us (32%)
  starting transfers between devices  44.8 us (26%)
  blocking collectives  24.1 us (14%)
  waiting for transfers between devices  22.8 us (13%)
  other arithmetic  14.1 us (8%)
  local copies, waits for them, and re-layouts  10.6 us (6%)
    ppermute x12, starting transfers between devices, shifted(): return lax.ppermute(face, axis, pairs)  33.3 us
    all_to_all x1, blocking collectives, swapped(): return lax.all_to_all(blocks, AXES, split_axis=0, concat_axis=0, tiled=True)  24.1 us
    pallas_call x1, Pallas kernels, gather(): pl.pallas_call(gather_kernel, in_specs=[pl.BlockSpec(memory_space=pltpu.S...  20 us
    pallas_call x1, Pallas kernels, pack(): pl.pallas_call(pack_kernel, out_shape=jax.ShapeDtypeStruct((devices, 8, c...  15.3 us
    pallas_call x1, Pallas kernels, scatter(): pl.pallas_call(scatter_kernel, in_specs=[pl.BlockSpec(memory_space=pltpu....  14.4 us
    sort x1, other arithmetic, body(): lax.sort((keys, *planes[:3], *planes[4:]), num_keys=1, is_stable=False)  12.6 us
    all_to_all x1, waiting for transfers between devices, swapped(): return lax.all_to_all(blocks, AXES, split_axis=0, concat_axis=0, tiled=True)  11.8 us
    all_to_all x1, starting transfers between devices, swapped(): return lax.all_to_all(blocks, AXES, split_axis=0, concat_axis=0, tiled=True)  11.5 us
  transfers between devices with their start and end apart: 13, of which 4 were waited for; matrix products, arithmetic and copies ran while one was open for 1% of the time, Pallas kernels for 0%

profile of v2, /device:TPU:1, one launch (start us, length us, event | category | flops | bytes accessed | tf_op | source)
XLA Modules:
  0.0 172.2 jit_solution(8275551876943944952)
XLA Ops:
  5.4 15.3 %pack_rows.1 = f32[128,8,128]{2,1,0:T(8,128)} custom-call(f32[3,8192]{1,0:T(4,128)S(1)} %copy-done.2, f32[1,8192]{1,0:T(1,128)S(1)} %bitcast.48, s32[1,8192]{1,0:T(1,128)S(1)} %bitcast.49, s32[1,8192]{1,0:T(1,128)S(1)} %bitcast.50, s32[1,8192]{1,0:T(1,128)S(1)} %bitcast.51, s32[1,8192]{1,0:T(1,128)S(1)} %bitcast.52), custom_call_target="tpu_custom_call" | custom-call | tf_op jit(solution)/shard_map/pack_rows/pallas_call | solution.py:80
  20.7 11.5 %all-to-all-start = ((f32[128,8,128]{2,1,0:T(8,128)}), f32[128,8,128]{2,1,0:T(8,128)S(1)}, u32[]{:S(2)}, u32[]{:S(2)}) async-start(f32[128,8,128]{2,1,0:T(8,128)} %pack_rows.1), calls=%async_computation | async-start | bytes 1048576 | tf_op jit(solution)/shard_map/all_to_all | solution.py:317
  32.3 1.5 fusion.4
  33.7 11.8 %all-to-all-done = f32[128,8,128]{2,1,0:T(8,128)S(1)} async-done(((f32[128,8,128]{2,1,0:T(8,128)}), f32[128,8,128]{2,1,0:T(8,128)S(1)}, u32[]{:S(2)}, u32[]{:S(2)}) %all-to-all-start) | async-done | bytes 524320 | tf_op jit(solution)/shard_map/all_to_all | solution.py:317
  47.2 12.6 %sort.39 = (s32[16384]{0:T(1024)S(1)}, f32[16384]{0:T(1024)S(1)}, f32[16384]{0:T(1024)S(1)}, f32[16384]{0:T(1024)S(1)}, f32[16384]{0:T(1024)S(1)}, /*index=5*/f32[16384]{0:T(1024)S(1)}) sort(s32[16384]{0:T(1024)} %bitcast.58, f32[16384]{0:T(1024)} %bitcast.57, f32[16384]{0:T(1024)} %bitcast.56, f32[16384]{0:T(1024)} %bitcast.55, f32[16384]{0:T(1024)} %bitcast.54, ...), dimensions={0}, to_apply=%region_0.0 | sort | flops 229376 | bytes 786432 | tf_op jit(solution)/shard_map/sort | solution.py:347
  61.1 14.4 %scatter_rows.1 = f32[3,512,256]{2,1,0:T(8,128)S(1)} custom-call(s32[2,32]{1,0:T(2,128)S(1)} %pad_add_fusion.ends, s32[128,128]{1,0:T(8,128)S(1)} %bitcast.41, f32[128,128]{1,0:T(8,128)S(1)} %bitcast.45, f32[128,128]{1,0:T(8,128)S(1)} %bitcast.46, f32[128,128]{1,0:T(8,128)S(1)} %bitcast.47), custom_call_target="tpu_custom_call" | custom-call | tf_op jit(solution)/shard_map/scatter_rows/pallas_call | solution.py:152
  76.2 3.4 %collective-permute-start.1 = (f32[3,32,256]{2,1,0:T(8,128)S(1)}, f32[3,32,256]{2,1,0:T(8,128)S(1)}, u32[]{:S(2)}, u32[]{:S(2)}) collective-permute-start(f32[3,32,256]{2,1,0:T(8,128)S(1)} %get-tuple-element.44), channel_id=1, source_target_pairs={{16,0},{32,16},{48,32},{64,48},{80,64},{96,80},{112,96},{17,1},{33... | collective-permute-start | bytes 294920 | tf_op jit(solution)/shard_map/ppermute | solution.py:227
  79.6 3.8 %collective-permute-start = (f32[3,32,256]{2,1,0:T(8,128)S(1)}, f32[3,32,256]{2,1,0:T(8,128)S(1)}, u32[]{:S(2)}, u32[]{:S(2)}) collective-permute-start(f32[3,32,256]{2,1,0:T(8,128)S(1)} %get-tuple-element.45), channel_id=1, source_target_pairs={{0,16},{16,32},{32,48},{48,64},{64,80},{80,96},{96,112},{1,17},{17... | collective-permute-start | bytes 294920 | tf_op jit(solution)/shard_map/ppermute | solution.py:227
  83.5 4.1 %collective-permute-start.2 = (f32[3,16,256]{2,1,0:T(8,128)S(1)}, f32[3,16,256]{2,1,0:T(8,128)S(1)}, u32[]{:S(2)}, u32[]{:S(2)}) collective-permute-start(f32[3,16,256]{2,1,0:T(8,128)S(1)} %bitcast.60), channel_id=1, source_target_pairs={{0,1},{1,2},{2,3},{3,4},{4,5},{5,6},{6,7},{7,8},{8,9},{9,10},{10,1... | collective-permute-start | bytes 147464 | tf_op jit(solution)/shard_map/ppermute | solution.py:227
  87.6 1.3 collective-permute-start.3
  89.0 3.6 %collective-permute-done.3.refs_8_ = f32[3,16,256]{2,1,0:T(8,128)S(1)} collective-permute-done((f32[3,16,256]{2,1,0:T(8,128)S(1)}, f32[3,16,256]{2,1,0:T(8,128)S(1)}, u32[]{:S(2)}, u32[]{:S(2)}) %collective-permute-start.3) | collective-permute-done | bytes 49184 | tf_op jit(solution)/shard_map/ppermute | solution.py:227
  92.6 1.4 sweep_cells.3
  94.0 3.3 %collective-permute-start.4 = (f32[3,32,256]{2,1,0:T(8,128)S(1)}, f32[3,32,256]{2,1,0:T(8,128)S(1)}, u32[]{:S(2)}, u32[]{:S(2)}) collective-permute-start(f32[3,32,256]{2,1,0:T(8,128)S(1)} %get-tuple-element.23), channel_id=1, source_target_pairs={{0,16},{16,32},{32,48},{48,64},{64,80},{80,96},{96,112},{1,17},{17... | collective-permute-start | bytes 294920 | tf_op jit(solution)/shard_map/ppermute | solution.py:227
  97.3 1.9 %collective-permute-start.5 = (f32[3,32,256]{2,1,0:T(8,128)S(1)}, f32[3,32,256]{2,1,0:T(8,128)S(1)}, u32[]{:S(2)}, u32[]{:S(2)}) collective-permute-start(f32[3,32,256]{2,1,0:T(8,128)S(1)} %get-tuple-element.24), channel_id=1, source_target_pairs={{16,0},{32,16},{48,32},{64,48},{80,64},{96,80},{112,96},{17,1},{33... | collective-permute-start | bytes 294920 | tf_op jit(solution)/shard_map/ppermute | solution.py:227
  99.2 2.1 %collective-permute-start.6 = (f32[3,16,256]{2,1,0:T(8,128)S(1)}, f32[3,16,256]{2,1,0:T(8,128)S(1)}, u32[]{:S(2)}, u32[]{:S(2)}) collective-permute-start(f32[3,16,256]{2,1,0:T(8,128)S(1)} %get-tuple-element.25), channel_id=1, source_target_pairs={{0,1},{1,2},{2,3},{3,4},{4,5},{5,6},{6,7},{7,8},{8,9},{9,10},{10,1... | collective-permute-start | bytes 147464 | tf_op jit(solution)/shard_map/ppermute | solution.py:227
  102.6 3.6 %collective-permute-done.7.refs_8_ = f32[3,16,256]{2,1,0:T(8,128)S(1)} collective-permute-done((f32[3,16,256]{2,1,0:T(8,128)S(1)}, f32[3,16,256]{2,1,0:T(8,128)S(1)}, u32[]{:S(2)}, u32[]{:S(2)}) %collective-permute-start.7) | collective-permute-done | bytes 49184 | tf_op jit(solution)/shard_map/ppermute | solution.py:227
  107.6 5.0 %collective-permute-start.8 = (f32[3,32,256]{2,1,0:T(8,128)S(1)}, f32[3,32,256]{2,1,0:T(8,128)S(1)}, u32[]{:S(2)}, u32[]{:S(2)}) collective-permute-start(f32[3,32,256]{2,1,0:T(8,128)S(1)} %get-tuple-element.28), channel_id=1, source_target_pairs={{0,16},{16,32},{32,48},{48,64},{64,80},{80,96},{96,112},{1,17},{17... | collective-permute-start | bytes 294920 | tf_op jit(solution)/shard_map/ppermute | solution.py:227
  112.5 1.9 %collective-permute-start.9 = (f32[3,32,256]{2,1,0:T(8,128)S(1)}, f32[3,32,256]{2,1,0:T(8,128)S(1)}, u32[]{:S(2)}, u32[]{:S(2)}) collective-permute-start(f32[3,32,256]{2,1,0:T(8,128)S(1)} %get-tuple-element.29), channel_id=1, source_target_pairs={{16,0},{32,16},{48,32},{64,48},{80,64},{96,80},{112,96},{17,1},{33... | collective-permute-start | bytes 294920 | tf_op jit(solution)/shard_map/ppermute | solution.py:227
  114.5 3.9 %collective-permute-start.10 = (f32[3,16,256]{2,1,0:T(8,128)S(1)}, f32[3,16,256]{2,1,0:T(8,128)S(1)}, u32[]{:S(2)}, u32[]{:S(2)}) collective-permute-start(f32[3,16,256]{2,1,0:T(8,128)S(1)} %get-tuple-element.30), channel_id=1, source_target_pairs={{0,1},{1,2},{2,3},{3,4},{4,5},{5,6},{6,7},{7,8},{8,9},{9,10},{10,1... | collective-permute-start | bytes 147464 | tf_op jit(solution)/shard_map/ppermute | solution.py:227
  119.6 3.8 %collective-permute-done.11.refs_8_ = f32[3,16,256]{2,1,0:T(8,128)S(1)} collective-permute-done((f32[3,16,256]{2,1,0:T(8,128)S(1)}, f32[3,16,256]{2,1,0:T(8,128)S(1)}, u32[]{:S(2)}, u32[]{:S(2)}) %collective-permute-start.11) | collective-permute-done | bytes 49184 | tf_op jit(solution)/shard_map/ppermute | solution.py:227
  123.5 2.3 %sweep_cells.5 = f32[3,16,32,256]{3,2,1,0:T(8,128)} custom-call(f32[3,16,32,256]{3,2,1,0:T(8,128)S(1)} %get-tuple-element.27.refs_0_, f32[3,16,32,256]{3,2,1,0:T(8,128)S(1)} %bitcast.38, f32[3,16,32,256]{3,2,1,0:T(8,128)S(1)} %get-tuple-element.38.refs_2_, f32[16,32,256]{2,1,0:T(8,128)S(1)} %copy-done, f32[9,16,32,256]{3,2,1,0:T(8,128)S(1)} %bitcast.34, ...), custom_call_target="tpu_custom_call" | custom-call | tf_op jit(solution)/shard_map/sweep_cells/pallas_call | solution.py:215
  125.8 1.4 copy-done.1
  127.2 20.0 %gather_rows.1 = f32[128,2,128]{2,1,0:T(2,128)S(1)} custom-call(s32[2,32]{1,0:T(2,128)S(1)} %pad_add_fusion.ends, f32[3,512,256]{2,1,0:T(8,128)S(1)} %bitcast.39, s32[128,128]{1,0:T(8,128)S(1)} %bitcast.42, f32[128,128]{1,0:T(8,128)S(1)} %bitcast.43, f32[128,128]{1,0:T(8,128)S(1)} %bitcast.44), custom_call_target="tpu_custom_call" | custom-call | tf_op jit(solution)/shard_map/gather_rows/pallas_call | solution.py:300
  147.2 24.1 %all_to_all.10 = f32[128,2,128]{2,1,0:T(2,128)S(1)} all-to-all(f32[128,2,128]{2,1,0:T(2,128)S(1)} %gather_rows.1), channel_id=1, replica_groups=mesh['gx'=8,'gy'=16] {'gx','gy'}, dimensions={0} | all-to-all | bytes 262144 | tf_op jit(solution)/shard_map/all_to_all | solution.py:317
  (46 shorter events, 13.1 us)
Async XLA Ops:
  0.6 31.6 %copy-start = (f32[16,32,256]{2,1,0:T(8,128)S(1)}, f32[16,32,256]{2,1,0:T(8,128)}, u32[]{:S(2)}) copy-start(f32[16,32,256]{2,1,0:T(8,128)} %refs_3_.5) | copy-start | bytes 1572868
  0.6 1.0 copy-start.2
  1.6 0.8 copy-start.3
  2.4 0.8 copy-start.4
  3.1 0.8 copy-start.5
  3.9 0.8 copy-start.6
  4.6 0.8 copy-start.7
  20.7 24.8 %all-to-all-start = ((f32[128,8,128]{2,1,0:T(8,128)}), f32[128,8,128]{2,1,0:T(8,128)S(1)}, u32[]{:S(2)}, u32[]{:S(2)}) async-start(f32[128,8,128]{2,1,0:T(8,128)} %pack_rows.1), calls=%async_computation | async-start | bytes 1048576 | tf_op jit(solution)/shard_map/all_to_all | solution.py:317
  59.8 15.7 %copy-start.8 = (f32[3,16,32,256]{3,2,1,0:T(8,128)S(1)}, f32[3,16,32,256]{3,2,1,0:T(8,128)}, u32[]{:S(2)}) copy-start(f32[3,16,32,256]{3,2,1,0:T(8,128)} %param.16) | copy-start | bytes 4718596
  75.5 17.1 %slice-start = ((s8[4718592]{0:T(1024)(128)(4,1)}), s8[4194304]{0:T(1024)(128)(4,1)S(1)}, s32[]{:S(2)}) async-start(s8[4718592]{0:T(1024)(128)(4,1)} %bitcast.33), calls=%async_computation.2 | async-start | bytes 8388608
  75.5 17.0 %slice-start.1 = ((s8[4718592]{0:T(1024)(128)(4,1)}), s8[524288]{0:T(1024)(128)(4,1)S(1)}, s32[]{:S(2)}) async-start(s8[4718592]{0:T(1024)(128)(4,1)} %bitcast.33), calls=%async_computation.3 | async-start | bytes 1048576
  76.2 16.4 %collective-permute-start.1 = (f32[3,32,256]{2,1,0:T(8,128)S(1)}, f32[3,32,256]{2,1,0:T(8,128)S(1)}, u32[]{:S(2)}, u32[]{:S(2)}) collective-permute-start(f32[3,32,256]{2,1,0:T(8,128)S(1)} %get-tuple-element.44), channel_id=1, source_target_pairs={{16,0},{32,16},{48,32},{64,48},{80,64},{96,80},{112,96},{17,1},{33... | collective-permute-start | bytes 294920 | tf_op jit(solution)/shard_map/ppermute | solution.py:227
  79.6 13.0 %collective-permute-start = (f32[3,32,256]{2,1,0:T(8,128)S(1)}, f32[3,32,256]{2,1,0:T(8,128)S(1)}, u32[]{:S(2)}, u32[]{:S(2)}) collective-permute-start(f32[3,32,256]{2,1,0:T(8,128)S(1)} %get-tuple-element.45), channel_id=1, source_target_pairs={{0,16},{16,32},{32,48},{48,64},{64,80},{80,96},{96,112},{1,17},{17... | collective-permute-start | bytes 294920 | tf_op jit(solution)/shard_map/ppermute | solution.py:227
  83.5 5.5 %collective-permute-start.2 = (f32[3,16,256]{2,1,0:T(8,128)S(1)}, f32[3,16,256]{2,1,0:T(8,128)S(1)}, u32[]{:S(2)}, u32[]{:S(2)}) collective-permute-start(f32[3,16,256]{2,1,0:T(8,128)S(1)} %bitcast.60), channel_id=1, source_target_pairs={{0,1},{1,2},{2,3},{3,4},{4,5},{5,6},{6,7},{7,8},{8,9},{9,10},{10,1... | collective-permute-start | bytes 147464 | tf_op jit(solution)/shard_map/ppermute | solution.py:227
  87.6 4.9 %collective-permute-start.3 = (f32[3,16,256]{2,1,0:T(8,128)S(1)}, f32[3,16,256]{2,1,0:T(8,128)S(1)}, u32[]{:S(2)}, u32[]{:S(2)}) collective-permute-start(f32[3,16,256]{2,1,0:T(8,128)S(1)} %bitcast.59), channel_id=1, source_target_pairs={{1,0},{2,1},{3,2},{4,3},{5,4},{6,5},{7,6},{8,7},{9,8},{10,9},{11,1... | collective-permute-start | bytes 147464 | tf_op jit(solution)/shard_map/ppermute | solution.py:227
  94.0 12.3 %collective-permute-start.4 = (f32[3,32,256]{2,1,0:T(8,128)S(1)}, f32[3,32,256]{2,1,0:T(8,128)S(1)}, u32[]{:S(2)}, u32[]{:S(2)}) collective-permute-start(f32[3,32,256]{2,1,0:T(8,128)S(1)} %get-tuple-element.23), channel_id=1, source_target_pairs={{0,16},{16,32},{32,48},{48,64},{64,80},{80,96},{96,112},{1,17},{17... | collective-permute-start | bytes 294920 | tf_op jit(solution)/shard_map/ppermute | solution.py:227
  97.3 9.0 %collective-permute-start.5 = (f32[3,32,256]{2,1,0:T(8,128)S(1)}, f32[3,32,256]{2,1,0:T(8,128)S(1)}, u32[]{:S(2)}, u32[]{:S(2)}) collective-permute-start(f32[3,32,256]{2,1,0:T(8,128)S(1)} %get-tuple-element.24), channel_id=1, source_target_pairs={{16,0},{32,16},{48,32},{64,48},{80,64},{96,80},{112,96},{17,1},{33... | collective-permute-start | bytes 294920 | tf_op jit(solution)/shard_map/ppermute | solution.py:227
  99.2 3.4 %collective-permute-start.6 = (f32[3,16,256]{2,1,0:T(8,128)S(1)}, f32[3,16,256]{2,1,0:T(8,128)S(1)}, u32[]{:S(2)}, u32[]{:S(2)}) collective-permute-start(f32[3,16,256]{2,1,0:T(8,128)S(1)} %get-tuple-element.25), channel_id=1, source_target_pairs={{0,1},{1,2},{2,3},{3,4},{4,5},{5,6},{6,7},{7,8},{8,9},{9,10},{10,1... | collective-permute-start | bytes 147464 | tf_op jit(solution)/shard_map/ppermute | solution.py:227
  101.3 4.9 %collective-permute-start.7 = (f32[3,16,256]{2,1,0:T(8,128)S(1)}, f32[3,16,256]{2,1,0:T(8,128)S(1)}, u32[]{:S(2)}, u32[]{:S(2)}) collective-permute-start(f32[3,16,256]{2,1,0:T(8,128)S(1)} %get-tuple-element.26), channel_id=1, source_target_pairs={{1,0},{2,1},{3,2},{4,3},{5,4},{6,5},{7,6},{8,7},{9,8},{10,9},{11,1... | collective-permute-start | bytes 147464 | tf_op jit(solution)/shard_map/ppermute | solution.py:227
  107.6 15.9 %collective-permute-start.8 = (f32[3,32,256]{2,1,0:T(8,128)S(1)}, f32[3,32,256]{2,1,0:T(8,128)S(1)}, u32[]{:S(2)}, u32[]{:S(2)}) collective-permute-start(f32[3,32,256]{2,1,0:T(8,128)S(1)} %get-tuple-element.28), channel_id=1, source_target_pairs={{0,16},{16,32},{32,48},{48,64},{64,80},{80,96},{96,112},{1,17},{17... | collective-permute-start | bytes 294920 | tf_op jit(solution)/shard_map/ppermute | solution.py:227
  112.5 10.9 %collective-permute-start.9 = (f32[3,32,256]{2,1,0:T(8,128)S(1)}, f32[3,32,256]{2,1,0:T(8,128)S(1)}, u32[]{:S(2)}, u32[]{:S(2)}) collective-permute-start(f32[3,32,256]{2,1,0:T(8,128)S(1)} %get-tuple-element.29), channel_id=1, source_target_pairs={{16,0},{32,16},{48,32},{64,48},{80,64},{96,80},{112,96},{17,1},{33... | collective-permute-start | bytes 294920 | tf_op jit(solution)/shard_map/ppermute | solution.py:227
  114.5 5.2 %collective-permute-start.10 = (f32[3,16,256]{2,1,0:T(8,128)S(1)}, f32[3,16,256]{2,1,0:T(8,128)S(1)}, u32[]{:S(2)}, u32[]{:S(2)}) collective-permute-start(f32[3,16,256]{2,1,0:T(8,128)S(1)} %get-tuple-element.30), channel_id=1, source_target_pairs={{0,1},{1,2},{2,3},{3,4},{4,5},{5,6},{6,7},{7,8},{8,9},{9,10},{10,1... | collective-permute-start | bytes 147464 | tf_op jit(solution)/shard_map/ppermute | solution.py:227
  118.3 5.1 %collective-permute-start.11 = (f32[3,16,256]{2,1,0:T(8,128)S(1)}, f32[3,16,256]{2,1,0:T(8,128)S(1)}, u32[]{:S(2)}, u32[]{:S(2)}) collective-permute-start(f32[3,16,256]{2,1,0:T(8,128)S(1)} %get-tuple-element.31), channel_id=1, source_target_pairs={{1,0},{2,1},{3,2},{4,3},{5,4},{6,5},{7,6},{8,7},{9,8},{10,9},{11,1... | collective-permute-start | bytes 147464 | tf_op jit(solution)/shard_map/ppermute | solution.py:227
  125.8 1.4 copy-start.1

commit v3 on v2

v3 whole, which is shorter than its diff:
```python
import jax
import jax.numpy as jnp
from jax import lax
from jax.experimental import pallas as pl
from jax.experimental.pallas import tpu as pltpu
from jax.sharding import PartitionSpec as P

BOX_DEV = 64
BOX_BITS = 6
SWEEPS = 4
AXES = ("gx", "gy")
STEP_ROWS = 512
RANK_ROWS = 256
WINDOW = 32
SIDE = 4
CELL_SHIFT = 257
MIB = 1024 * 1024


def dot_last(left, right):
    return lax.dot_general(
        left, right, (((1,), (1,)), ((), ())), preferred_element_type=jnp.float32
    )


def halves(values):
    high = values.astype(jnp.bfloat16).astype(jnp.float32)
    return high, values - high


def places(height, width):
    return lax.broadcasted_iota(jnp.int32, (height, width), 0)


def marked(mask, row):
    return jnp.where(mask, row, 0.0).astype(jnp.bfloat16)


def pack_kernel(*refs):
    given, rows, kept = refs[:6], refs[6], refs[7:13]
    ranks, upper, left, right, total, arrivals = refs[13:]
    sens, weight, device, cell, owner, slot = kept
    devices, _, capacity = rows.shape
    part = upper.shape[0]
    step = STEP_ROWS
    steps = sens.shape[1] // step
    copies = [
        pltpu.make_async_copy(given[p], kept[p], arrivals.at[p]) for p in range(len(given))
    ]
    for copy in copies:
        copy.start()
    before = lax.broadcasted_iota(jnp.int32, (part, part), 0)
    after = lax.broadcasted_iota(jnp.int32, (part, part), 1)
    upper[...] = marked(before < after, 1.0)
    total[...] = jnp.zeros_like(total)
    for copy in copies:
        copy.wait()

    def rank(i, base):
        for b in range(4):
            at = pl.ds(pl.multiple_of((i * 4 + b) * part, part), part)
            here = places(devices, part) == device[:, at]
            ones = jnp.where(here, 1.0, 0.0)
            within = jnp.dot(
                ones.astype(jnp.bfloat16), upper[...], preferred_element_type=jnp.float32
            )
            ranks[:, at] = jnp.sum(
                jnp.where(here, within + base, 0.0), axis=0, keepdims=True
            ).astype(jnp.int32)
            base = base + jnp.sum(ones, axis=1, keepdims=True)
        return base

    lax.fori_loop(0, sens.shape[1] // part // 4, rank, jnp.zeros((devices, 1), jnp.float32))

    def chunk(i, _):
        for b in range(2):
            at = pl.ds(pl.multiple_of((i * 2 + b) * step, step), step)
            ones = marked(places(devices, step) == device[:, at], 1.0)
            left[b, :, :step] = ones
            left[b, :, step:] = ones
            here = places(capacity, step) == ranks[:, at]
            own_cell = cell[:, at]
            pairs = [halves(sens[k : k + 1, at]) for k in range(3)]
            pairs.append(
                (
                    (((own_cell >> 9) + 1) << 9).astype(jnp.float32),
                    ((own_cell & 511) + (CELL_SHIFT - 512)).astype(jnp.float32),
                )
            )
            pairs.append(halves(weight[:, at]))
            pairs.append(
                ((owner[:, at] * BOX_DEV).astype(jnp.float32), slot[:, at].astype(jnp.float32))
            )
            for p, (high, low) in enumerate(pairs):
                band = slice(p * capacity, (p + 1) * capacity)
                right[b, band, :step] = marked(here, high)
                right[b, band, step:] = marked(here, low)
        total[...] += dot_last(left[0], right[0]) + dot_last(left[1], right[1])
        return 0

    lax.fori_loop(0, steps // 2, chunk, 0)
    for p in range(6):
        rows[:, p, :] = total[:, p * capacity : (p + 1) * capacity]
    for p in range(6, 8):
        rows[:, p, :] = jnp.zeros((devices, capacity), jnp.float32)


def pack(devices, *given):
    count = given[0].shape[1]
    capacity = 2 * count // devices
    return pl.pallas_call(
        pack_kernel,
        in_specs=[pl.BlockSpec(memory_space=pltpu.HBM)] * len(given),
        out_shape=jax.ShapeDtypeStruct((devices, 8, capacity), jnp.float32),
        scratch_shapes=[pltpu.VMEM(part.shape, part.dtype) for part in given]
        + [
            pltpu.VMEM((1, count), jnp.int32),
            pltpu.VMEM((RANK_ROWS, RANK_ROWS), jnp.bfloat16),
            pltpu.VMEM((2, devices, 2 * STEP_ROWS), jnp.bfloat16),
            pltpu.VMEM((2, 6 * capacity, 2 * STEP_ROWS), jnp.bfloat16),
            pltpu.VMEM((devices, 6 * capacity), jnp.float32),
            pltpu.SemaphoreType.DMA((len(given),)),
        ],
        compiler_params=pltpu.CompilerParams(vmem_limit_bytes=20 * MIB),
        name="pack_rows",
    )(*given)


def windows(ends, i):
    first = jnp.maximum(ends[0, i] >> 8, 0)
    start = first & ~7
    return start, (jnp.maximum((ends[1, i] >> 8) + WINDOW - start, 0)) // WINDOW


def filled(ends):
    groups = ends.shape[1] // SIDE

    def count(g, empty):
        return empty + jnp.where(ends[1, g * SIDE + SIDE - 1] < 0, 1, 0)

    return lax.fori_loop(0, groups, count, 0)


def scatter_kernel(ends, cells, one, two, three, inverse, stiff, load, field, *rest):
    head_x, tail_x, head_y, tail_y, left, right = rest
    height, depth = load.shape[1:]
    lines, width = cells.shape
    half = depth // 2
    group = STEP_ROWS // width
    step = STEP_ROWS
    load[...] = jnp.zeros_like(load)

    def fill(i, b):
        for q in range(group):
            row = pl.ds(i * group + q, 1)
            there = places(half, width) == (cells[row, :] & (half - 1))
            for k, sens in enumerate((one, two, three)):
                high, low = halves(sens[row, :])
                band = slice(k * half, (k + 1) * half)
                right[b, band, q * width : (q + 1) * width] = marked(there, high)
                right[b, band, step + q * width : step + (q + 1) * width] = marked(there, low)

    def window(i, b, start, w):
        least = start + w * WINDOW
        base = pl.multiple_of(jnp.minimum(least, height - WINDOW), 8)
        for q in range(group):
            cell = cells[pl.ds(i * group + q, 1), :]
            hot = marked(places(2 * WINDOW, width) == window_place(cell, least, base), 1.0)
            left[b, :, q * width : (q + 1) * width] = hot
            left[b, :, step + q * width : step + (q + 1) * width] = hot
        sums = dot_last(left[b], right[b])

        def add():
            for k in range(3):
                for side in range(2):
                    at = (k, pl.ds(base, WINDOW), slice(side * half, (side + 1) * half))
                    load[at] += sums[
                        side * WINDOW : (side + 1) * WINDOW, k * half : (k + 1) * half
                    ]

        return add

    def chunks(i, _):
        own = [i * SIDE + b for b in range(SIDE)]
        spans = [windows(ends, j) for j in own]
        for b in range(SIDE):
            fill(own[b], b)
        adds = [window(own[b], b, spans[b][0], 0) for b in range(SIDE)]
        for add in adds:
            add()
        for b in range(SIDE):

            def more(w, _, b=b):
                window(own[b], b, spans[b][0], w)()
                return 0

            lax.fori_loop(1, spans[b][1], more, 0)
        return 0

    lax.fori_loop(filled(ends), lines // group // SIDE, chunks, 0)
    size_x, size_y = head_y.shape[1], head_x.shape[1]
    for k in range(3):
        field[k] = load[k] * inverse[k]
        head_x[k] = field[k, :size_y] * stiff[:size_y]
        tail_x[k] = field[k, height - size_y :] * stiff[height - size_y :]
        for x in range(size_x):
            for y, face in ((0, head_y), (size_y - 1, tail_y)):
                at = slice(x * size_y + y, x * size_y + y + 1)
                face[k, x : x + 1] = field[k, at] * stiff[at]


def window_place(cell, least, base):
    line = cell >> 8
    place = ((cell >> 7) & 1) * WINDOW + line - base
    inside = (line >= least) & (line < base + WINDOW)
    return jnp.where(inside, place, -1)


def scatter(ends, cells, values, inverse, stiff):
    size_x, size_y, depth = stiff.shape
    height = size_x * size_y
    vmem = pl.BlockSpec(memory_space=pltpu.VMEM)
    cube = (3, height, depth)
    shapes = [cube] * 2 + [(3, size_y, depth)] * 2 + [(3, size_x, depth)] * 2
    load, field, *faces = pl.pallas_call(
        scatter_kernel,
        in_specs=[pl.BlockSpec(memory_space=pltpu.SMEM)] + [vmem] * 6,
        out_specs=[vmem] * 6,
        out_shape=[jax.ShapeDtypeStruct(shape, jnp.float32) for shape in shapes],
        scratch_shapes=[
            pltpu.VMEM((SIDE, 2 * WINDOW, 2 * STEP_ROWS), jnp.bfloat16),
            pltpu.VMEM((SIDE, 3 * depth // 2, 2 * STEP_ROWS), jnp.bfloat16),
        ],
        compiler_params=pltpu.CompilerParams(vmem_limit_bytes=20 * MIB),
        name="scatter_rows",
    )(ends, cells, *values, inverse.reshape(cube), stiff.reshape(cube[1:]))
    whole = (3, size_x, size_y, depth)
    return load.reshape(whole), field.reshape(whole), faces


def sweep_kernel(last, field, load, inverse, stiff, coupling, west, east, south, north, *outs):
    _, size_x, size_y, size_z = field.shape
    padded = outs[-1]
    result = outs[0]
    padded[:, 0] = west[...]
    padded[:, size_x + 1] = east[...]
    for x in range(size_x):
        for k in range(3):
            padded[k, x + 1] = stiff[x] * field[k, x]
    row = lax.broadcasted_iota(jnp.int32, (size_y, size_z), 0)
    column = lax.broadcasted_iota(jnp.int32, (size_y, size_z), 1)
    for x in range(size_x):
        own = [field[k, x] for k in range(3)]
        for k in range(3):
            middle = padded[k, x + 1]
            total = load[k, x] + padded[k, x] + padded[k, x + 2]
            total = total + jnp.where(row == 0, south[k, x : x + 1], pltpu.roll(middle, 1, 0))
            total = total + jnp.where(
                row == size_y - 1, north[k, x : x + 1], pltpu.roll(middle, size_y - 1, 0)
            )
            total = total + jnp.where(column == 0, 0.0, pltpu.roll(middle, 1, 1))
            total = total + jnp.where(
                column == size_z - 1, 0.0, pltpu.roll(middle, size_z - 1, 1)
            )
            for j in range(3):
                if j != k:
                    total = total - coupling[3 * j + k, x] * own[j]
            fresh = total * inverse[k, x]
            result[k, x] = fresh
            if not last:
                head_x, tail_x, head_y, tail_y = outs[1:5]
                moved = stiff[x] * fresh
                if x == 0:
                    head_x[k] = moved
                if x == size_x - 1:
                    tail_x[k] = moved
                head_y[k, x : x + 1] = moved[:1]
                tail_y[k, x : x + 1] = moved[size_y - 1 :]


def sweep(last, field, load, inverse, stiff, coupling, halo):
    _, size_x, size_y, size_z = field.shape
    shapes = [field.shape]
    if not last:
        shapes += [(3, size_y, size_z)] * 2 + [(3, size_x, size_z)] * 2

    def kernel(*refs):
        sweep_kernel(last, *refs)

    return pl.pallas_call(
        kernel,
        out_shape=[jax.ShapeDtypeStruct(shape, jnp.float32) for shape in shapes],
        scratch_shapes=[pltpu.VMEM((3, size_x + 2, size_y, size_z), jnp.float32)],
        compiler_params=pltpu.CompilerParams(vmem_limit_bytes=24 * MIB),
        name="sweep_cells",
    )(field, load, inverse, stiff, coupling, *halo)


def exchange(head_x, tail_x, head_y, tail_y):
    def shifted(face, axis, up):
        pairs = [(i, i + 1) if up else (i + 1, i) for i in range(lax.axis_size(axis) - 1)]
        return lax.ppermute(face, axis, pairs)

    south = shifted(tail_y, "gy", True)
    north = shifted(head_y, "gy", False)
    west = shifted(tail_x, "gx", True)
    east = shifted(head_x, "gx", False)
    return west, east, south, north


def gather_kernel(ends, field, cells, weights, boxes, sums, hot, left, right, total):
    height, depth = field.shape[1:]
    lines, width = cells.shape
    half = depth // 2
    group = STEP_ROWS // width
    step = STEP_ROWS
    total[...] = jnp.zeros_like(total)
    right[...] = jnp.zeros_like(right)

    def rows(i):
        return [pl.ds(i * group + q, 1) for q in range(group)]

    def window(i, b, start, w):
        least = start + w * WINDOW
        base = pl.multiple_of(jnp.minimum(least, height - WINDOW), 8)
        own = [cells[row, :] for row in rows(i)]
        for q in range(group):
            ones = marked(places(2 * WINDOW, width) == window_place(own[q], least, base), 1.0)
            hot[b, : 2 * WINDOW, q * width : (q + 1) * width] = ones
            hot[b, 2 * WINDOW :, q * width : (q + 1) * width] = ones
        there = [places(half, width) == (cell & (half - 1)) for cell in own]
        picked = []
        for k in range(3):
            block = field[k, pl.ds(base, WINDOW), :]
            block = jnp.concatenate([block[:, :half], block[:, half:]], axis=0)
            high, low = halves(block)
            both = jnp.concatenate([high, low], axis=0).T.astype(jnp.bfloat16)
            part = jnp.dot(both, hot[b], preferred_element_type=jnp.float32)
            picked.append(
                jnp.concatenate(
                    [
                        jnp.sum(
                            jnp.where(there[q], part[:, q * width : (q + 1) * width], 0.0),
                            axis=0,
                            keepdims=True,
                        )
                        for q in range(group)
                    ],
                    axis=1,
                )
            )
        return tuple(picked)

    def spread(i, b, picked):
        for q, row in enumerate(rows(i)):
            at = slice(q * width, (q + 1) * width)
            low_at = slice(step + q * width, step + (q + 1) * width)
            weight = weights[row, :]
            box = boxes[row, :].astype(jnp.int32)
            owned = marked(places(left.shape[1], width) == (box >> BOX_BITS), 1.0)
            left[b, :, at] = owned
            left[b, :, low_at] = owned
            inside = places(BOX_DEV, width) == (box & (BOX_DEV - 1))
            for k in range(3):
                high, low = halves(picked[k][:, at] * weight)
                band = slice(k * BOX_DEV, (k + 1) * BOX_DEV)
                right[b, band, at] = marked(inside, high)
                right[b, band, low_at] = marked(inside, low)

    def chunks(i, _):
        own = [i * SIDE + b for b in range(SIDE)]
        spans = [windows(ends, j) for j in own]
        firsts = [window(own[b], b, spans[b][0], 0) for b in range(SIDE)]
        finals = []
        for b in range(SIDE):

            def more(w, picked, b=b):
                fresh = window(own[b], b, spans[b][0], w)
                return tuple(old + new for old, new in zip(picked, fresh))

            finals.append(lax.fori_loop(1, spans[b][1], more, firsts[b]))
        for b in range(SIDE):
            spread(own[b], b, finals[b])
        parts = [dot_last(left[b], right[b]) for b in range(SIDE)]
        total[...] += sum(parts[1:], parts[0])
        return 0

    lax.fori_loop(filled(ends), lines // group // SIDE, chunks, 0)
    for p in range(2):
        sums[:, p, :] = total[:, p * 128 : (p + 1) * 128]


def gather(ends, field, cells, weights, boxes, devices):
    vmem = pl.BlockSpec(memory_space=pltpu.VMEM)
    return pl.pallas_call(
        gather_kernel,
        in_specs=[pl.BlockSpec(memory_space=pltpu.SMEM)] + [vmem] * 4,
        out_specs=vmem,
        out_shape=jax.ShapeDtypeStruct((devices, 2, 128), jnp.float32),
        scratch_shapes=[
            pltpu.VMEM((SIDE, 4 * WINDOW, STEP_ROWS), jnp.bfloat16),
            pltpu.VMEM((SIDE, devices, 2 * STEP_ROWS), jnp.bfloat16),
            pltpu.VMEM((SIDE, 4 * BOX_DEV, 2 * STEP_ROWS), jnp.bfloat16),
            pltpu.VMEM((devices, 4 * BOX_DEV), jnp.float32),
        ],
        compiler_params=pltpu.CompilerParams(vmem_limit_bytes=16 * MIB),
        name="gather_rows",
    )(ends, field, cells, weights, boxes)


def swapped(blocks):
    return lax.all_to_all(blocks, AXES, split_axis=0, concat_axis=0, tiled=True)


def body(
    sensitivity,
    node_weight,
    dest_device,
    dest_cell,
    box_owner,
    box_slot,
    stiffness,
    anchor,
    coupling,
):
    devices = lax.axis_size("gx") * lax.axis_size("gy")
    count = sensitivity.shape[1]
    size_x, size_y, size_z = stiffness.shape
    lane = lambda values: values.reshape(1, count)
    rows = pack(
        devices,
        sensitivity,
        lane(node_weight),
        lane(dest_device),
        lane(dest_cell),
        lane(box_owner),
        lane(box_slot),
    )
    rows = swapped(rows)
    planes = [rows[:, p].reshape(-1) for p in range(6)]
    keys = jnp.maximum(planes[3].astype(jnp.int32) - CELL_SHIFT, -1)
    ordered = lax.sort((keys, *planes[:3], *planes[4:]), num_keys=1, is_stable=False)
    cells, *values, weights, boxes = [part.reshape(-1, 128) for part in ordered]
    blocks = cells.reshape(-1, STEP_ROWS // 128, 128)
    ends = jnp.stack([blocks[:, 0, 0], blocks[:, -1, -1]])
    diagonal = 6.0 * stiffness[None] + anchor + jnp.stack([coupling[0], coupling[4], coupling[8]])
    inverse = 1.0 / diagonal
    load, field, faces = scatter(ends, cells, values, inverse, stiffness)
    for turn in range(1, SWEEPS):
        last = turn == SWEEPS - 1
        field, *faces = sweep(
            last, field, load, inverse, stiffness, coupling, exchange(*faces)
        )
    flat = field.reshape(3, size_x * size_y, size_z)
    partial = gather(ends, flat, cells, weights, boxes, devices)
    summed = jnp.sum(swapped(partial), axis=0).reshape(4, BOX_DEV)
    return (field, summed[:3])


def solution(mesh):
    placed = (
        P(None, AXES),
        P(AXES),
        P(AXES, None),
        P(AXES),
        P(AXES, None),
        P(AXES),
        P("gx", "gy", None),
        P(None, "gx", "gy", None),
        P(None, "gx", "gy", None),
    )
    return jax.shard_map(
        body,
        mesh=mesh,
        in_specs=placed,
        out_specs=(P(None, "gx", "gy", None), P(None, AXES)),
        check_vma=False,
    )
```

time: 173 us -> 157 us (0.908)
  Pallas kernels: 54.7 us -> 44.4 us
  starting transfers between devices: 44.8 us -> 41.2 us
  local copies, waits for them, and re-layouts: 10.6 us -> 12.7 us
  other arithmetic: 14.1 us -> 12.3 us
    pallas_call x1, Pallas kernels: 20 us -> 15.2 us  [gather(): pl.pallas_call(gather_kernel, in_specs=[pl.BlockSpec(memory_space=pltpu.S...]
    ppermute x12, starting transfers between devices: 33.3 us -> 29.7 us  [shifted(): return lax.ppermute(face, axis, pairs)]
    pallas_call x1, Pallas kernels: 14.4 us -> 11.7 us  [scatter(): pl.pallas_call(scatter_kernel, in_specs=[pl.BlockSpec(memory_space=pltpu....]
    unnamed x24 -> x20, local copies, waits for them, and re-layouts: 6.18 us -> 8.73 us
    pallas_call x1, Pallas kernels: 15.3 us -> 12.8 us  [pack(): pl.pallas_call(pack_kernel, in_specs=[pl.BlockSpec(memory_space=pltpu.HBM...]
  transfers between devices with their start and end apart: 13 -> 13, of which waited for: 4 -> 5; matrix products, arithmetic and copies ran while one was open for 1% -> 1% of each run, Pallas kernels for 0% -> 0%
where the time goes in v3:
time: 157 us; the launch traced here: 158 us
  Pallas kernels  44.4 us (28%)
  starting transfers between devices  41.2 us (26%)
  blocking collectives  23.9 us (15%)
  waiting for transfers between devices  22.4 us (14%)
  local copies, waits for them, and re-layouts  12.7 us (8%)
  other arithmetic  12.3 us (8%)
    ppermute x12, starting transfers between devices, shifted(): return lax.ppermute(face, axis, pairs)  29.7 us
    all_to_all x1, blocking collectives, swapped(): return lax.all_to_all(blocks, AXES, split_axis=0, concat_axis=0, tiled=True)  23.9 us
    pallas_call x1, Pallas kernels, gather(): pl.pallas_call(gather_kernel, in_specs=[pl.BlockSpec(memory_space=pltpu.S...  15.2 us
    pallas_call x1, Pallas kernels, pack(): pl.pallas_call(pack_kernel, in_specs=[pl.BlockSpec(memory_space=pltpu.HBM...  12.8 us
    pallas_call x1, Pallas kernels, scatter(): pl.pallas_call(scatter_kernel, in_specs=[pl.BlockSpec(memory_space=pltpu....  11.7 us
    ppermute x12, waiting for transfers between devices, shifted(): return lax.ppermute(face, axis, pairs)  11.6 us
    sort x1, other arithmetic, body(): lax.sort((keys, *planes[:3], *planes[4:]), num_keys=1, is_stable=False)  11.5 us
    all_to_all x1, starting transfers between devices, swapped(): return lax.all_to_all(blocks, AXES, split_axis=0, concat_axis=0, tiled=True)  11.5 us
  transfers between devices with their start and end apart: 13, of which 5 were waited for; matrix products, arithmetic and copies ran while one was open for 1% of the time, Pallas kernels for 0%

profile of v3, /device:TPU:1, one launch (start us, length us, event | category | flops | bytes accessed | tf_op | source)
XLA Modules:
  0.0 157.8 jit_solution(7408838386029497880)
XLA Ops:
  5.3 12.8 %pack_rows.1 = f32[128,8,128]{2,1,0:T(8,128)} custom-call(f32[3,8192]{1,0:T(4,128)S(1)} %copy-done.3, f32[1,8192]{1,0:T(1,128)S(1)} %bitcast.41, s32[1,8192]{1,0:T(1,128)S(1)} %bitcast.42, s32[1,8192]{1,0:T(1,128)S(1)} %bitcast.43, s32[1,8192]{1,0:T(1,128)S(1)} %bitcast.44, s32[1,8192]{1,0:T(1,128)S(1)} %bitcast.45), custom_call_target="tpu_custom_call" | custom-call | tf_op jit(solution)/shard_map/pack_rows/pallas_call | solution.py:111
  18.2 11.5 %all-to-all-start = ((f32[128,8,128]{2,1,0:T(8,128)}), f32[128,8,128]{2,1,0:T(8,128)S(1)}, u32[]{:S(2)}, u32[]{:S(2)}) async-start(f32[128,8,128]{2,1,0:T(8,128)} %pack_rows.1), calls=%async_computation | async-start | bytes 1048576 | tf_op jit(solution)/shard_map/all_to_all | solution.py:412
  29.7 1.7 %fusion.3 = (f32[1,16,32,256]{3,2,1,0:T(8,128)S(1)}, f32[1,16,32,256]{3,2,1,0:T(8,128)S(1)}, f32[1,16,32,256]{3,2,1,0:T(8,128)S(1)}) fusion(f32[9,16,32,256]{3,2,1,0:T(8,128)} %refs_4_.5), kind=kLoop, calls=%fused_computation.9 | loop fusion | bytes 3145728 | tf_op jit(solution)/shard_map/slice | solution.py:446
  32.2 10.8 %all-to-all-done = f32[128,8,128]{2,1,0:T(8,128)S(1)} async-done(((f32[128,8,128]{2,1,0:T(8,128)}), f32[128,8,128]{2,1,0:T(8,128)S(1)}, u32[]{:S(2)}, u32[]{:S(2)}) %all-to-all-start) | async-done | bytes 524320 | tf_op jit(solution)/shard_map/all_to_all | solution.py:412
  43.4 11.5 %sort.39 = (s32[16384]{0:T(1024)S(1)}, f32[16384]{0:T(1024)S(1)}, f32[16384]{0:T(1024)S(1)}, f32[16384]{0:T(1024)S(1)}, f32[16384]{0:T(1024)S(1)}, /*index=5*/f32[16384]{0:T(1024)S(1)}) sort(s32[16384]{0:T(1024)S(1)} %bitcast.51, f32[16384]{0:T(1024)S(1)} %bitcast.50, f32[16384]{0:T(1024)S(1)} %bitcast.49, f32[16384]{0:T(1024)S(1)} %bitcast.48, ...), dimensions={0}, to_apply=%region_0.0 | sort | flops 229376 | bytes 786432 | tf_op jit(solution)/shard_map/sort | solution.py:442
  54.9 1.5 slice_reduce_fusion.1
  56.4 11.7 %scatter_rows.1 = (f32[3,512,256]{2,1,0:T(8,128)S(1)}, f32[3,512,256]{2,1,0:T(8,128)S(1)}, f32[3,32,256]{2,1,0:T(8,128)S(1)}, f32[3,32,256]{2,1,0:T(8,128)S(1)},...) custom-call(s32[2,32]{1,0:T(2,128)S(1)} %pad_add_fusion.ends, s32[128,128]{1,0:T(8,128)S(1)} %bitcast.34, ...), custom_call_target="tpu_custom_call" | custom-call | tf_op jit(solution)/shard_map/scatter_rows/pallas_call | solution.py:225
  68.1 2.7 %collective-permute-start = (f32[3,32,256]{2,1,0:T(8,128)S(1)}, f32[3,32,256]{2,1,0:T(8,128)S(1)}, u32[]{:S(2)}, u32[]{:S(2)}) collective-permute-start(f32[3,32,256]{2,1,0:T(8,128)S(1)} %get-tuple-element.30), channel_id=1, source_target_pairs={{0,16},{16,32},{32,48},{48,64},{64,80},{80,96},{96,112},{1,17},{17... | collective-permute-start | bytes 294920 | tf_op jit(solution)/shard_map/ppermute | solution.py:302
  70.8 1.9 %collective-permute-start.1 = (f32[3,32,256]{2,1,0:T(8,128)S(1)}, f32[3,32,256]{2,1,0:T(8,128)S(1)}, u32[]{:S(2)}, u32[]{:S(2)}) collective-permute-start(f32[3,32,256]{2,1,0:T(8,128)S(1)} %get-tuple-element.31), channel_id=1, source_target_pairs={{16,0},{32,16},{48,32},{64,48},{80,64},{96,80},{112,96},{17,1},{33... | collective-permute-start | bytes 294920 | tf_op jit(solution)/shard_map/ppermute | solution.py:302
  72.8 1.8 %collective-permute-start.2 = (f32[3,16,256]{2,1,0:T(8,128)S(1)}, f32[3,16,256]{2,1,0:T(8,128)S(1)}, u32[]{:S(2)}, u32[]{:S(2)}) collective-permute-start(f32[3,16,256]{2,1,0:T(8,128)S(1)} %get-tuple-element.32), channel_id=1, source_target_pairs={{0,1},{1,2},{2,3},{3,4},{4,5},{5,6},{6,7},{7,8},{8,9},{9,10},{10,1... | collective-permute-start | bytes 147464 | tf_op jit(solution)/shard_map/ppermute | solution.py:302
  76.0 4.1 %collective-permute-done.3.refs_8_ = f32[3,16,256]{2,1,0:T(8,128)S(1)} collective-permute-done((f32[3,16,256]{2,1,0:T(8,128)S(1)}, f32[3,16,256]{2,1,0:T(8,128)S(1)}, u32[]{:S(2)}, u32[]{:S(2)}) %collective-permute-start.3) | collective-permute-done | bytes 49184 | tf_op jit(solution)/shard_map/ppermute | solution.py:302
  80.1 2.3 %copy-done = f32[9,16,32,256]{3,2,1,0:T(8,128)S(1)} copy-done((f32[9,16,32,256]{3,2,1,0:T(8,128)S(1)}, f32[9,16,32,256]{3,2,1,0:T(8,128)}, u32[]{:S(2)}) %copy-start) | copy-done | bytes 4718616
  83.6 3.9 %collective-permute-start.4 = (f32[3,32,256]{2,1,0:T(8,128)S(1)}, f32[3,32,256]{2,1,0:T(8,128)S(1)}, u32[]{:S(2)}, u32[]{:S(2)}) collective-permute-start(f32[3,32,256]{2,1,0:T(8,128)S(1)} %get-tuple-element.35), channel_id=1, source_target_pairs={{0,16},{16,32},{32,48},{48,64},{64,80},{80,96},{96,112},{1,17},{17... | collective-permute-start | bytes 294920 | tf_op jit(solution)/shard_map/ppermute | solution.py:302
  87.5 1.9 %collective-permute-start.5 = (f32[3,32,256]{2,1,0:T(8,128)S(1)}, f32[3,32,256]{2,1,0:T(8,128)S(1)}, u32[]{:S(2)}, u32[]{:S(2)}) collective-permute-start(f32[3,32,256]{2,1,0:T(8,128)S(1)} %get-tuple-element.36), channel_id=1, source_target_pairs={{16,0},{32,16},{48,32},{64,48},{80,64},{96,80},{112,96},{17,1},{33... | collective-permute-start | bytes 294920 | tf_op jit(solution)/shard_map/ppermute | solution.py:302
  89.5 1.9 %collective-permute-start.6 = (f32[3,16,256]{2,1,0:T(8,128)S(1)}, f32[3,16,256]{2,1,0:T(8,128)S(1)}, u32[]{:S(2)}, u32[]{:S(2)}) collective-permute-start(f32[3,16,256]{2,1,0:T(8,128)S(1)} %get-tuple-element.37), channel_id=1, source_target_pairs={{0,1},{1,2},{2,3},{3,4},{4,5},{5,6},{6,7},{7,8},{8,9},{9,10},{10,1... | collective-permute-start | bytes 147464 | tf_op jit(solution)/shard_map/ppermute | solution.py:302
  92.7 3.5 %collective-permute-done.7.refs_8_ = f32[3,16,256]{2,1,0:T(8,128)S(1)} collective-permute-done((f32[3,16,256]{2,1,0:T(8,128)S(1)}, f32[3,16,256]{2,1,0:T(8,128)S(1)}, u32[]{:S(2)}, u32[]{:S(2)}) %collective-permute-start.7) | collective-permute-done | bytes 49184 | tf_op jit(solution)/shard_map/ppermute | solution.py:302
  97.5 5.1 %collective-permute-start.8 = (f32[3,32,256]{2,1,0:T(8,128)S(1)}, f32[3,32,256]{2,1,0:T(8,128)S(1)}, u32[]{:S(2)}, u32[]{:S(2)}) collective-permute-start(f32[3,32,256]{2,1,0:T(8,128)S(1)} %get-tuple-element.40), channel_id=1, source_target_pairs={{0,16},{16,32},{32,48},{48,64},{64,80},{80,96},{96,112},{1,17},{17... | collective-permute-start | bytes 294920 | tf_op jit(solution)/shard_map/ppermute | solution.py:302
  102.5 1.9 %collective-permute-start.9 = (f32[3,32,256]{2,1,0:T(8,128)S(1)}, f32[3,32,256]{2,1,0:T(8,128)S(1)}, u32[]{:S(2)}, u32[]{:S(2)}) collective-permute-start(f32[3,32,256]{2,1,0:T(8,128)S(1)} %get-tuple-element.41), channel_id=1, source_target_pairs={{16,0},{32,16},{48,32},{64,48},{80,64},{96,80},{112,96},{17,1},{33... | collective-permute-start | bytes 294920 | tf_op jit(solution)/shard_map/ppermute | solution.py:302
  104.5 4.6 %collective-permute-start.10 = (f32[3,16,256]{2,1,0:T(8,128)S(1)}, f32[3,16,256]{2,1,0:T(8,128)S(1)}, u32[]{:S(2)}, u32[]{:S(2)}) collective-permute-start(f32[3,16,256]{2,1,0:T(8,128)S(1)} %get-tuple-element.42), channel_id=1, source_target_pairs={{0,1},{1,2},{2,3},{3,4},{4,5},{5,6},{6,7},{7,8},{8,9},{9,10},{10,1... | collective-permute-start | bytes 147464 | tf_op jit(solution)/shard_map/ppermute | solution.py:302
  110.4 3.8 %collective-permute-done.11.refs_8_ = f32[3,16,256]{2,1,0:T(8,128)S(1)} collective-permute-done((f32[3,16,256]{2,1,0:T(8,128)S(1)}, f32[3,16,256]{2,1,0:T(8,128)S(1)}, u32[]{:S(2)}, u32[]{:S(2)}) %collective-permute-start.11) | collective-permute-done | bytes 49184 | tf_op jit(solution)/shard_map/ppermute | solution.py:302
  114.2 2.3 %sweep_cells.5 = f32[3,16,32,256]{3,2,1,0:T(8,128)} custom-call(f32[3,16,32,256]{3,2,1,0:T(8,128)S(1)} %get-tuple-element.39.refs_0_, f32[3,16,32,256]{3,2,1,0:T(8,128)S(1)} %bitcast.29, f32[3,16,32,256]{3,2,1,0:T(8,128)S(1)} %fusion.refs_2_, f32[16,32,256]{2,1,0:T(8,128)S(1)} %copy-done.1, f32[9,16,32,256]{3,2,1,0:T(8,128)S(1)} %copy-done, ...), custom_call_target="tpu_custom_call" | custom-call | tf_op jit(solution)/shard_map/sweep_cells/pallas_call | solution.py:290
  116.5 1.4 copy-done.2
  117.9 15.2 %gather_rows.1 = f32[128,2,128]{2,1,0:T(2,128)S(1)} custom-call(s32[2,32]{1,0:T(2,128)S(1)} %pad_add_fusion.ends, f32[3,512,256]{2,1,0:T(8,128)S(1)} %bitcast.31, s32[128,128]{1,0:T(8,128)S(1)} %bitcast.35, f32[128,128]{1,0:T(8,128)S(1)} %bitcast.36, f32[128,128]{1,0:T(8,128)S(1)} %bitcast.37), custom_call_target="tpu_custom_call" | custom-call | tf_op jit(solution)/shard_map/gather_rows/pallas_call | solution.py:395
  133.1 23.9 %all_to_all.10 = f32[128,2,128]{2,1,0:T(2,128)S(1)} all-to-all(f32[128,2,128]{2,1,0:T(2,128)S(1)} %gather_rows.1), channel_id=1, replica_groups=mesh['gx'=8,'gy'=16] {'gx','gy'}, dimensions={0} | all-to-all | bytes 262144 | tf_op jit(solution)/shard_map/all_to_all | solution.py:412
  (39 shorter events, 13.1 us)
Async XLA Ops:
  0.6 0.9 copy-start.3
  1.5 0.8 copy-start.4
  2.3 0.8 copy-start.5
  3.1 0.8 copy-start.6
  3.8 0.8 copy-start.7
  4.6 0.8 copy-start.8
  18.2 24.8 %all-to-all-start = ((f32[128,8,128]{2,1,0:T(8,128)}), f32[128,8,128]{2,1,0:T(8,128)S(1)}, u32[]{:S(2)}, u32[]{:S(2)}) async-start(f32[128,8,128]{2,1,0:T(8,128)} %pack_rows.1), calls=%async_computation | async-start | bytes 1048576 | tf_op jit(solution)/shard_map/all_to_all | solution.py:412
  29.7 1.7 %copy-start.1 = (f32[16,32,256]{2,1,0:T(8,128)S(1)}, f32[16,32,256]{2,1,0:T(8,128)}, u32[]{:S(2)}) copy-start(f32[16,32,256]{2,1,0:T(8,128)} %refs_3_.5) | copy-start | bytes 1572868
  29.7 2.0 %copy-start.9 = (f32[3,16,32,256]{3,2,1,0:T(8,128)S(1)}, f32[3,16,32,256]{3,2,1,0:T(8,128)}, u32[]{:S(2)}) copy-start(f32[3,16,32,256]{3,2,1,0:T(8,128)} %param.16) | copy-start | bytes 4718596
  68.1 12.0 %collective-permute-start = (f32[3,32,256]{2,1,0:T(8,128)S(1)}, f32[3,32,256]{2,1,0:T(8,128)S(1)}, u32[]{:S(2)}, u32[]{:S(2)}) collective-permute-start(f32[3,32,256]{2,1,0:T(8,128)S(1)} %get-tuple-element.30), channel_id=1, source_target_pairs={{0,16},{16,32},{32,48},{48,64},{64,80},{80,96},{96,112},{1,17},{17... | collective-permute-start | bytes 294920 | tf_op jit(solution)/shard_map/ppermute | solution.py:302
  70.8 9.3 %collective-permute-start.1 = (f32[3,32,256]{2,1,0:T(8,128)S(1)}, f32[3,32,256]{2,1,0:T(8,128)S(1)}, u32[]{:S(2)}, u32[]{:S(2)}) collective-permute-start(f32[3,32,256]{2,1,0:T(8,128)S(1)} %get-tuple-element.31), channel_id=1, source_target_pairs={{16,0},{32,16},{48,32},{64,48},{80,64},{96,80},{112,96},{17,1},{33... | collective-permute-start | bytes 294920 | tf_op jit(solution)/shard_map/ppermute | solution.py:302
  72.8 3.3 %collective-permute-start.2 = (f32[3,16,256]{2,1,0:T(8,128)S(1)}, f32[3,16,256]{2,1,0:T(8,128)S(1)}, u32[]{:S(2)}, u32[]{:S(2)}) collective-permute-start(f32[3,16,256]{2,1,0:T(8,128)S(1)} %get-tuple-element.32), channel_id=1, source_target_pairs={{0,1},{1,2},{2,3},{3,4},{4,5},{5,6},{6,7},{7,8},{8,9},{9,10},{10,1... | collective-permute-start | bytes 147464 | tf_op jit(solution)/shard_map/ppermute | solution.py:302
  74.6 5.5 %collective-permute-start.3 = (f32[3,16,256]{2,1,0:T(8,128)S(1)}, f32[3,16,256]{2,1,0:T(8,128)S(1)}, u32[]{:S(2)}, u32[]{:S(2)}) collective-permute-start(f32[3,16,256]{2,1,0:T(8,128)S(1)} %get-tuple-element.33), channel_id=1, source_target_pairs={{1,0},{2,1},{3,2},{4,3},{5,4},{6,5},{7,6},{8,7},{9,8},{10,9},{11,1... | collective-permute-start | bytes 147464 | tf_op jit(solution)/shard_map/ppermute | solution.py:302
  80.1 2.3 %copy-start = (f32[9,16,32,256]{3,2,1,0:T(8,128)S(1)}, f32[9,16,32,256]{3,2,1,0:T(8,128)}, u32[]{:S(2)}) copy-start(f32[9,16,32,256]{3,2,1,0:T(8,128)} %refs_4_.5) | copy-start | bytes 14155780
  83.6 12.6 %collective-permute-start.4 = (f32[3,32,256]{2,1,0:T(8,128)S(1)}, f32[3,32,256]{2,1,0:T(8,128)S(1)}, u32[]{:S(2)}, u32[]{:S(2)}) collective-permute-start(f32[3,32,256]{2,1,0:T(8,128)S(1)} %get-tuple-element.35), channel_id=1, source_target_pairs={{0,16},{16,32},{32,48},{48,64},{64,80},{80,96},{96,112},{1,17},{17... | collective-permute-start | bytes 294920 | tf_op jit(solution)/shard_map/ppermute | solution.py:302
  87.5 8.7 %collective-permute-start.5 = (f32[3,32,256]{2,1,0:T(8,128)S(1)}, f32[3,32,256]{2,1,0:T(8,128)S(1)}, u32[]{:S(2)}, u32[]{:S(2)}) collective-permute-start(f32[3,32,256]{2,1,0:T(8,128)S(1)} %get-tuple-element.36), channel_id=1, source_target_pairs={{16,0},{32,16},{48,32},{64,48},{80,64},{96,80},{112,96},{17,1},{33... | collective-permute-start | bytes 294920 | tf_op jit(solution)/shard_map/ppermute | solution.py:302
  89.5 3.3 %collective-permute-start.6 = (f32[3,16,256]{2,1,0:T(8,128)S(1)}, f32[3,16,256]{2,1,0:T(8,128)S(1)}, u32[]{:S(2)}, u32[]{:S(2)}) collective-permute-start(f32[3,16,256]{2,1,0:T(8,128)S(1)} %get-tuple-element.37), channel_id=1, source_target_pairs={{0,1},{1,2},{2,3},{3,4},{4,5},{5,6},{6,7},{7,8},{8,9},{9,10},{10,1... | collective-permute-start | bytes 147464 | tf_op jit(solution)/shard_map/ppermute | solution.py:302
  91.4 4.8 %collective-permute-start.7 = (f32[3,16,256]{2,1,0:T(8,128)S(1)}, f32[3,16,256]{2,1,0:T(8,128)S(1)}, u32[]{:S(2)}, u32[]{:S(2)}) collective-permute-start(f32[3,16,256]{2,1,0:T(8,128)S(1)} %get-tuple-element.38), channel_id=1, source_target_pairs={{1,0},{2,1},{3,2},{4,3},{5,4},{6,5},{7,6},{8,7},{9,8},{10,9},{11,1... | collective-permute-start | bytes 147464 | tf_op jit(solution)/shard_map/ppermute | solution.py:302
  97.5 16.8 %collective-permute-start.8 = (f32[3,32,256]{2,1,0:T(8,128)S(1)}, f32[3,32,256]{2,1,0:T(8,128)S(1)}, u32[]{:S(2)}, u32[]{:S(2)}) collective-permute-start(f32[3,32,256]{2,1,0:T(8,128)S(1)} %get-tuple-element.40), channel_id=1, source_target_pairs={{0,16},{16,32},{32,48},{48,64},{64,80},{80,96},{96,112},{1,17},{17... | collective-permute-start | bytes 294920 | tf_op jit(solution)/shard_map/ppermute | solution.py:302
  102.5 11.7 %collective-permute-start.9 = (f32[3,32,256]{2,1,0:T(8,128)S(1)}, f32[3,32,256]{2,1,0:T(8,128)S(1)}, u32[]{:S(2)}, u32[]{:S(2)}) collective-permute-start(f32[3,32,256]{2,1,0:T(8,128)S(1)} %get-tuple-element.41), channel_id=1, source_target_pairs={{16,0},{32,16},{48,32},{64,48},{80,64},{96,80},{112,96},{17,1},{33... | collective-permute-start | bytes 294920 | tf_op jit(solution)/shard_map/ppermute | solution.py:302
  104.5 5.9 %collective-permute-start.10 = (f32[3,16,256]{2,1,0:T(8,128)S(1)}, f32[3,16,256]{2,1,0:T(8,128)S(1)}, u32[]{:S(2)}, u32[]{:S(2)}) collective-permute-start(f32[3,16,256]{2,1,0:T(8,128)S(1)} %get-tuple-element.42), channel_id=1, source_target_pairs={{0,1},{1,2},{2,3},{3,4},{4,5},{5,6},{6,7},{7,8},{8,9},{9,10},{10,1... | collective-permute-start | bytes 147464 | tf_op jit(solution)/shard_map/ppermute | solution.py:302
  109.1 5.1 %collective-permute-start.11 = (f32[3,16,256]{2,1,0:T(8,128)S(1)}, f32[3,16,256]{2,1,0:T(8,128)S(1)}, u32[]{:S(2)}, u32[]{:S(2)}) collective-permute-start(f32[3,16,256]{2,1,0:T(8,128)S(1)} %get-tuple-element.43), channel_id=1, source_target_pairs={{1,0},{2,1},{3,2},{4,3},{5,4},{6,5},{7,6},{8,7},{9,8},{10,9},{11,1... | collective-permute-start | bytes 147464 | tf_op jit(solution)/shard_map/ppermute | solution.py:302
  116.5 1.4 copy-start.2

commit v4 on v3

--- a/solution.py
+++ b/solution.py
@@ -12,7 +12,8 @@
 STEP_ROWS = 512
 RANK_ROWS = 256
 WINDOW = 32
-SIDE = 4
+SIDE = 8
+PARTS = 4
 CELL_SHIFT = 257
 MIB = 1024 * 1024
 
@@ -41,6 +42,7 @@
     ranks, upper, left, right, total, arrivals = refs[13:]
     sens, weight, device, cell, owner, slot = kept
     devices, _, capacity = rows.shape
+    half = capacity // 2
     part = upper.shape[0]
     step = STEP_ROWS
     steps = sens.shape[1] // step
@@ -75,10 +77,12 @@
     def chunk(i, _):
         for b in range(2):
             at = pl.ds(pl.multiple_of((i * 2 + b) * step, step), step)
-            ones = marked(places(devices, step) == device[:, at], 1.0)
+            rank = ranks[:, at]
+            lane = device[:, at] + jnp.where(rank >= half, devices, 0)
+            ones = marked(places(2 * devices, step) == lane, 1.0)
             left[b, :, :step] = ones
             left[b, :, step:] = ones
-            here = places(capacity, step) == ranks[:, at]
+            here = places(half, step) == (rank & (half - 1))
             own_cell = cell[:, at]
             pairs = [halves(sens[k : k + 1, at]) for k in range(3)]
             pairs.append(
@@ -92,15 +96,16 @@
                 ((owner[:, at] * BOX_DEV).astype(jnp.float32), slot[:, at].astype(jnp.float32))
             )
             for p, (high, low) in enumerate(pairs):
-                band = slice(p * capacity, (p + 1) * capacity)
+                band = slice(p * half, (p + 1) * half)
                 right[b, band, :step] = marked(here, high)
                 right[b, band, step:] = marked(here, low)
-        total[...] += dot_last(left[0], right[0]) + dot_last(left[1], right[1])
+        total[...] += dot_last(right[0], left[0]) + dot_last(right[1], left[1])
         return 0
 
     lax.fori_loop(0, steps // 2, chunk, 0)
     for p in range(6):
-        rows[:, p, :] = total[:, p * capacity : (p + 1) * capacity]
+        band = total[p * half : (p + 1) * half, :]
+        rows[:, p, :] = jnp.concatenate([band[:, :devices].T, band[:, devices:].T], axis=1)
     for p in range(6, 8):
         rows[:, p, :] = jnp.zeros((devices, capacity), jnp.float32)
 
@@ -116,12 +121,12 @@
         + [
             pltpu.VMEM((1, count), jnp.int32),
             pltpu.VMEM((RANK_ROWS, RANK_ROWS), jnp.bfloat16),
-            pltpu.VMEM((2, devices, 2 * STEP_ROWS), jnp.bfloat16),
-            pltpu.VMEM((2, 6 * capacity, 2 * STEP_ROWS), jnp.bfloat16),
-            pltpu.VMEM((devices, 6 * capacity), jnp.float32),
+            pltpu.VMEM((2, 2 * devices, 2 * STEP_ROWS), jnp.bfloat16),
+            pltpu.VMEM((2, 3 * capacity, 2 * STEP_ROWS), jnp.bfloat16),
+            pltpu.VMEM((3 * capacity, 2 * devices), jnp.float32),
             pltpu.SemaphoreType.DMA((len(given),)),
         ],
-        compiler_params=pltpu.CompilerParams(vmem_limit_bytes=20 * MIB),
+        compiler_params=pltpu.CompilerParams(vmem_limit_bytes=58 * MIB),
         name="pack_rows",
     )(*given)
 
@@ -141,11 +146,21 @@
     return lax.fori_loop(0, groups, count, 0)
 
 
-def scatter_kernel(ends, cells, one, two, three, inverse, stiff, load, field, *rest):
-    head_x, tail_x, head_y, tail_y, left, right = rest
+def scatter_kernel(*refs):
+    ends, cells, one, two, three, stiff_at, anchor_at, coupling_at = refs[:8]
+    load, scaled, inverse, stiff, head_x, tail_x, head_y, tail_y = refs[8:16]
+    anchor, coupling, left, right, arrivals = refs[16:]
+    copies = [
+        pltpu.make_async_copy(source, target, arrivals.at[p])
+        for p, (source, target) in enumerate(
+            ((stiff_at, stiff), (anchor_at, anchor), (coupling_at, coupling))
+        )
+    ]
+    for copy in copies:
+        copy.start()
     height, depth = load.shape[1:]
     lines, width = cells.shape
-    half = depth // 2
+    part = depth // PARTS
     group = STEP_ROWS // width
     step = STEP_ROWS
     load[...] = jnp.zeros_like(load)
@@ -153,10 +168,10 @@
     def fill(i, b):
         for q in range(group):
             row = pl.ds(i * group + q, 1)
-            there = places(half, width) == (cells[row, :] & (half - 1))
+            there = places(part, width) == (cells[row, :] & (part - 1))
             for k, sens in enumerate((one, two, three)):
                 high, low = halves(sens[row, :])
-                band = slice(k * half, (k + 1) * half)
+                band = slice(k * part, (k + 1) * part)
                 right[b, band, q * width : (q + 1) * width] = marked(there, high)
                 right[b, band, step + q * width : step + (q + 1) * width] = marked(there, low)
 
@@ -165,18 +180,23 @@
         base = pl.multiple_of(jnp.minimum(least, height - WINDOW), 8)
         for q in range(group):
             cell = cells[pl.ds(i * group + q, 1), :]
-            hot = marked(places(2 * WINDOW, width) == window_place(cell, least, base), 1.0)
+            place = window_place(cell, least, base, PARTS)
+            hot = marked(places(PARTS * WINDOW, width) == place, 1.0)
             left[b, :, q * width : (q + 1) * width] = hot
             left[b, :, step + q * width : step + (q + 1) * width] = hot
         sums = dot_last(left[b], right[b])
 
         def add():
             for k in range(3):
-                for side in range(2):
-                    at = (k, pl.ds(base, WINDOW), slice(side * half, (side + 1) * half))
-                    load[at] += sums[
-                        side * WINDOW : (side + 1) * WINDOW, k * half : (k + 1) * half
-                    ]
+                for side in range(PARTS // 2):
+                    at = (k, pl.ds(base, WINDOW), slice(side * 2 * part, (side + 1) * 2 * part))
+                    load[at] += jnp.concatenate(
+                        [
+                            sums[p * WINDOW : (p + 1) * WINDOW, k * part : (k + 1) * part]
+                            for p in (2 * side, 2 * side + 1)
+                        ],
+                        axis=1,
+                    )
 
         return add
 
@@ -198,50 +218,70 @@
         return 0
 
     lax.fori_loop(filled(ends), lines // group // SIDE, chunks, 0)
+    for copy in copies:
+        copy.wait()
     size_x, size_y = head_y.shape[1], head_x.shape[1]
-    for k in range(3):
-        field[k] = load[k] * inverse[k]
-        head_x[k] = field[k, :size_y] * stiff[:size_y]
-        tail_x[k] = field[k, height - size_y :] * stiff[height - size_y :]
-        for x in range(size_x):
-            for y, face in ((0, head_y), (size_y - 1, tail_y)):
-                at = slice(x * size_y + y, x * size_y + y + 1)
-                face[k, x : x + 1] = field[k, at] * stiff[at]
-
-
-def window_place(cell, least, base):
+    for x in range(size_x):
+        at = slice(x * size_y, (x + 1) * size_y)
+        weight = stiff[at]
+        for k in range(3):
+            own = 1.0 / (6.0 * weight + anchor[k, at] + coupling[4 * k, at])
+            inverse[k, at] = own
+            for place, j in enumerate(others(k)):
+                scaled[2 * k + place, at] = coupling[3 * j + k, at] * own
+            fresh = load[k, at] * own
+            load[k, at] = fresh
+            moved = weight * fresh
+            if x == 0:
+                head_x[k] = moved
+            if x == size_x - 1:
+                tail_x[k] = moved
+            head_y[k, x : x + 1] = moved[:1]
+            tail_y[k, x : x + 1] = moved[size_y - 1 :]
+
+
+def window_place(cell, least, base, parts):
     line = cell >> 8
-    place = ((cell >> 7) & 1) * WINDOW + line - base
+    place = ((cell & 255) * parts >> 8) * WINDOW + line - base
     inside = (line >= least) & (line < base + WINDOW)
     return jnp.where(inside, place, -1)
 
 
-def scatter(ends, cells, values, inverse, stiff):
+def scatter(ends, cells, values, stiff, anchor, coupling):
     size_x, size_y, depth = stiff.shape
     height = size_x * size_y
     vmem = pl.BlockSpec(memory_space=pltpu.VMEM)
-    cube = (3, height, depth)
-    shapes = [cube] * 2 + [(3, size_y, depth)] * 2 + [(3, size_x, depth)] * 2
-    load, field, *faces = pl.pallas_call(
+    shapes = [(3, height, depth), (6, height, depth), (3, height, depth), (height, depth)]
+    shapes += [(3, size_y, depth)] * 2 + [(3, size_x, depth)] * 2
+    outs = pl.pallas_call(
         scatter_kernel,
-        in_specs=[pl.BlockSpec(memory_space=pltpu.SMEM)] + [vmem] * 6,
-        out_specs=[vmem] * 6,
+        in_specs=[pl.BlockSpec(memory_space=pltpu.SMEM)]
+        + [vmem] * 4
+        + [pl.BlockSpec(memory_space=pltpu.HBM)] * 3,
+        out_specs=[vmem] * 8,
         out_shape=[jax.ShapeDtypeStruct(shape, jnp.float32) for shape in shapes],
         scratch_shapes=[
-            pltpu.VMEM((SIDE, 2 * WINDOW, 2 * STEP_ROWS), jnp.bfloat16),
-            pltpu.VMEM((SIDE, 3 * depth // 2, 2 * STEP_ROWS), jnp.bfloat16),
+            pltpu.VMEM((3, height, depth), jnp.float32),
+            pltpu.VMEM((9, height, depth), jnp.float32),
+            pltpu.VMEM((SIDE, PARTS * WINDOW, 2 * STEP_ROWS), jnp.bfloat16),
+            pltpu.VMEM((SIDE, 3 * depth // PARTS, 2 * STEP_ROWS), jnp.bfloat16),
+            pltpu.SemaphoreType.DMA((3,)),
         ],
-        compiler_params=pltpu.CompilerParams(vmem_limit_bytes=20 * MIB),
+        compiler_params=pltpu.CompilerParams(vmem_limit_bytes=24 * MIB),
         name="scatter_rows",
-    )(ends, cells, *values, inverse.reshape(cube), stiff.reshape(cube[1:]))
-    whole = (3, size_x, size_y, depth)
-    return load.reshape(whole), field.reshape(whole), faces
-
-
-def sweep_kernel(last, field, load, inverse, stiff, coupling, west, east, south, north, *outs):
+    )(
+        ends,
+        cells,
+        *values,
+        *(part.reshape(*part.shape[:-3], height, depth) for part in (stiff, anchor, coupling)),
+    )
+    cells_of = [part.reshape(*part.shape[:-2], size_x, size_y, depth) for part in outs[:4]]
+    return cells_of, outs[4:]
+
+
+def swept(first, scaled, inverse, stiff, field, halo, padded, store):
     _, size_x, size_y, size_z = field.shape
-    padded = outs[-1]
-    result = outs[0]
+    south, north, west, east = halo
     padded[:, 0] = west[...]
     padded[:, size_x + 1] = east[...]
     for x in range(size_x):
@@ -253,7 +293,7 @@
         own = [field[k, x] for k in range(3)]
         for k in range(3):
             middle = padded[k, x + 1]
-            total = load[k, x] + padded[k, x] + padded[k, x + 2]
+            total = padded[k, x] + padded[k, x + 2]
             total = total + jnp.where(row == 0, south[k, x : x + 1], pltpu.roll(middle, 1, 0))
             total = total + jnp.where(
                 row == size_y - 1, north[k, x : x + 1], pltpu.roll(middle, size_y - 1, 0)
@@ -262,38 +302,43 @@
             total = total + jnp.where(
                 column == size_z - 1, 0.0, pltpu.roll(middle, size_z - 1, 1)
             )
-            for j in range(3):
-                if j != k:
-                    total = total - coupling[3 * j + k, x] * own[j]
-            fresh = total * inverse[k, x]
-            result[k, x] = fresh
-            if not last:
-                head_x, tail_x, head_y, tail_y = outs[1:5]
-                moved = stiff[x] * fresh
-                if x == 0:
-                    head_x[k] = moved
-                if x == size_x - 1:
-                    tail_x[k] = moved
-                head_y[k, x : x + 1] = moved[:1]
-                tail_y[k, x : x + 1] = moved[size_y - 1 :]
-
-
-def sweep(last, field, load, inverse, stiff, coupling, halo):
-    _, size_x, size_y, size_z = field.shape
-    shapes = [field.shape]
-    if not last:
-        shapes += [(3, size_y, size_z)] * 2 + [(3, size_x, size_z)] * 2
-
-    def kernel(*refs):
-        sweep_kernel(last, *refs)
-
+            fresh = first[k, x] + total * inverse[k, x]
+            for place, j in enumerate(others(k)):
+                fresh = fresh - scaled[2 * k + place, x] * own[j]
+            store(k, x, fresh)
+
+
+def others(k):
+    return [j for j in range(3) if j != k]
+
+
+def sweep_kernel(first, scaled, inverse, stiff, field, south, north, west, east, *outs):
+    result, head_x, tail_x, head_y, tail_y, padded = outs
+    size_x, size_y = field.shape[1:3]
+
+    def store(k, x, fresh):
+        result[k, x] = fresh
+        moved = stiff[x] * fresh
+        if x == 0:
+            head_x[k] = moved
+        if x == size_x - 1:
+            tail_x[k] = moved
+        head_y[k, x : x + 1] = moved[:1]
+        tail_y[k, x : x + 1] = moved[size_y - 1 :]
+
+    swept(first, scaled, inverse, stiff, field, (south, north, west, east), padded, store)
+
+
+def sweep(*given):
+    _, size_x, size_y, size_z = given[0].shape
+    shapes = [given[0].shape] + [(3, size_y, size_z)] * 2 + [(3, size_x, size_z)] * 2
     return pl.pallas_call(
-        kernel,
+        sweep_kernel,
         out_shape=[jax.ShapeDtypeStruct(shape, jnp.float32) for shape in shapes],
         scratch_shapes=[pltpu.VMEM((3, size_x + 2, size_y, size_z), jnp.float32)],
-        compiler_params=pltpu.CompilerParams(vmem_limit_bytes=24 * MIB),
+        compiler_params=pltpu.CompilerParams(vmem_limit_bytes=8 * MIB),
         name="sweep_cells",
-    )(field, load, inverse, stiff, coupling, *halo)
+    )(*given)
 
 
 def exchange(head_x, tail_x, head_y, tail_y):
@@ -305,10 +350,20 @@
     north = shifted(head_y, "gy", False)
     west = shifted(tail_x, "gx", True)
     east = shifted(head_x, "gx", False)
-    return west, east, south, north
-
-
-def gather_kernel(ends, field, cells, weights, boxes, sums, hot, left, right, total):
+    return south, north, west, east
+
+
+def gather_kernel(*refs):
+    ends, first, scaled, inverse, stiff, before, south, north, west, east = refs[:10]
+    cells, weights, boxes, final, sums, padded, field, hot, left, right, total, sent = refs[10:]
+    size_y = before.shape[2]
+
+    def store(k, x, fresh):
+        field[k, x * size_y : (x + 1) * size_y] = fresh
+
+    swept(first, scaled, inverse, stiff, before, (south, north, west, east), padded, store)
+    out = pltpu.make_async_copy(field, final, sent)
+    out.start()
     height, depth = field.shape[1:]
     lines, width = cells.shape
     half = depth // 2
@@ -325,17 +380,25 @@
         base = pl.multiple_of(jnp.minimum(least, height - WINDOW), 8)
         own = [cells[row, :] for row in rows(i)]
         for q in range(group):
-            ones = marked(places(2 * WINDOW, width) == window_place(own[q], least, base), 1.0)
+            ones = marked(places(2 * WINDOW, width) == window_place(own[q], least, base, 2), 1.0)
             hot[b, : 2 * WINDOW, q * width : (q + 1) * width] = ones
             hot[b, 2 * WINDOW :, q * width : (q + 1) * width] = ones
         there = [places(half, width) == (cell & (half - 1)) for cell in own]
         picked = []
+        block = jnp.concatenate(
+            [
+                jnp.concatenate(
+                    [field[k, pl.ds(base, WINDOW), side * half : (side + 1) * half] for k in range(3)],
+                    axis=1,
+                )
+                for side in range(2)
+            ],
+            axis=0,
+        )
+        both = jnp.concatenate(halves(block), axis=0).T.astype(jnp.bfloat16)
+        parts = jnp.dot(both, hot[b], preferred_element_type=jnp.float32)
         for k in range(3):
-            block = field[k, pl.ds(base, WINDOW), :]
-            block = jnp.concatenate([block[:, :half], block[:, half:]], axis=0)
-            high, low = halves(block)
-            both = jnp.concatenate([high, low], axis=0).T.astype(jnp.bfloat16)
-            part = jnp.dot(both, hot[b], preferred_element_type=jnp.float32)
+            part = parts[k * half : (k + 1) * half]
             picked.append(
                 jnp.concatenate(
                     [
@@ -381,31 +444,40 @@
             finals.append(lax.fori_loop(1, spans[b][1], more, firsts[b]))
         for b in range(SIDE):
             spread(own[b], b, finals[b])
-        parts = [dot_last(left[b], right[b]) for b in range(SIDE)]
+        parts = [dot_last(right[b], left[b]) for b in range(SIDE)]
         total[...] += sum(parts[1:], parts[0])
         return 0
 
     lax.fori_loop(filled(ends), lines // group // SIDE, chunks, 0)
     for p in range(2):
-        sums[:, p, :] = total[:, p * 128 : (p + 1) * 128]
-
-
-def gather(ends, field, cells, weights, boxes, devices):
+        sums[:, p, :] = total[p * 128 : (p + 1) * 128, :].T
+    out.wait()
+
+
+def gather(ends, swept_from, cells, weights, boxes, devices):
+    _, size_x, size_y, depth = swept_from[0].shape
+    cube = (3, size_x * size_y, depth)
     vmem = pl.BlockSpec(memory_space=pltpu.VMEM)
     return pl.pallas_call(
         gather_kernel,
-        in_specs=[pl.BlockSpec(memory_space=pltpu.SMEM)] + [vmem] * 4,
-        out_specs=vmem,
-        out_shape=jax.ShapeDtypeStruct((devices, 2, 128), jnp.float32),
+        in_specs=[pl.BlockSpec(memory_space=pltpu.SMEM)] + [vmem] * (len(swept_from) + 3),
+        out_specs=[pl.BlockSpec(memory_space=pltpu.HBM), vmem],
+        out_shape=[
+            jax.ShapeDtypeStruct(cube, jnp.float32),
+            jax.ShapeDtypeStruct((devices, 2, 128), jnp.float32),
+        ],
         scratch_shapes=[
+            pltpu.VMEM((3, size_x + 2, size_y, depth), jnp.float32),
+            pltpu.VMEM(cube, jnp.float32),
             pltpu.VMEM((SIDE, 4 * WINDOW, STEP_ROWS), jnp.bfloat16),
             pltpu.VMEM((SIDE, devices, 2 * STEP_ROWS), jnp.bfloat16),
             pltpu.VMEM((SIDE, 4 * BOX_DEV, 2 * STEP_ROWS), jnp.bfloat16),
-            pltpu.VMEM((devices, 4 * BOX_DEV), jnp.float32),
+            pltpu.VMEM((4 * BOX_DEV, devices), jnp.float32),
+            pltpu.SemaphoreType.DMA,
         ],
-        compiler_params=pltpu.CompilerParams(vmem_limit_bytes=16 * MIB),
+        compiler_params=pltpu.CompilerParams(vmem_limit_bytes=32 * MIB),
         name="gather_rows",
-    )(ends, field, cells, weights, boxes)
+    )(ends, *swept_from, cells, weights, boxes)
 
 
 def swapped(blocks):
@@ -443,16 +515,13 @@
     cells, *values, weights, boxes = [part.reshape(-1, 128) for part in ordered]
     blocks = cells.reshape(-1, STEP_ROWS // 128, 128)
     ends = jnp.stack([blocks[:, 0, 0], blocks[:, -1, -1]])
-    diagonal = 6.0 * stiffness[None] + anchor + jnp.stack([coupling[0], coupling[4], coupling[8]])
-    inverse = 1.0 / diagonal
-    load, field, faces = scatter(ends, cells, values, inverse, stiffness)
-    for turn in range(1, SWEEPS):
-        last = turn == SWEEPS - 1
-        field, *faces = sweep(
-            last, field, load, inverse, stiffness, coupling, exchange(*faces)
-        )
-    flat = field.reshape(3, size_x * size_y, size_z)
-    partial = gather(ends, flat, cells, weights, boxes, devices)
+    fixed, faces = scatter(ends, cells, values, stiffness, anchor, coupling)
+    field = fixed[0]
+    for turn in range(1, SWEEPS - 1):
+        field, *faces = sweep(*fixed, field, *exchange(*faces))
+    swept_from = (*fixed, field, *exchange(*faces))
+    field, partial = gather(ends, swept_from, cells, weights, boxes, devices)
+    field = field.reshape(3, size_x, size_y, size_z)
     summed = jnp.sum(swapped(partial), axis=0).reshape(4, BOX_DEV)
     return (field, summed[:3])
 

time: 157 us -> 144 us (0.917)
  blocking collectives: 23.9 us -> 43 us
  starting transfers between devices: 41.2 us -> 31.9 us
  local copies, waits for them, and re-layouts: 12.7 us -> 4.5 us
  waiting for transfers between devices: 22.4 us -> 14.2 us
  Pallas kernels: 44.4 us -> 37 us
    all_to_all x1 -> x2, blocking collectives: 23.9 us -> 43 us  [swapped(): return lax.all_to_all(blocks, AXES, split_axis=0, concat_axis=0, tiled=True)]
    all_to_all x1 -> x0, starting transfers between devices: 11.5 us -> none  [swapped(): return lax.all_to_all(blocks, AXES, split_axis=0, concat_axis=0, tiled=True)]
    all_to_all x1 -> x0, waiting for transfers between devices: 10.8 us -> none  [swapped(): return lax.all_to_all(blocks, AXES, split_axis=0, concat_axis=0, tiled=True)]
    unnamed x20 -> x6, local copies, waits for them, and re-layouts: 8.73 us -> 2.34 us
    pallas_call x1, Pallas kernels: 12.8 us -> 9.5 us  [pack(): pl.pallas_call(pack_kernel, in_specs=[pl.BlockSpec(memory_space=pltpu.HBM...]
    ppermute x12, waiting for transfers between devices: 11.6 us -> 14.2 us  [shifted(): return lax.ppermute(face, axis, pairs)]
    ppermute x12, starting transfers between devices: 29.7 us -> 31.9 us  [shifted(): return lax.ppermute(face, axis, pairs)]
    pallas_call x3 -> x2, Pallas kernels: 4.65 us -> 2.64 us  [sweep(): pl.pallas_call(sweep_kernel, out_shape=[jax.ShapeDtypeStruct(shape, jnp.f...]
  transfers between devices with their start and end apart: 13 -> 12, of which waited for: 5 -> 3; matrix products, arithmetic and copies ran while one was open for 1% -> 0% of each run, Pallas kernels for 0% -> 0%
where the time goes in v4:
time: 144 us; the launch traced here: 143 us
  blocking collectives  43 us (30%)
  Pallas kernels  37 us (26%)
  starting transfers between devices  31.9 us (22%)
  waiting for transfers between devices  14.2 us (10%)
  other arithmetic  11.8 us (8%)
  local copies, waits for them, and re-layouts  4.5 us (3%)
    all_to_all x2, blocking collectives, swapped(): return lax.all_to_all(blocks, AXES, split_axis=0, concat_axis=0, tiled=True)  43 us
    ppermute x12, starting transfers between devices, shifted(): return lax.ppermute(face, axis, pairs)  31.9 us
    pallas_call x1, Pallas kernels, gather(): pl.pallas_call(gather_kernel, in_specs=[pl.BlockSpec(memory_space=pltpu.S...  14.9 us
    ppermute x12, waiting for transfers between devices, shifted(): return lax.ppermute(face, axis, pairs)  14.2 us
    sort x1, other arithmetic, body(): lax.sort((keys, *planes[:3], *planes[4:]), num_keys=1, is_stable=False)  11.5 us
    pallas_call x1, Pallas kernels, scatter(): pl.pallas_call(scatter_kernel, in_specs=[pl.BlockSpec(memory_space=pltpu....  9.94 us
    pallas_call x1, Pallas kernels, pack(): pl.pallas_call(pack_kernel, in_specs=[pl.BlockSpec(memory_space=pltpu.HBM...  9.5 us
  transfers between devices with their start and end apart: 12, of which 3 were waited for; matrix products, arithmetic and copies ran while one was open for 0% of the time, Pallas kernels for 0%

profile of v4, /device:TPU:1, one launch (start us, length us, event | category | flops | bytes accessed | tf_op | source)
XLA Modules:
  0.0 143.3 jit_solution(9160098744764583608)
XLA Ops:
  0.7 9.5 %pack_rows.1 = f32[128,8,128]{2,1,0:T(8,128)} custom-call(f32[3,8192]{1,0:T(4,128)} %refs_0_.1, f32[1,8192]{1,0:T(1,128)} %bitcast.59, s32[1,8192]{1,0:T(1,128)} %bitcast.60, s32[1,8192]{1,0:T(1,128)} %bitcast.61, s32[1,8192]{1,0:T(1,128)} %bitcast.62, s32[1,8192]{1,0:T(1,128)} %bitcast.63), custom_call_target="tpu_custom_call" | custom-call | tf_op jit(solution)/shard_map/pack_rows/pallas_call | solution.py:116
  10.2 24.9 %all_to_all.10 = f32[128,8,128]{2,1,0:T(8,128)S(1)} all-to-all(f32[128,8,128]{2,1,0:T(8,128)} %pack_rows.1), channel_id=1, replica_groups=mesh['gx'=8,'gy'=16] {'gx','gy'}, dimensions={0} | all-to-all | bytes 1048576 | tf_op jit(solution)/shard_map/all_to_all | solution.py:484
  35.4 11.5 %sort.39 = (s32[16384]{0:T(1024)S(1)}, f32[16384]{0:T(1024)S(1)}, f32[16384]{0:T(1024)S(1)}, f32[16384]{0:T(1024)S(1)}, f32[16384]{0:T(1024)S(1)}, /*index=5*/f32[16384]{0:T(1024)S(1)}) sort(s32[16384]{0:T(1024)S(1)} %bitcast.58, f32[16384]{0:T(1024)S(1)} %bitcast.57, f32[16384]{0:T(1024)S(1)} %bitcast.56, f32[16384]{0:T(1024)S(1)} %bitcast.55, ...), dimensions={0}, to_apply=%region_0.0 | sort | flops 229376 | bytes 786432 | tf_op jit(solution)/shard_map/sort | solution.py:514
  48.2 2.3 %copy-done = f32[9,16,32,256]{3,2,1,0:T(8,128)S(1)} copy-done((f32[9,16,32,256]{3,2,1,0:T(8,128)S(1)}, f32[9,16,32,256]{3,2,1,0:T(8,128)}, u32[]{:S(2)}) %copy-start) | copy-done | bytes 4718616
  50.6 9.9 %scatter_rows.1 = (f32[3,512,256]{2,1,0:T(8,128)S(1)}, f32[6,512,256]{2,1,0:T(8,128)S(1)}, f32[3,512,256]{2,1,0:T(8,128)S(1)}, f32[512,256]{1,0:T(8,128)S(1)}, f...) custom-call(s32[2,32]{1,0:T(2,128)S(1)} %pad_add_fusion.refs_0_, ...), custom_call_target="tpu_custom_call" | custom-call | tf_op jit(solution)/shard_map/scatter_rows/pallas_call | solution.py:256
  60.5 3.1 %collective-permute-start.2 = (f32[3,32,256]{2,1,0:T(8,128)S(1)}, f32[3,32,256]{2,1,0:T(8,128)S(1)}, u32[]{:S(2)}, u32[]{:S(2)}) collective-permute-start(f32[3,32,256]{2,1,0:T(8,128)S(1)} %get-tuple-element.38), channel_id=1, source_target_pairs={{0,16},{16,32},{32,48},{48,64},{64,80},{80,96},{96,112},{1,17},{17... | collective-permute-start | bytes 294920 | tf_op jit(solution)/shard_map/ppermute | solution.py:347
  63.6 1.9 %collective-permute-start.3 = (f32[3,32,256]{2,1,0:T(8,128)S(1)}, f32[3,32,256]{2,1,0:T(8,128)S(1)}, u32[]{:S(2)}, u32[]{:S(2)}) collective-permute-start(f32[3,32,256]{2,1,0:T(8,128)S(1)} %get-tuple-element.39), channel_id=1, source_target_pairs={{16,0},{32,16},{48,32},{64,48},{80,64},{96,80},{112,96},{17,1},{33... | collective-permute-start | bytes 294920 | tf_op jit(solution)/shard_map/ppermute | solution.py:347
  65.6 1.7 %collective-permute-start = (f32[3,16,256]{2,1,0:T(8,128)S(1)}, f32[3,16,256]{2,1,0:T(8,128)S(1)}, u32[]{:S(2)}, u32[]{:S(2)}) collective-permute-start(f32[3,16,256]{2,1,0:T(8,128)S(1)} %get-tuple-element.36), channel_id=1, source_target_pairs={{0,1},{1,2},{2,3},{3,4},{4,5},{5,6},{6,7},{7,8},{8,9},{9,10},{10,1... | collective-permute-start | bytes 147464 | tf_op jit(solution)/shard_map/ppermute | solution.py:347
  67.3 1.3 collective-permute-start.1
  68.6 4.3 %collective-permute-done.1.north = f32[3,16,256]{2,1,0:T(8,128)S(1)} collective-permute-done((f32[3,16,256]{2,1,0:T(8,128)S(1)}, f32[3,16,256]{2,1,0:T(8,128)S(1)}, u32[]{:S(2)}, u32[]{:S(2)}) %collective-permute-start.1) | collective-permute-done | bytes 49184 | tf_op jit(solution)/shard_map/ppermute | solution.py:347
  72.9 1.3 sweep_cells.2
  74.2 4.3 %collective-permute-start.6 = (f32[3,32,256]{2,1,0:T(8,128)S(1)}, f32[3,32,256]{2,1,0:T(8,128)S(1)}, u32[]{:S(2)}, u32[]{:S(2)}) collective-permute-start(f32[3,32,256]{2,1,0:T(8,128)S(1)} %get-tuple-element.43), channel_id=1, source_target_pairs={{0,16},{16,32},{32,48},{48,64},{64,80},{80,96},{96,112},{1,17},{17... | collective-permute-start | bytes 294920 | tf_op jit(solution)/shard_map/ppermute | solution.py:347
  78.5 1.9 %collective-permute-start.7 = (f32[3,32,256]{2,1,0:T(8,128)S(1)}, f32[3,32,256]{2,1,0:T(8,128)S(1)}, u32[]{:S(2)}, u32[]{:S(2)}) collective-permute-start(f32[3,32,256]{2,1,0:T(8,128)S(1)} %get-tuple-element.44), channel_id=1, source_target_pairs={{16,0},{32,16},{48,32},{64,48},{80,64},{96,80},{112,96},{17,1},{33... | collective-permute-start | bytes 294920 | tf_op jit(solution)/shard_map/ppermute | solution.py:347
  80.5 2.6 %collective-permute-start.4 = (f32[3,16,256]{2,1,0:T(8,128)S(1)}, f32[3,16,256]{2,1,0:T(8,128)S(1)}, u32[]{:S(2)}, u32[]{:S(2)}) collective-permute-start(f32[3,16,256]{2,1,0:T(8,128)S(1)} %get-tuple-element.41), channel_id=1, source_target_pairs={{0,1},{1,2},{2,3},{3,4},{4,5},{5,6},{6,7},{7,8},{8,9},{9,10},{10,1... | collective-permute-start | bytes 147464 | tf_op jit(solution)/shard_map/ppermute | solution.py:347
  83.1 1.3 collective-permute-start.5
  84.4 6.1 %collective-permute-done.5.north = f32[3,16,256]{2,1,0:T(8,128)S(1)} collective-permute-done((f32[3,16,256]{2,1,0:T(8,128)S(1)}, f32[3,16,256]{2,1,0:T(8,128)S(1)}, u32[]{:S(2)}, u32[]{:S(2)}) %collective-permute-start.5) | collective-permute-done | bytes 49184 | tf_op jit(solution)/shard_map/ppermute | solution.py:347
  90.4 1.3 sweep_cells.3
  91.8 4.8 %collective-permute-start.10 = (f32[3,32,256]{2,1,0:T(8,128)S(1)}, f32[3,32,256]{2,1,0:T(8,128)S(1)}, u32[]{:S(2)}, u32[]{:S(2)}) collective-permute-start(f32[3,32,256]{2,1,0:T(8,128)S(1)} %get-tuple-element.48), channel_id=1, source_target_pairs={{0,16},{16,32},{32,48},{48,64},{64,80},{80,96},{96,112},{1,17},{17... | collective-permute-start | bytes 294920 | tf_op jit(solution)/shard_map/ppermute | solution.py:347
  96.6 1.9 %collective-permute-start.11 = (f32[3,32,256]{2,1,0:T(8,128)S(1)}, f32[3,32,256]{2,1,0:T(8,128)S(1)}, u32[]{:S(2)}, u32[]{:S(2)}) collective-permute-start(f32[3,32,256]{2,1,0:T(8,128)S(1)} %get-tuple-element.49), channel_id=1, source_target_pairs={{16,0},{32,16},{48,32},{64,48},{80,64},{96,80},{112,96},{17,1},{33... | collective-permute-start | bytes 294920 | tf_op jit(solution)/shard_map/ppermute | solution.py:347
  98.5 5.7 %collective-permute-start.8 = (f32[3,16,256]{2,1,0:T(8,128)S(1)}, f32[3,16,256]{2,1,0:T(8,128)S(1)}, u32[]{:S(2)}, u32[]{:S(2)}) collective-permute-start(f32[3,16,256]{2,1,0:T(8,128)S(1)} %get-tuple-element.46), channel_id=1, source_target_pairs={{0,1},{1,2},{2,3},{3,4},{4,5},{5,6},{6,7},{7,8},{8,9},{9,10},{10,1... | collective-permute-start | bytes 147464 | tf_op jit(solution)/shard_map/ppermute | solution.py:347
  104.2 1.3 collective-permute-start.9
  105.6 3.8 %collective-permute-done.9.refs_7_ = f32[3,16,256]{2,1,0:T(8,128)S(1)} collective-permute-done((f32[3,16,256]{2,1,0:T(8,128)S(1)}, f32[3,16,256]{2,1,0:T(8,128)S(1)}, u32[]{:S(2)}, u32[]{:S(2)}) %collective-permute-start.9) | collective-permute-done | bytes 49184 | tf_op jit(solution)/shard_map/ppermute | solution.py:347
  109.4 14.9 %gather_rows.1 = (f32[3,512,256]{2,1,0:T(8,128)}, f32[128,2,128]{2,1,0:T(2,128)S(1)}) custom-call(s32[2,32]{1,0:T(2,128)S(1)} %pad_add_fusion.refs_0_, f32[3,16,32,256]{3,2,1,0:T(8,128)S(1)} %bitcast.35, f32[6,16,32,256]{3,2,1,0:T(8,128)S(1)} %bitcast.31, f32[3,16,32,256]{3,2,1,0:T(8,128)S(1)} %bitcast.38, f32[16,32,256]{2,1,0:T(8,128)S(1)} %bitcast.41, ...), custom_call_target="tpu_custom_call" | custom-call | tf_op jit(solution)/shard_map/gather_rows/pallas_call | solution.py:461
  124.3 18.1 %all_to_all.11 = f32[128,2,128]{2,1,0:T(2,128)S(1)} all-to-all(f32[128,2,128]{2,1,0:T(2,128)S(1)} %get-tuple-element.53), channel_id=1, replica_groups=mesh['gx'=8,'gy'=16] {'gx','gy'}, dimensions={0} | all-to-all | bytes 262144 | tf_op jit(solution)/shard_map/all_to_all | solution.py:484
  (20 shorter events, 2.5 us)
Async XLA Ops:
  0.6 47.6 %copy-start.1 = (f32[3,16,32,256]{3,2,1,0:T(8,128)S(1)}, f32[3,16,32,256]{3,2,1,0:T(8,128)}, u32[]{:S(2)}) copy-start(f32[3,16,32,256]{3,2,1,0:T(8,128)} %param.16) | copy-start | bytes 4718596
  0.6 47.6 %copy-start.2 = (f32[16,32,256]{2,1,0:T(8,128)S(1)}, f32[16,32,256]{2,1,0:T(8,128)}, u32[]{:S(2)}) copy-start(f32[16,32,256]{2,1,0:T(8,128)} %param.15) | copy-start | bytes 1572868
  48.2 2.3 %copy-start = (f32[9,16,32,256]{3,2,1,0:T(8,128)S(1)}, f32[9,16,32,256]{3,2,1,0:T(8,128)}, u32[]{:S(2)}) copy-start(f32[9,16,32,256]{3,2,1,0:T(8,128)} %param.17) | copy-start | bytes 14155780
  60.5 12.3 %collective-permute-start.2 = (f32[3,32,256]{2,1,0:T(8,128)S(1)}, f32[3,32,256]{2,1,0:T(8,128)S(1)}, u32[]{:S(2)}, u32[]{:S(2)}) collective-permute-start(f32[3,32,256]{2,1,0:T(8,128)S(1)} %get-tuple-element.38), channel_id=1, source_target_pairs={{0,16},{16,32},{32,48},{48,64},{64,80},{80,96},{96,112},{1,17},{17... | collective-permute-start | bytes 294920 | tf_op jit(solution)/shard_map/ppermute | solution.py:347
  63.6 9.2 %collective-permute-start.3 = (f32[3,32,256]{2,1,0:T(8,128)S(1)}, f32[3,32,256]{2,1,0:T(8,128)S(1)}, u32[]{:S(2)}, u32[]{:S(2)}) collective-permute-start(f32[3,32,256]{2,1,0:T(8,128)S(1)} %get-tuple-element.39), channel_id=1, source_target_pairs={{16,0},{32,16},{48,32},{64,48},{80,64},{96,80},{112,96},{17,1},{33... | collective-permute-start | bytes 294920 | tf_op jit(solution)/shard_map/ppermute | solution.py:347
  65.6 3.0 %collective-permute-start = (f32[3,16,256]{2,1,0:T(8,128)S(1)}, f32[3,16,256]{2,1,0:T(8,128)S(1)}, u32[]{:S(2)}, u32[]{:S(2)}) collective-permute-start(f32[3,16,256]{2,1,0:T(8,128)S(1)} %get-tuple-element.36), channel_id=1, source_target_pairs={{0,1},{1,2},{2,3},{3,4},{4,5},{5,6},{6,7},{7,8},{8,9},{9,10},{10,1... | collective-permute-start | bytes 147464 | tf_op jit(solution)/shard_map/ppermute | solution.py:347
  67.3 5.6 %collective-permute-start.1 = (f32[3,16,256]{2,1,0:T(8,128)S(1)}, f32[3,16,256]{2,1,0:T(8,128)S(1)}, u32[]{:S(2)}, u32[]{:S(2)}) collective-permute-start(f32[3,16,256]{2,1,0:T(8,128)S(1)} %get-tuple-element.37), channel_id=1, source_target_pairs={{1,0},{2,1},{3,2},{4,3},{5,4},{6,5},{7,6},{8,7},{9,8},{10,9},{11,1... | collective-permute-start | bytes 147464 | tf_op jit(solution)/shard_map/ppermute | solution.py:347
  74.2 16.2 %collective-permute-start.6 = (f32[3,32,256]{2,1,0:T(8,128)S(1)}, f32[3,32,256]{2,1,0:T(8,128)S(1)}, u32[]{:S(2)}, u32[]{:S(2)}) collective-permute-start(f32[3,32,256]{2,1,0:T(8,128)S(1)} %get-tuple-element.43), channel_id=1, source_target_pairs={{0,16},{16,32},{32,48},{48,64},{64,80},{80,96},{96,112},{1,17},{17... | collective-permute-start | bytes 294920 | tf_op jit(solution)/shard_map/ppermute | solution.py:347
  78.5 11.9 %collective-permute-start.7 = (f32[3,32,256]{2,1,0:T(8,128)S(1)}, f32[3,32,256]{2,1,0:T(8,128)S(1)}, u32[]{:S(2)}, u32[]{:S(2)}) collective-permute-start(f32[3,32,256]{2,1,0:T(8,128)S(1)} %get-tuple-element.44), channel_id=1, source_target_pairs={{16,0},{32,16},{48,32},{64,48},{80,64},{96,80},{112,96},{17,1},{33... | collective-permute-start | bytes 294920 | tf_op jit(solution)/shard_map/ppermute | solution.py:347
  80.5 3.9 %collective-permute-start.4 = (f32[3,16,256]{2,1,0:T(8,128)S(1)}, f32[3,16,256]{2,1,0:T(8,128)S(1)}, u32[]{:S(2)}, u32[]{:S(2)}) collective-permute-start(f32[3,16,256]{2,1,0:T(8,128)S(1)} %get-tuple-element.41), channel_id=1, source_target_pairs={{0,1},{1,2},{2,3},{3,4},{4,5},{5,6},{6,7},{7,8},{8,9},{9,10},{10,1... | collective-permute-start | bytes 147464 | tf_op jit(solution)/shard_map/ppermute | solution.py:347
  83.1 7.4 %collective-permute-start.5 = (f32[3,16,256]{2,1,0:T(8,128)S(1)}, f32[3,16,256]{2,1,0:T(8,128)S(1)}, u32[]{:S(2)}, u32[]{:S(2)}) collective-permute-start(f32[3,16,256]{2,1,0:T(8,128)S(1)} %get-tuple-element.42), channel_id=1, source_target_pairs={{1,0},{2,1},{3,2},{4,3},{5,4},{6,5},{7,6},{8,7},{9,8},{10,9},{11,1... | collective-permute-start | bytes 147464 | tf_op jit(solution)/shard_map/ppermute | solution.py:347
  91.8 17.6 %collective-permute-start.10 = (f32[3,32,256]{2,1,0:T(8,128)S(1)}, f32[3,32,256]{2,1,0:T(8,128)S(1)}, u32[]{:S(2)}, u32[]{:S(2)}) collective-permute-start(f32[3,32,256]{2,1,0:T(8,128)S(1)} %get-tuple-element.48), channel_id=1, source_target_pairs={{0,16},{16,32},{32,48},{48,64},{64,80},{80,96},{96,112},{1,17},{17... | collective-permute-start | bytes 294920 | tf_op jit(solution)/shard_map/ppermute | solution.py:347
  96.6 12.8 %collective-permute-start.11 = (f32[3,32,256]{2,1,0:T(8,128)S(1)}, f32[3,32,256]{2,1,0:T(8,128)S(1)}, u32[]{:S(2)}, u32[]{:S(2)}) collective-permute-start(f32[3,32,256]{2,1,0:T(8,128)S(1)} %get-tuple-element.49), channel_id=1, source_target_pairs={{16,0},{32,16},{48,32},{64,48},{80,64},{96,80},{112,96},{17,1},{33... | collective-permute-start | bytes 294920 | tf_op jit(solution)/shard_map/ppermute | solution.py:347
  98.5 7.1 %collective-permute-start.8 = (f32[3,16,256]{2,1,0:T(8,128)S(1)}, f32[3,16,256]{2,1,0:T(8,128)S(1)}, u32[]{:S(2)}, u32[]{:S(2)}) collective-permute-start(f32[3,16,256]{2,1,0:T(8,128)S(1)} %get-tuple-element.46), channel_id=1, source_target_pairs={{0,1},{1,2},{2,3},{3,4},{4,5},{5,6},{6,7},{7,8},{8,9},{9,10},{10,1... | collective-permute-start | bytes 147464 | tf_op jit(solution)/shard_map/ppermute | solution.py:347
  104.2 5.1 %collective-permute-start.9 = (f32[3,16,256]{2,1,0:T(8,128)S(1)}, f32[3,16,256]{2,1,0:T(8,128)S(1)}, u32[]{:S(2)}, u32[]{:S(2)}) collective-permute-start(f32[3,16,256]{2,1,0:T(8,128)S(1)} %get-tuple-element.47), channel_id=1, source_target_pairs={{1,0},{2,1},{3,2},{4,3},{5,4},{6,5},{7,6},{8,7},{9,8},{10,9},{11,1... | collective-permute-start | bytes 147464 | tf_op jit(solution)/shard_map/ppermute | solution.py:347

commit v5 on v4

--- a/solution.py
+++ b/solution.py
@@ -15,6 +15,7 @@
 SIDE = 8
 PARTS = 4
 CELL_SHIFT = 257
+KEY_BITS = 13
 MIB = 1024 * 1024
 
 
@@ -75,8 +76,8 @@
     lax.fori_loop(0, sens.shape[1] // part // 4, rank, jnp.zeros((devices, 1), jnp.float32))
 
     def chunk(i, _):
-        for b in range(2):
-            at = pl.ds(pl.multiple_of((i * 2 + b) * step, step), step)
+        for b in range(4):
+            at = pl.ds(pl.multiple_of((i * 4 + b) * step, step), step)
             rank = ranks[:, at]
             lane = device[:, at] + jnp.where(rank >= half, devices, 0)
             ones = marked(places(2 * devices, step) == lane, 1.0)
@@ -99,10 +100,10 @@
                 band = slice(p * half, (p + 1) * half)
                 right[b, band, :step] = marked(here, high)
                 right[b, band, step:] = marked(here, low)
-        total[...] += dot_last(right[0], left[0]) + dot_last(right[1], left[1])
+        total[...] += sum(dot_last(right[b], left[b]) for b in range(4))
         return 0
 
-    lax.fori_loop(0, steps // 2, chunk, 0)
+    lax.fori_loop(0, steps // 4, chunk, 0)
     for p in range(6):
         band = total[p * half : (p + 1) * half, :]
         rows[:, p, :] = jnp.concatenate([band[:, :devices].T, band[:, devices:].T], axis=1)
@@ -121,8 +122,8 @@
         + [
             pltpu.VMEM((1, count), jnp.int32),
             pltpu.VMEM((RANK_ROWS, RANK_ROWS), jnp.bfloat16),
-            pltpu.VMEM((2, 2 * devices, 2 * STEP_ROWS), jnp.bfloat16),
-            pltpu.VMEM((2, 3 * capacity, 2 * STEP_ROWS), jnp.bfloat16),
+            pltpu.VMEM((4, 2 * devices, 2 * STEP_ROWS), jnp.bfloat16),
+            pltpu.VMEM((4, 3 * capacity, 2 * STEP_ROWS), jnp.bfloat16),
             pltpu.VMEM((3 * capacity, 2 * devices), jnp.float32),
             pltpu.SemaphoreType.DMA((len(given),)),
         ],
@@ -168,7 +169,7 @@
     def fill(i, b):
         for q in range(group):
             row = pl.ds(i * group + q, 1)
-            there = places(part, width) == (cells[row, :] & (part - 1))
+            there = places(part, width) == ((cells[row, :] >> KEY_BITS) & (part - 1))
             for k, sens in enumerate((one, two, three)):
                 high, low = halves(sens[row, :])
                 band = slice(k * part, (k + 1) * part)
@@ -179,7 +180,7 @@
         least = start + w * WINDOW
         base = pl.multiple_of(jnp.minimum(least, height - WINDOW), 8)
         for q in range(group):
-            cell = cells[pl.ds(i * group + q, 1), :]
+            cell = cells[pl.ds(i * group + q, 1), :] >> KEY_BITS
             place = window_place(cell, least, base, PARTS)
             hot = marked(places(PARTS * WINDOW, width) == place, 1.0)
             left[b, :, q * width : (q + 1) * width] = hot
@@ -267,7 +268,7 @@
             pltpu.VMEM((SIDE, 3 * depth // PARTS, 2 * STEP_ROWS), jnp.bfloat16),
             pltpu.SemaphoreType.DMA((3,)),
         ],
-        compiler_params=pltpu.CompilerParams(vmem_limit_bytes=24 * MIB),
+        compiler_params=pltpu.CompilerParams(vmem_limit_bytes=41 * MIB),
         name="scatter_rows",
     )(
         ends,
@@ -355,7 +356,7 @@
 
 def gather_kernel(*refs):
     ends, first, scaled, inverse, stiff, before, south, north, west, east = refs[:10]
-    cells, weights, boxes, final, sums, padded, field, hot, left, right, total, sent = refs[10:]
+    cells, weights, final, sums, padded, field, hot, left, right, total, sent = refs[10:]
     size_y = before.shape[2]
 
     def store(k, x, fresh):
@@ -378,7 +379,7 @@
     def window(i, b, start, w):
         least = start + w * WINDOW
         base = pl.multiple_of(jnp.minimum(least, height - WINDOW), 8)
-        own = [cells[row, :] for row in rows(i)]
+        own = [cells[row, :] >> KEY_BITS for row in rows(i)]
         for q in range(group):
             ones = marked(places(2 * WINDOW, width) == window_place(own[q], least, base, 2), 1.0)
             hot[b, : 2 * WINDOW, q * width : (q + 1) * width] = ones
@@ -419,7 +420,7 @@
             at = slice(q * width, (q + 1) * width)
             low_at = slice(step + q * width, step + (q + 1) * width)
             weight = weights[row, :]
-            box = boxes[row, :].astype(jnp.int32)
+            box = cells[row, :] & (2**KEY_BITS - 1)
             owned = marked(places(left.shape[1], width) == (box >> BOX_BITS), 1.0)
             left[b, :, at] = owned
             left[b, :, low_at] = owned
@@ -454,13 +455,13 @@
     out.wait()
 
 
-def gather(ends, swept_from, cells, weights, boxes, devices):
+def gather(ends, swept_from, cells, weights, devices):
     _, size_x, size_y, depth = swept_from[0].shape
     cube = (3, size_x * size_y, depth)
     vmem = pl.BlockSpec(memory_space=pltpu.VMEM)
     return pl.pallas_call(
         gather_kernel,
-        in_specs=[pl.BlockSpec(memory_space=pltpu.SMEM)] + [vmem] * (len(swept_from) + 3),
+        in_specs=[pl.BlockSpec(memory_space=pltpu.SMEM)] + [vmem] * (len(swept_from) + 2),
         out_specs=[pl.BlockSpec(memory_space=pltpu.HBM), vmem],
         out_shape=[
             jax.ShapeDtypeStruct(cube, jnp.float32),
@@ -477,7 +478,7 @@
         ],
         compiler_params=pltpu.CompilerParams(vmem_limit_bytes=32 * MIB),
         name="gather_rows",
-    )(ends, *swept_from, cells, weights, boxes)
+    )(ends, *swept_from, cells, weights)
 
 
 def swapped(blocks):
@@ -510,17 +511,18 @@
     )
     rows = swapped(rows)
     planes = [rows[:, p].reshape(-1) for p in range(6)]
-    keys = jnp.maximum(planes[3].astype(jnp.int32) - CELL_SHIFT, -1)
-    ordered = lax.sort((keys, *planes[:3], *planes[4:]), num_keys=1, is_stable=False)
-    cells, *values, weights, boxes = [part.reshape(-1, 128) for part in ordered]
+    found = (planes[3].astype(jnp.int32) - CELL_SHIFT) << KEY_BITS
+    keys = jnp.maximum(found + planes[5].astype(jnp.int32), -1)
+    ordered = lax.sort((keys, *planes[:3], planes[4]), num_keys=1, is_stable=False)
+    cells, *values, weights = [part.reshape(-1, 128) for part in ordered]
     blocks = cells.reshape(-1, STEP_ROWS // 128, 128)
-    ends = jnp.stack([blocks[:, 0, 0], blocks[:, -1, -1]])
+    ends = jnp.stack([blocks[:, 0, 0], blocks[:, -1, -1]]) >> KEY_BITS
     fixed, faces = scatter(ends, cells, values, stiffness, anchor, coupling)
     field = fixed[0]
     for turn in range(1, SWEEPS - 1):
         field, *faces = sweep(*fixed, field, *exchange(*faces))
     swept_from = (*fixed, field, *exchange(*faces))
-    field, partial = gather(ends, swept_from, cells, weights, boxes, devices)
+    field, partial = gather(ends, swept_from, cells, weights, devices)
     field = field.reshape(3, size_x, size_y, size_z)
     summed = jnp.sum(swapped(partial), axis=0).reshape(4, BOX_DEV)
     return (field, summed[:3])

time: 144 us -> 139 us (0.965)
  waiting for transfers between devices: 14.2 us -> 11.2 us
  local copies, waits for them, and re-layouts: 4.5 us -> 2.12 us
  blocking collectives: 43 us -> 44.7 us
    ppermute x12, waiting for transfers between devices: 14.2 us -> 11.2 us  [shifted(): return lax.ppermute(face, axis, pairs)]
    unnamed x6 -> x4, local copies, waits for them, and re-layouts: 2.34 us -> 0.01 us
    all_to_all x2, blocking collectives: 43 us -> 44.7 us  [swapped(): return lax.all_to_all(blocks, AXES, split_axis=0, concat_axis=0, tiled=True)]
    sort x1, other arithmetic: 11.5 us -> 10 us  [body(): lax.sort((keys, *planes[:3], planes[4]), num_keys=1, is_stable=False)]
where the time goes in v5:
time: 139 us; the launch traced here: 138 us
  blocking collectives  44.7 us (32%)
  Pallas kernels  36.3 us (26%)
  starting transfers between devices  32.8 us (24%)
  waiting for transfers between devices  11.2 us (8%)
  other arithmetic  10.4 us (7%)
  local copies, waits for them, and re-layouts  2.12 us (2%)
    all_to_all x2, blocking collectives, swapped(): return lax.all_to_all(blocks, AXES, split_axis=0, concat_axis=0, tiled=True)  44.7 us
    ppermute x12, starting transfers between devices, shifted(): return lax.ppermute(face, axis, pairs)  32.8 us
    pallas_call x1, Pallas kernels, gather(): pl.pallas_call(gather_kernel, in_specs=[pl.BlockSpec(memory_space=pltpu.S...  15 us
    ppermute x12, waiting for transfers between devices, shifted(): return lax.ppermute(face, axis, pairs)  11.2 us
    sort x1, other arithmetic, body(): lax.sort((keys, *planes[:3], planes[4]), num_keys=1, is_stable=False)  10 us
    pallas_call x1, Pallas kernels, scatter(): pl.pallas_call(scatter_kernel, in_specs=[pl.BlockSpec(memory_space=pltpu....  9.79 us
    pallas_call x1, Pallas kernels, pack(): pl.pallas_call(pack_kernel, in_specs=[pl.BlockSpec(memory_space=pltpu.HBM...  8.73 us
  transfers between devices with their start and end apart: 12, of which 3 were waited for; matrix products, arithmetic and copies ran while one was open for 0% of the time, Pallas kernels for 0%

profile of v5, /device:TPU:1, one launch (start us, length us, event | category | flops | bytes accessed | tf_op | source)
XLA Modules:
  0.0 138.4 jit_solution(2978350585396614896)
XLA Ops:
  0.7 8.7 %pack_rows.1 = f32[128,8,128]{2,1,0:T(8,128)} custom-call(f32[3,8192]{1,0:T(4,128)} %refs_0_.1, f32[1,8192]{1,0:T(1,128)} %bitcast.55, s32[1,8192]{1,0:T(1,128)} %bitcast.56, s32[1,8192]{1,0:T(1,128)} %bitcast.57, s32[1,8192]{1,0:T(1,128)} %bitcast.58, s32[1,8192]{1,0:T(1,128)} %bitcast.59), custom_call_target="tpu_custom_call" | custom-call | tf_op jit(solution)/shard_map/pack_rows/pallas_call | solution.py:117
  9.4 24.8 %all_to_all.10 = f32[128,8,128]{2,1,0:T(8,128)S(1)} all-to-all(f32[128,8,128]{2,1,0:T(8,128)} %pack_rows.1), channel_id=1, replica_groups=mesh['gx'=8,'gy'=16] {'gx','gy'}, dimensions={0} | all-to-all | bytes 1048576 | tf_op jit(solution)/shard_map/all_to_all | solution.py:485
  34.7 10.0 %sort.33 = (s32[16384]{0:T(1024)S(1)}, f32[16384]{0:T(1024)S(1)}, f32[16384]{0:T(1024)S(1)}, f32[16384]{0:T(1024)S(1)}, f32[16384]{0:T(1024)S(1)}) sort(s32[16384]{0:T(1024)S(1)} %bitcast.50, f32[16384]{0:T(1024)S(1)} %bitcast.54, f32[16384]{0:T(1024)S(1)} %bitcast.53, f32[16384]{0:T(1024)S(1)} %bitcast.52, f32[16384]{0:T(1024)S(1)} %bitcast.51), dimensions={0}, to_apply=%region_0.0 | sort | flops 229376 | bytes 655360 | tf_op jit(solution)/shard_map/sort | solution.py:516
  44.7 1.3 slice_reduce_fusion.1
  46.0 9.8 %scatter_rows.1 = (f32[3,512,256]{2,1,0:T(8,128)S(1)}, f32[6,512,256]{2,1,0:T(8,128)S(1)}, f32[3,512,256]{2,1,0:T(8,128)S(1)}, f32[512,256]{1,0:T(8,128)S(1)}, f...) custom-call(s32[2,32]{1,0:T(2,128)S(1)} %add_shift-right-arithmetic_, ...), custom_call_target="tpu_custom_call" | custom-call | tf_op jit(solution)/shard_map/scatter_rows/pallas_call | solution.py:257
  55.8 3.0 %collective-permute-start.2 = (f32[3,32,256]{2,1,0:T(8,128)S(1)}, f32[3,32,256]{2,1,0:T(8,128)S(1)}, u32[]{:S(2)}, u32[]{:S(2)}) collective-permute-start(f32[3,32,256]{2,1,0:T(8,128)S(1)} %get-tuple-element.37), channel_id=1, source_target_pairs={{0,16},{16,32},{32,48},{48,64},{64,80},{80,96},{96,112},{1,17},{17... | collective-permute-start | bytes 294920 | tf_op jit(solution)/shard_map/ppermute | solution.py:348
  58.8 1.9 %collective-permute-start.3 = (f32[3,32,256]{2,1,0:T(8,128)S(1)}, f32[3,32,256]{2,1,0:T(8,128)S(1)}, u32[]{:S(2)}, u32[]{:S(2)}) collective-permute-start(f32[3,32,256]{2,1,0:T(8,128)S(1)} %get-tuple-element.38), channel_id=1, source_target_pairs={{16,0},{32,16},{48,32},{64,48},{80,64},{96,80},{112,96},{17,1},{33... | collective-permute-start | bytes 294920 | tf_op jit(solution)/shard_map/ppermute | solution.py:348
  60.8 2.9 %collective-permute-start = (f32[3,16,256]{2,1,0:T(8,128)S(1)}, f32[3,16,256]{2,1,0:T(8,128)S(1)}, u32[]{:S(2)}, u32[]{:S(2)}) collective-permute-start(f32[3,16,256]{2,1,0:T(8,128)S(1)} %get-tuple-element.35), channel_id=1, source_target_pairs={{0,1},{1,2},{2,3},{3,4},{4,5},{5,6},{6,7},{7,8},{8,9},{9,10},{10,1... | collective-permute-start | bytes 147464 | tf_op jit(solution)/shard_map/ppermute | solution.py:348
  63.7 1.3 collective-permute-start.1
  65.0 3.5 %collective-permute-done.1.north = f32[3,16,256]{2,1,0:T(8,128)S(1)} collective-permute-done((f32[3,16,256]{2,1,0:T(8,128)S(1)}, f32[3,16,256]{2,1,0:T(8,128)S(1)}, u32[]{:S(2)}, u32[]{:S(2)}) %collective-permute-start.1) | collective-permute-done | bytes 49184 | tf_op jit(solution)/shard_map/ppermute | solution.py:348
  68.6 1.3 sweep_cells.2
  69.9 5.1 %collective-permute-start.6 = (f32[3,32,256]{2,1,0:T(8,128)S(1)}, f32[3,32,256]{2,1,0:T(8,128)S(1)}, u32[]{:S(2)}, u32[]{:S(2)}) collective-permute-start(f32[3,32,256]{2,1,0:T(8,128)S(1)} %get-tuple-element.42), channel_id=1, source_target_pairs={{0,16},{16,32},{32,48},{48,64},{64,80},{80,96},{96,112},{1,17},{17... | collective-permute-start | bytes 294920 | tf_op jit(solution)/shard_map/ppermute | solution.py:348
  75.0 1.9 %collective-permute-start.7 = (f32[3,32,256]{2,1,0:T(8,128)S(1)}, f32[3,32,256]{2,1,0:T(8,128)S(1)}, u32[]{:S(2)}, u32[]{:S(2)}) collective-permute-start(f32[3,32,256]{2,1,0:T(8,128)S(1)} %get-tuple-element.43), channel_id=1, source_target_pairs={{16,0},{32,16},{48,32},{64,48},{80,64},{96,80},{112,96},{17,1},{33... | collective-permute-start | bytes 294920 | tf_op jit(solution)/shard_map/ppermute | solution.py:348
  76.9 1.8 %collective-permute-start.4 = (f32[3,16,256]{2,1,0:T(8,128)S(1)}, f32[3,16,256]{2,1,0:T(8,128)S(1)}, u32[]{:S(2)}, u32[]{:S(2)}) collective-permute-start(f32[3,16,256]{2,1,0:T(8,128)S(1)} %get-tuple-element.40), channel_id=1, source_target_pairs={{0,1},{1,2},{2,3},{3,4},{4,5},{5,6},{6,7},{7,8},{8,9},{9,10},{10,1... | collective-permute-start | bytes 147464 | tf_op jit(solution)/shard_map/ppermute | solution.py:348
  78.7 1.3 collective-permute-start.5
  80.0 3.8 %collective-permute-done.5.north = f32[3,16,256]{2,1,0:T(8,128)S(1)} collective-permute-done((f32[3,16,256]{2,1,0:T(8,128)S(1)}, f32[3,16,256]{2,1,0:T(8,128)S(1)}, u32[]{:S(2)}, u32[]{:S(2)}) %collective-permute-start.5) | collective-permute-done | bytes 49184 | tf_op jit(solution)/shard_map/ppermute | solution.py:348
  83.8 1.4 %sweep_cells.3 = (f32[3,16,32,256]{3,2,1,0:T(8,128)S(1)}, f32[3,32,256]{2,1,0:T(8,128)S(1)}, f32[3,32,256]{2,1,0:T(8,128)S(1)}, f32[3,16,256]{2,1,0:T(8,128)S(1)}, f32[3,16,256]{2,1,0:T(8,128)S(1)}) custom-call(f32[3,16,32,256]{3,2,1,0:T(8,128)S(1)} %bitcast.32, f32[6,16,32,256]{3,2,1,0:T(8,128)S(1)} %bitcast.28, f32[3,16,32,256]{3,2,1,0:T(8,128)S(1)} %bitcast.35, ...), custom_call_target="tpu_custom_call" | custom-call | tf_op jit(solution)/shard_map/sweep_cells/pallas_call | solution.py:336
  85.2 4.8 %collective-permute-start.10 = (f32[3,32,256]{2,1,0:T(8,128)S(1)}, f32[3,32,256]{2,1,0:T(8,128)S(1)}, u32[]{:S(2)}, u32[]{:S(2)}) collective-permute-start(f32[3,32,256]{2,1,0:T(8,128)S(1)} %get-tuple-element.47), channel_id=1, source_target_pairs={{0,16},{16,32},{32,48},{48,64},{64,80},{80,96},{96,112},{1,17},{17... | collective-permute-start | bytes 294920 | tf_op jit(solution)/shard_map/ppermute | solution.py:348
  90.0 1.9 %collective-permute-start.11 = (f32[3,32,256]{2,1,0:T(8,128)S(1)}, f32[3,32,256]{2,1,0:T(8,128)S(1)}, u32[]{:S(2)}, u32[]{:S(2)}) collective-permute-start(f32[3,32,256]{2,1,0:T(8,128)S(1)} %get-tuple-element.48), channel_id=1, source_target_pairs={{16,0},{32,16},{48,32},{64,48},{80,64},{96,80},{112,96},{17,1},{33... | collective-permute-start | bytes 294920 | tf_op jit(solution)/shard_map/ppermute | solution.py:348
  92.0 5.6 %collective-permute-start.8 = (f32[3,16,256]{2,1,0:T(8,128)S(1)}, f32[3,16,256]{2,1,0:T(8,128)S(1)}, u32[]{:S(2)}, u32[]{:S(2)}) collective-permute-start(f32[3,16,256]{2,1,0:T(8,128)S(1)} %get-tuple-element.45), channel_id=1, source_target_pairs={{0,1},{1,2},{2,3},{3,4},{4,5},{5,6},{6,7},{7,8},{8,9},{9,10},{10,1... | collective-permute-start | bytes 147464 | tf_op jit(solution)/shard_map/ppermute | solution.py:348
  97.5 1.3 collective-permute-start.9
  98.9 3.8 %collective-permute-done.9.refs_7_ = f32[3,16,256]{2,1,0:T(8,128)S(1)} collective-permute-done((f32[3,16,256]{2,1,0:T(8,128)S(1)}, f32[3,16,256]{2,1,0:T(8,128)S(1)}, u32[]{:S(2)}, u32[]{:S(2)}) %collective-permute-start.9) | collective-permute-done | bytes 49184 | tf_op jit(solution)/shard_map/ppermute | solution.py:348
  102.7 15.0 %gather_rows.1 = (f32[3,512,256]{2,1,0:T(8,128)}, f32[128,2,128]{2,1,0:T(2,128)S(1)}) custom-call(s32[2,32]{1,0:T(2,128)S(1)} %add_shift-right-arithmetic_fusion.refs_0_, f32[3,16,32,256]{3,2,1,0:T(8,128)S(1)} %bitcast.33, f32[6,16,32,256]{3,2,1,0:T(8,128)S(1)} %bitcast.29, f32[3,16,32,256]{3,2,1,0:T(8,128)S(1)} %bitcast.36, f32[16,32,256]{2,1,0:T(8,128)S(1)} %bitcast.39, ...), custom_call_target="tpu_custom_call" | custom-call | tf_op jit(solution)/shard_map/gather_rows/pallas_call | solution.py:462
  117.7 19.9 %all_to_all.11 = f32[128,2,128]{2,1,0:T(2,128)S(1)} all-to-all(f32[128,2,128]{2,1,0:T(2,128)S(1)} %get-tuple-element.51), channel_id=1, replica_groups=mesh['gx'=8,'gy'=16] {'gx','gy'}, dimensions={0} | all-to-all | bytes 262144 | tf_op jit(solution)/shard_map/all_to_all | solution.py:485
  (18 shorter events, 1.3 us)
Async XLA Ops:
  0.6 45.4 %copy-start = (f32[3,16,32,256]{3,2,1,0:T(8,128)S(1)}, f32[3,16,32,256]{3,2,1,0:T(8,128)}, u32[]{:S(2)}) copy-start(f32[3,16,32,256]{3,2,1,0:T(8,128)} %param.16) | copy-start | bytes 4718596
  0.6 45.4 %copy-start.1 = (f32[16,32,256]{2,1,0:T(8,128)S(1)}, f32[16,32,256]{2,1,0:T(8,128)}, u32[]{:S(2)}) copy-start(f32[16,32,256]{2,1,0:T(8,128)} %param.15) | copy-start | bytes 1572868
  55.8 12.8 %collective-permute-start.2 = (f32[3,32,256]{2,1,0:T(8,128)S(1)}, f32[3,32,256]{2,1,0:T(8,128)S(1)}, u32[]{:S(2)}, u32[]{:S(2)}) collective-permute-start(f32[3,32,256]{2,1,0:T(8,128)S(1)} %get-tuple-element.37), channel_id=1, source_target_pairs={{0,16},{16,32},{32,48},{48,64},{64,80},{80,96},{96,112},{1,17},{17... | collective-permute-start | bytes 294920 | tf_op jit(solution)/shard_map/ppermute | solution.py:348
  58.8 9.7 %collective-permute-start.3 = (f32[3,32,256]{2,1,0:T(8,128)S(1)}, f32[3,32,256]{2,1,0:T(8,128)S(1)}, u32[]{:S(2)}, u32[]{:S(2)}) collective-permute-start(f32[3,32,256]{2,1,0:T(8,128)S(1)} %get-tuple-element.38), channel_id=1, source_target_pairs={{16,0},{32,16},{48,32},{64,48},{80,64},{96,80},{112,96},{17,1},{33... | collective-permute-start | bytes 294920 | tf_op jit(solution)/shard_map/ppermute | solution.py:348
  60.8 4.3 %collective-permute-start = (f32[3,16,256]{2,1,0:T(8,128)S(1)}, f32[3,16,256]{2,1,0:T(8,128)S(1)}, u32[]{:S(2)}, u32[]{:S(2)}) collective-permute-start(f32[3,16,256]{2,1,0:T(8,128)S(1)} %get-tuple-element.35), channel_id=1, source_target_pairs={{0,1},{1,2},{2,3},{3,4},{4,5},{5,6},{6,7},{7,8},{8,9},{9,10},{10,1... | collective-permute-start | bytes 147464 | tf_op jit(solution)/shard_map/ppermute | solution.py:348
  63.7 4.8 %collective-permute-start.1 = (f32[3,16,256]{2,1,0:T(8,128)S(1)}, f32[3,16,256]{2,1,0:T(8,128)S(1)}, u32[]{:S(2)}, u32[]{:S(2)}) collective-permute-start(f32[3,16,256]{2,1,0:T(8,128)S(1)} %get-tuple-element.36), channel_id=1, source_target_pairs={{1,0},{2,1},{3,2},{4,3},{5,4},{6,5},{7,6},{8,7},{9,8},{10,9},{11,1... | collective-permute-start | bytes 147464 | tf_op jit(solution)/shard_map/ppermute | solution.py:348
  69.9 13.9 %collective-permute-start.6 = (f32[3,32,256]{2,1,0:T(8,128)S(1)}, f32[3,32,256]{2,1,0:T(8,128)S(1)}, u32[]{:S(2)}, u32[]{:S(2)}) collective-permute-start(f32[3,32,256]{2,1,0:T(8,128)S(1)} %get-tuple-element.42), channel_id=1, source_target_pairs={{0,16},{16,32},{32,48},{48,64},{64,80},{80,96},{96,112},{1,17},{17... | collective-permute-start | bytes 294920 | tf_op jit(solution)/shard_map/ppermute | solution.py:348
  75.0 8.8 %collective-permute-start.7 = (f32[3,32,256]{2,1,0:T(8,128)S(1)}, f32[3,32,256]{2,1,0:T(8,128)S(1)}, u32[]{:S(2)}, u32[]{:S(2)}) collective-permute-start(f32[3,32,256]{2,1,0:T(8,128)S(1)} %get-tuple-element.43), channel_id=1, source_target_pairs={{16,0},{32,16},{48,32},{64,48},{80,64},{96,80},{112,96},{17,1},{33... | collective-permute-start | bytes 294920 | tf_op jit(solution)/shard_map/ppermute | solution.py:348
  76.9 3.1 %collective-permute-start.4 = (f32[3,16,256]{2,1,0:T(8,128)S(1)}, f32[3,16,256]{2,1,0:T(8,128)S(1)}, u32[]{:S(2)}, u32[]{:S(2)}) collective-permute-start(f32[3,16,256]{2,1,0:T(8,128)S(1)} %get-tuple-element.40), channel_id=1, source_target_pairs={{0,1},{1,2},{2,3},{3,4},{4,5},{5,6},{6,7},{7,8},{8,9},{9,10},{10,1... | collective-permute-start | bytes 147464 | tf_op jit(solution)/shard_map/ppermute | solution.py:348
  78.7 5.1 %collective-permute-start.5 = (f32[3,16,256]{2,1,0:T(8,128)S(1)}, f32[3,16,256]{2,1,0:T(8,128)S(1)}, u32[]{:S(2)}, u32[]{:S(2)}) collective-permute-start(f32[3,16,256]{2,1,0:T(8,128)S(1)} %get-tuple-element.41), channel_id=1, source_target_pairs={{1,0},{2,1},{3,2},{4,3},{5,4},{6,5},{7,6},{8,7},{9,8},{10,9},{11,1... | collective-permute-start | bytes 147464 | tf_op jit(solution)/shard_map/ppermute | solution.py:348
  85.2 17.4 %collective-permute-start.10 = (f32[3,32,256]{2,1,0:T(8,128)S(1)}, f32[3,32,256]{2,1,0:T(8,128)S(1)}, u32[]{:S(2)}, u32[]{:S(2)}) collective-permute-start(f32[3,32,256]{2,1,0:T(8,128)S(1)} %get-tuple-element.47), channel_id=1, source_target_pairs={{0,16},{16,32},{32,48},{48,64},{64,80},{80,96},{96,112},{1,17},{17... | collective-permute-start | bytes 294920 | tf_op jit(solution)/shard_map/ppermute | solution.py:348
  90.0 12.6 %collective-permute-start.11 = (f32[3,32,256]{2,1,0:T(8,128)S(1)}, f32[3,32,256]{2,1,0:T(8,128)S(1)}, u32[]{:S(2)}, u32[]{:S(2)}) collective-permute-start(f32[3,32,256]{2,1,0:T(8,128)S(1)} %get-tuple-element.48), channel_id=1, source_target_pairs={{16,0},{32,16},{48,32},{64,48},{80,64},{96,80},{112,96},{17,1},{33... | collective-permute-start | bytes 294920 | tf_op jit(solution)/shard_map/ppermute | solution.py:348
  92.0 6.9 %collective-permute-start.8 = (f32[3,16,256]{2,1,0:T(8,128)S(1)}, f32[3,16,256]{2,1,0:T(8,128)S(1)}, u32[]{:S(2)}, u32[]{:S(2)}) collective-permute-start(f32[3,16,256]{2,1,0:T(8,128)S(1)} %get-tuple-element.45), channel_id=1, source_target_pairs={{0,1},{1,2},{2,3},{3,4},{4,5},{5,6},{6,7},{7,8},{8,9},{9,10},{10,1... | collective-permute-start | bytes 147464 | tf_op jit(solution)/shard_map/ppermute | solution.py:348
  97.5 5.1 %collective-permute-start.9 = (f32[3,16,256]{2,1,0:T(8,128)S(1)}, f32[3,16,256]{2,1,0:T(8,128)S(1)}, u32[]{:S(2)}, u32[]{:S(2)}) collective-permute-start(f32[3,16,256]{2,1,0:T(8,128)S(1)} %get-tuple-element.46), channel_id=1, source_target_pairs={{1,0},{2,1},{3,2},{4,3},{5,4},{6,5},{7,6},{8,7},{9,8},{10,9},{11,1... | collective-permute-start | bytes 147464 | tf_op jit(solution)/shard_map/ppermute | solution.py:348

commit v6 on v5

--- a/solution.py
+++ b/solution.py
@@ -376,30 +376,34 @@
     def rows(i):
         return [pl.ds(i * group + q, 1) for q in range(group)]
 
+    def fill(i, b):
+        for q, row in enumerate(rows(i)):
+            place = (cells[row, :] >> KEY_BITS) & (half - 1)
+            ones = marked(places(half, width) == place, 1.0)
+            hot[b, :half, q * width : (q + 1) * width] = ones
+            hot[b, half:, q * width : (q + 1) * width] = ones
+
     def window(i, b, start, w):
         least = start + w * WINDOW
         base = pl.multiple_of(jnp.minimum(least, height - WINDOW), 8)
-        own = [cells[row, :] >> KEY_BITS for row in rows(i)]
-        for q in range(group):
-            ones = marked(places(2 * WINDOW, width) == window_place(own[q], least, base, 2), 1.0)
-            hot[b, : 2 * WINDOW, q * width : (q + 1) * width] = ones
-            hot[b, 2 * WINDOW :, q * width : (q + 1) * width] = ones
-        there = [places(half, width) == (cell & (half - 1)) for cell in own]
-        picked = []
+        there = [
+            places(2 * WINDOW, width)
+            == window_place(cells[row, :] >> KEY_BITS, least, base, 2)
+            for row in rows(i)
+        ]
         block = jnp.concatenate(
             [
-                jnp.concatenate(
-                    [field[k, pl.ds(base, WINDOW), side * half : (side + 1) * half] for k in range(3)],
-                    axis=1,
-                )
+                field[k, pl.ds(base, WINDOW), side * half : (side + 1) * half]
+                for k in range(3)
                 for side in range(2)
             ],
             axis=0,
         )
-        both = jnp.concatenate(halves(block), axis=0).T.astype(jnp.bfloat16)
+        both = jnp.concatenate(halves(block), axis=1).astype(jnp.bfloat16)
         parts = jnp.dot(both, hot[b], preferred_element_type=jnp.float32)
+        picked = []
         for k in range(3):
-            part = parts[k * half : (k + 1) * half]
+            part = parts[k * 2 * WINDOW : (k + 1) * 2 * WINDOW]
             picked.append(
                 jnp.concatenate(
                     [
@@ -434,6 +438,8 @@
     def chunks(i, _):
         own = [i * SIDE + b for b in range(SIDE)]
         spans = [windows(ends, j) for j in own]
+        for b in range(SIDE):
+            fill(own[b], b)
         firsts = [window(own[b], b, spans[b][0], 0) for b in range(SIDE)]
         finals = []
         for b in range(SIDE):
@@ -470,7 +476,7 @@
         scratch_shapes=[
             pltpu.VMEM((3, size_x + 2, size_y, depth), jnp.float32),
             pltpu.VMEM(cube, jnp.float32),
-            pltpu.VMEM((SIDE, 4 * WINDOW, STEP_ROWS), jnp.bfloat16),
+            pltpu.VMEM((SIDE, depth, STEP_ROWS), jnp.bfloat16),
             pltpu.VMEM((SIDE, devices, 2 * STEP_ROWS), jnp.bfloat16),
             pltpu.VMEM((SIDE, 4 * BOX_DEV, 2 * STEP_ROWS), jnp.bfloat16),
             pltpu.VMEM((4 * BOX_DEV, devices), jnp.float32),

time: 139 us -> 137 us (0.986)
  Pallas kernels: 36.3 us -> 34.2 us
    pallas_call x1, Pallas kernels: 15 us -> 13 us  [gather(): pl.pallas_call(gather_kernel, in_specs=[pl.BlockSpec(memory_space=pltpu.S...]
where the time goes in v6:
time: 137 us; the launch traced here: 136 us
  blocking collectives  43.7 us (32%)
  Pallas kernels  34.2 us (25%)
  starting transfers between devices  33.3 us (24%)
  waiting for transfers between devices  11.1 us (8%)
  other arithmetic  10.4 us (8%)
  local copies, waits for them, and re-layouts  2.12 us (2%)
    all_to_all x2, blocking collectives, swapped(): return lax.all_to_all(blocks, AXES, split_axis=0, concat_axis=0, tiled=True)  43.7 us
    ppermute x12, starting transfers between devices, shifted(): return lax.ppermute(face, axis, pairs)  33.3 us
    pallas_call x1, Pallas kernels, gather(): pl.pallas_call(gather_kernel, in_specs=[pl.BlockSpec(memory_space=pltpu.S...  13 us
    ppermute x12, waiting for transfers between devices, shifted(): return lax.ppermute(face, axis, pairs)  11.1 us
    sort x1, other arithmetic, body(): lax.sort((keys, *planes[:3], planes[4]), num_keys=1, is_stable=False)  10 us
    pallas_call x1, Pallas kernels, scatter(): pl.pallas_call(scatter_kernel, in_specs=[pl.BlockSpec(memory_space=pltpu....  9.79 us
    pallas_call x1, Pallas kernels, pack(): pl.pallas_call(pack_kernel, in_specs=[pl.BlockSpec(memory_space=pltpu.HBM...  8.73 us
  transfers between devices with their start and end apart: 12, of which 3 were waited for; matrix products, arithmetic and copies ran while one was open for 0% of the time, Pallas kernels for 0%

profile of v6, /device:TPU:1, one launch (start us, length us, event | category | flops | bytes accessed | tf_op | source)
XLA Modules:
  0.0 135.7 jit_solution(11292435096187418487)
XLA Ops:
  0.7 8.7 %pack_rows.1 = f32[128,8,128]{2,1,0:T(8,128)} custom-call(f32[3,8192]{1,0:T(4,128)} %refs_0_.1, f32[1,8192]{1,0:T(1,128)} %bitcast.55, s32[1,8192]{1,0:T(1,128)} %bitcast.56, s32[1,8192]{1,0:T(1,128)} %bitcast.57, s32[1,8192]{1,0:T(1,128)} %bitcast.58, s32[1,8192]{1,0:T(1,128)} %bitcast.59), custom_call_target="tpu_custom_call" | custom-call | tf_op jit(solution)/shard_map/pack_rows/pallas_call | solution.py:117
  9.4 24.8 %all_to_all.10 = f32[128,8,128]{2,1,0:T(8,128)S(1)} all-to-all(f32[128,8,128]{2,1,0:T(8,128)} %pack_rows.1), channel_id=1, replica_groups=mesh['gx'=8,'gy'=16] {'gx','gy'}, dimensions={0} | all-to-all | bytes 1048576 | tf_op jit(solution)/shard_map/all_to_all | solution.py:491
  34.7 10.0 %sort.33 = (s32[16384]{0:T(1024)S(1)}, f32[16384]{0:T(1024)S(1)}, f32[16384]{0:T(1024)S(1)}, f32[16384]{0:T(1024)S(1)}, f32[16384]{0:T(1024)S(1)}) sort(s32[16384]{0:T(1024)S(1)} %bitcast.50, f32[16384]{0:T(1024)S(1)} %bitcast.54, f32[16384]{0:T(1024)S(1)} %bitcast.53, f32[16384]{0:T(1024)S(1)} %bitcast.52, f32[16384]{0:T(1024)S(1)} %bitcast.51), dimensions={0}, to_apply=%region_0.0 | sort | flops 229376 | bytes 655360 | tf_op jit(solution)/shard_map/sort | solution.py:522
  44.7 1.3 slice_reduce_fusion.1
  46.0 9.8 %scatter_rows.1 = (f32[3,512,256]{2,1,0:T(8,128)S(1)}, f32[6,512,256]{2,1,0:T(8,128)S(1)}, f32[3,512,256]{2,1,0:T(8,128)S(1)}, f32[512,256]{1,0:T(8,128)S(1)}, f...) custom-call(s32[2,32]{1,0:T(2,128)S(1)} %add_shift-right-arithmetic_, ...), custom_call_target="tpu_custom_call" | custom-call | tf_op jit(solution)/shard_map/scatter_rows/pallas_call | solution.py:257
  55.8 5.7 %collective-permute-start.2 = (f32[3,32,256]{2,1,0:T(8,128)S(1)}, f32[3,32,256]{2,1,0:T(8,128)S(1)}, u32[]{:S(2)}, u32[]{:S(2)}) collective-permute-start(f32[3,32,256]{2,1,0:T(8,128)S(1)} %get-tuple-element.37), channel_id=1, source_target_pairs={{0,16},{16,32},{32,48},{48,64},{64,80},{80,96},{96,112},{1,17},{17... | collective-permute-start | bytes 294920 | tf_op jit(solution)/shard_map/ppermute | solution.py:348
  61.5 1.9 %collective-permute-start.3 = (f32[3,32,256]{2,1,0:T(8,128)S(1)}, f32[3,32,256]{2,1,0:T(8,128)S(1)}, u32[]{:S(2)}, u32[]{:S(2)}) collective-permute-start(f32[3,32,256]{2,1,0:T(8,128)S(1)} %get-tuple-element.38), channel_id=1, source_target_pairs={{16,0},{32,16},{48,32},{64,48},{80,64},{96,80},{112,96},{17,1},{33... | collective-permute-start | bytes 294920 | tf_op jit(solution)/shard_map/ppermute | solution.py:348
  63.5 1.3 collective-permute-start
  64.8 1.3 collective-permute-start.1
  66.1 3.5 %collective-permute-done.1.north = f32[3,16,256]{2,1,0:T(8,128)S(1)} collective-permute-done((f32[3,16,256]{2,1,0:T(8,128)S(1)}, f32[3,16,256]{2,1,0:T(8,128)S(1)}, u32[]{:S(2)}, u32[]{:S(2)}) %collective-permute-start.1) | collective-permute-done | bytes 49184 | tf_op jit(solution)/shard_map/ppermute | solution.py:348
  69.6 1.3 sweep_cells.2
  70.9 4.8 %collective-permute-start.6 = (f32[3,32,256]{2,1,0:T(8,128)S(1)}, f32[3,32,256]{2,1,0:T(8,128)S(1)}, u32[]{:S(2)}, u32[]{:S(2)}) collective-permute-start(f32[3,32,256]{2,1,0:T(8,128)S(1)} %get-tuple-element.42), channel_id=1, source_target_pairs={{0,16},{16,32},{32,48},{48,64},{64,80},{80,96},{96,112},{1,17},{17... | collective-permute-start | bytes 294920 | tf_op jit(solution)/shard_map/ppermute | solution.py:348
  75.7 1.9 %collective-permute-start.7 = (f32[3,32,256]{2,1,0:T(8,128)S(1)}, f32[3,32,256]{2,1,0:T(8,128)S(1)}, u32[]{:S(2)}, u32[]{:S(2)}) collective-permute-start(f32[3,32,256]{2,1,0:T(8,128)S(1)} %get-tuple-element.43), channel_id=1, source_target_pairs={{16,0},{32,16},{48,32},{64,48},{80,64},{96,80},{112,96},{17,1},{33... | collective-permute-start | bytes 294920 | tf_op jit(solution)/shard_map/ppermute | solution.py:348
  77.7 1.3 collective-permute-start.4
  79.0 1.3 collective-permute-start.5
  80.3 3.7 %collective-permute-done.5.north = f32[3,16,256]{2,1,0:T(8,128)S(1)} collective-permute-done((f32[3,16,256]{2,1,0:T(8,128)S(1)}, f32[3,16,256]{2,1,0:T(8,128)S(1)}, u32[]{:S(2)}, u32[]{:S(2)}) %collective-permute-start.5) | collective-permute-done | bytes 49184 | tf_op jit(solution)/shard_map/ppermute | solution.py:348
  84.0 1.4 %sweep_cells.3 = (f32[3,16,32,256]{3,2,1,0:T(8,128)S(1)}, f32[3,32,256]{2,1,0:T(8,128)S(1)}, f32[3,32,256]{2,1,0:T(8,128)S(1)}, f32[3,16,256]{2,1,0:T(8,128)S(1)}, f32[3,16,256]{2,1,0:T(8,128)S(1)}) custom-call(f32[3,16,32,256]{3,2,1,0:T(8,128)S(1)} %bitcast.32, f32[6,16,32,256]{3,2,1,0:T(8,128)S(1)} %bitcast.28, f32[3,16,32,256]{3,2,1,0:T(8,128)S(1)} %bitcast.35, ...), custom_call_target="tpu_custom_call" | custom-call | tf_op jit(solution)/shard_map/sweep_cells/pallas_call | solution.py:336
  85.4 4.9 %collective-permute-start.10 = (f32[3,32,256]{2,1,0:T(8,128)S(1)}, f32[3,32,256]{2,1,0:T(8,128)S(1)}, u32[]{:S(2)}, u32[]{:S(2)}) collective-permute-start(f32[3,32,256]{2,1,0:T(8,128)S(1)} %get-tuple-element.47), channel_id=1, source_target_pairs={{0,16},{16,32},{32,48},{48,64},{64,80},{80,96},{96,112},{1,17},{17... | collective-permute-start | bytes 294920 | tf_op jit(solution)/shard_map/ppermute | solution.py:348
  90.3 1.9 %collective-permute-start.11 = (f32[3,32,256]{2,1,0:T(8,128)S(1)}, f32[3,32,256]{2,1,0:T(8,128)S(1)}, u32[]{:S(2)}, u32[]{:S(2)}) collective-permute-start(f32[3,32,256]{2,1,0:T(8,128)S(1)} %get-tuple-element.48), channel_id=1, source_target_pairs={{16,0},{32,16},{48,32},{64,48},{80,64},{96,80},{112,96},{17,1},{33... | collective-permute-start | bytes 294920 | tf_op jit(solution)/shard_map/ppermute | solution.py:348
  92.3 5.7 %collective-permute-start.8 = (f32[3,16,256]{2,1,0:T(8,128)S(1)}, f32[3,16,256]{2,1,0:T(8,128)S(1)}, u32[]{:S(2)}, u32[]{:S(2)}) collective-permute-start(f32[3,16,256]{2,1,0:T(8,128)S(1)} %get-tuple-element.45), channel_id=1, source_target_pairs={{0,1},{1,2},{2,3},{3,4},{4,5},{5,6},{6,7},{7,8},{8,9},{9,10},{10,1... | collective-permute-start | bytes 147464 | tf_op jit(solution)/shard_map/ppermute | solution.py:348
  97.9 1.3 collective-permute-start.9
  99.2 3.8 %collective-permute-done.9.refs_7_ = f32[3,16,256]{2,1,0:T(8,128)S(1)} collective-permute-done((f32[3,16,256]{2,1,0:T(8,128)S(1)}, f32[3,16,256]{2,1,0:T(8,128)S(1)}, u32[]{:S(2)}, u32[]{:S(2)}) %collective-permute-start.9) | collective-permute-done | bytes 49184 | tf_op jit(solution)/shard_map/ppermute | solution.py:348
  103.1 13.0 %gather_rows.1 = (f32[3,512,256]{2,1,0:T(8,128)}, f32[128,2,128]{2,1,0:T(2,128)S(1)}) custom-call(s32[2,32]{1,0:T(2,128)S(1)} %add_shift-right-arithmetic_fusion.refs_0_, f32[3,16,32,256]{3,2,1,0:T(8,128)S(1)} %bitcast.33, f32[6,16,32,256]{3,2,1,0:T(8,128)S(1)} %bitcast.29, f32[3,16,32,256]{3,2,1,0:T(8,128)S(1)} %bitcast.36, f32[16,32,256]{2,1,0:T(8,128)S(1)} %bitcast.39, ...), custom_call_target="tpu_custom_call" | custom-call | tf_op jit(solution)/shard_map/gather_rows/pallas_call | solution.py:468
  116.1 18.8 %all_to_all.11 = f32[128,2,128]{2,1,0:T(2,128)S(1)} all-to-all(f32[128,2,128]{2,1,0:T(2,128)S(1)} %get-tuple-element.51), channel_id=1, replica_groups=mesh['gx'=8,'gy'=16] {'gx','gy'}, dimensions={0} | all-to-all | bytes 262144 | tf_op jit(solution)/shard_map/all_to_all | solution.py:491
  (18 shorter events, 1.3 us)
Async XLA Ops:
  0.6 45.4 %copy-start = (f32[3,16,32,256]{3,2,1,0:T(8,128)S(1)}, f32[3,16,32,256]{3,2,1,0:T(8,128)}, u32[]{:S(2)}) copy-start(f32[3,16,32,256]{3,2,1,0:T(8,128)} %param.16) | copy-start | bytes 4718596
  0.6 45.4 %copy-start.1 = (f32[16,32,256]{2,1,0:T(8,128)S(1)}, f32[16,32,256]{2,1,0:T(8,128)}, u32[]{:S(2)}) copy-start(f32[16,32,256]{2,1,0:T(8,128)} %param.15) | copy-start | bytes 1572868
  55.8 13.8 %collective-permute-start.2 = (f32[3,32,256]{2,1,0:T(8,128)S(1)}, f32[3,32,256]{2,1,0:T(8,128)S(1)}, u32[]{:S(2)}, u32[]{:S(2)}) collective-permute-start(f32[3,32,256]{2,1,0:T(8,128)S(1)} %get-tuple-element.37), channel_id=1, source_target_pairs={{0,16},{16,32},{32,48},{48,64},{64,80},{80,96},{96,112},{1,17},{17... | collective-permute-start | bytes 294920 | tf_op jit(solution)/shard_map/ppermute | solution.py:348
  61.5 8.1 %collective-permute-start.3 = (f32[3,32,256]{2,1,0:T(8,128)S(1)}, f32[3,32,256]{2,1,0:T(8,128)S(1)}, u32[]{:S(2)}, u32[]{:S(2)}) collective-permute-start(f32[3,32,256]{2,1,0:T(8,128)S(1)} %get-tuple-element.38), channel_id=1, source_target_pairs={{16,0},{32,16},{48,32},{64,48},{80,64},{96,80},{112,96},{17,1},{33... | collective-permute-start | bytes 294920 | tf_op jit(solution)/shard_map/ppermute | solution.py:348
  63.5 2.6 %collective-permute-start = (f32[3,16,256]{2,1,0:T(8,128)S(1)}, f32[3,16,256]{2,1,0:T(8,128)S(1)}, u32[]{:S(2)}, u32[]{:S(2)}) collective-permute-start(f32[3,16,256]{2,1,0:T(8,128)S(1)} %get-tuple-element.35), channel_id=1, source_target_pairs={{0,1},{1,2},{2,3},{3,4},{4,5},{5,6},{6,7},{7,8},{8,9},{9,10},{10,1... | collective-permute-start | bytes 147464 | tf_op jit(solution)/shard_map/ppermute | solution.py:348
  64.8 4.8 %collective-permute-start.1 = (f32[3,16,256]{2,1,0:T(8,128)S(1)}, f32[3,16,256]{2,1,0:T(8,128)S(1)}, u32[]{:S(2)}, u32[]{:S(2)}) collective-permute-start(f32[3,16,256]{2,1,0:T(8,128)S(1)} %get-tuple-element.36), channel_id=1, source_target_pairs={{1,0},{2,1},{3,2},{4,3},{5,4},{6,5},{7,6},{8,7},{9,8},{10,9},{11,1... | collective-permute-start | bytes 147464 | tf_op jit(solution)/shard_map/ppermute | solution.py:348
  70.9 13.1 %collective-permute-start.6 = (f32[3,32,256]{2,1,0:T(8,128)S(1)}, f32[3,32,256]{2,1,0:T(8,128)S(1)}, u32[]{:S(2)}, u32[]{:S(2)}) collective-permute-start(f32[3,32,256]{2,1,0:T(8,128)S(1)} %get-tuple-element.42), channel_id=1, source_target_pairs={{0,16},{16,32},{32,48},{48,64},{64,80},{80,96},{96,112},{1,17},{17... | collective-permute-start | bytes 294920 | tf_op jit(solution)/shard_map/ppermute | solution.py:348
  75.7 8.3 %collective-permute-start.7 = (f32[3,32,256]{2,1,0:T(8,128)S(1)}, f32[3,32,256]{2,1,0:T(8,128)S(1)}, u32[]{:S(2)}, u32[]{:S(2)}) collective-permute-start(f32[3,32,256]{2,1,0:T(8,128)S(1)} %get-tuple-element.43), channel_id=1, source_target_pairs={{16,0},{32,16},{48,32},{64,48},{80,64},{96,80},{112,96},{17,1},{33... | collective-permute-start | bytes 294920 | tf_op jit(solution)/shard_map/ppermute | solution.py:348
  77.7 2.6 %collective-permute-start.4 = (f32[3,16,256]{2,1,0:T(8,128)S(1)}, f32[3,16,256]{2,1,0:T(8,128)S(1)}, u32[]{:S(2)}, u32[]{:S(2)}) collective-permute-start(f32[3,16,256]{2,1,0:T(8,128)S(1)} %get-tuple-element.40), channel_id=1, source_target_pairs={{0,1},{1,2},{2,3},{3,4},{4,5},{5,6},{6,7},{7,8},{8,9},{9,10},{10,1... | collective-permute-start | bytes 147464 | tf_op jit(solution)/shard_map/ppermute | solution.py:348
  79.0 5.0 %collective-permute-start.5 = (f32[3,16,256]{2,1,0:T(8,128)S(1)}, f32[3,16,256]{2,1,0:T(8,128)S(1)}, u32[]{:S(2)}, u32[]{:S(2)}) collective-permute-start(f32[3,16,256]{2,1,0:T(8,128)S(1)} %get-tuple-element.41), channel_id=1, source_target_pairs={{1,0},{2,1},{3,2},{4,3},{5,4},{6,5},{7,6},{8,7},{9,8},{10,9},{11,1... | collective-permute-start | bytes 147464 | tf_op jit(solution)/shard_map/ppermute | solution.py:348
  85.4 17.6 %collective-permute-start.10 = (f32[3,32,256]{2,1,0:T(8,128)S(1)}, f32[3,32,256]{2,1,0:T(8,128)S(1)}, u32[]{:S(2)}, u32[]{:S(2)}) collective-permute-start(f32[3,32,256]{2,1,0:T(8,128)S(1)} %get-tuple-element.47), channel_id=1, source_target_pairs={{0,16},{16,32},{32,48},{48,64},{64,80},{80,96},{96,112},{1,17},{17... | collective-permute-start | bytes 294920 | tf_op jit(solution)/shard_map/ppermute | solution.py:348
  90.3 12.7 %collective-permute-start.11 = (f32[3,32,256]{2,1,0:T(8,128)S(1)}, f32[3,32,256]{2,1,0:T(8,128)S(1)}, u32[]{:S(2)}, u32[]{:S(2)}) collective-permute-start(f32[3,32,256]{2,1,0:T(8,128)S(1)} %get-tuple-element.48), channel_id=1, source_target_pairs={{16,0},{32,16},{48,32},{64,48},{80,64},{96,80},{112,96},{17,1},{33... | collective-permute-start | bytes 294920 | tf_op jit(solution)/shard_map/ppermute | solution.py:348
  92.3 7.0 %collective-permute-start.8 = (f32[3,16,256]{2,1,0:T(8,128)S(1)}, f32[3,16,256]{2,1,0:T(8,128)S(1)}, u32[]{:S(2)}, u32[]{:S(2)}) collective-permute-start(f32[3,16,256]{2,1,0:T(8,128)S(1)} %get-tuple-element.45), channel_id=1, source_target_pairs={{0,1},{1,2},{2,3},{3,4},{4,5},{5,6},{6,7},{7,8},{8,9},{9,10},{10,1... | collective-permute-start | bytes 147464 | tf_op jit(solution)/shard_map/ppermute | solution.py:348
  97.9 5.1 %collective-permute-start.9 = (f32[3,16,256]{2,1,0:T(8,128)S(1)}, f32[3,16,256]{2,1,0:T(8,128)S(1)}, u32[]{:S(2)}, u32[]{:S(2)}) collective-permute-start(f32[3,16,256]{2,1,0:T(8,128)S(1)} %get-tuple-element.46), channel_id=1, source_target_pairs={{1,0},{2,1},{3,2},{4,3},{5,4},{6,5},{7,6},{8,7},{9,8},{10,9},{11,1... | collective-permute-start | bytes 147464 | tf_op jit(solution)/shard_map/ppermute | solution.py:348

commit v7 on v6

--- a/solution.py
+++ b/solution.py
@@ -371,7 +371,6 @@
     group = STEP_ROWS // width
     step = STEP_ROWS
     total[...] = jnp.zeros_like(total)
-    right[...] = jnp.zeros_like(right)
 
     def rows(i):
         return [pl.ds(i * group + q, 1) for q in range(group)]
@@ -452,7 +451,7 @@
         for b in range(SIDE):
             spread(own[b], b, finals[b])
         parts = [dot_last(right[b], left[b]) for b in range(SIDE)]
-        total[...] += sum(parts[1:], parts[0])
+        total[: 3 * BOX_DEV, :] += sum(parts[1:], parts[0])
         return 0
 
     lax.fori_loop(filled(ends), lines // group // SIDE, chunks, 0)
@@ -478,7 +477,7 @@
             pltpu.VMEM(cube, jnp.float32),
             pltpu.VMEM((SIDE, depth, STEP_ROWS), jnp.bfloat16),
             pltpu.VMEM((SIDE, devices, 2 * STEP_ROWS), jnp.bfloat16),
-            pltpu.VMEM((SIDE, 4 * BOX_DEV, 2 * STEP_ROWS), jnp.bfloat16),
+            pltpu.VMEM((SIDE, 3 * BOX_DEV, 2 * STEP_ROWS), jnp.bfloat16),
             pltpu.VMEM((4 * BOX_DEV, devices), jnp.float32),
             pltpu.SemaphoreType.DMA,
         ],

time: 137 us -> 137 us (level)
  transfers between devices with their start and end apart: 12 -> 12, of which waited for: 3 -> 4; matrix products, arithmetic and copies ran while one was open for 0% -> 0% of each run, Pallas kernels for 0% -> 0%
where the time goes in v7:
time: 137 us
  blocking collectives  44.7 us (33%)
  Pallas kernels  34.5 us (25%)
  starting transfers between devices  32.2 us (24%)
  waiting for transfers between devices  12.2 us (9%)
  other arithmetic  10.4 us (8%)
  local copies, waits for them, and re-layouts  2.12 us (2%)
    all_to_all x2, blocking collectives, swapped(): return lax.all_to_all(blocks, AXES, split_axis=0, concat_axis=0, tiled=True)  44.7 us
    ppermute x12, starting transfers between devices, shifted(): return lax.ppermute(face, axis, pairs)  32.2 us
    pallas_call x1, Pallas kernels, gather(): pl.pallas_call(gather_kernel, in_specs=[pl.BlockSpec(memory_space=pltpu.S...  13.3 us
    ppermute x12, waiting for transfers between devices, shifted(): return lax.ppermute(face, axis, pairs)  12.2 us
    sort x1, other arithmetic, body(): lax.sort((keys, *planes[:3], planes[4]), num_keys=1, is_stable=False)  10 us
    pallas_call x1, Pallas kernels, scatter(): pl.pallas_call(scatter_kernel, in_specs=[pl.BlockSpec(memory_space=pltpu....  9.79 us
    pallas_call x1, Pallas kernels, pack(): pl.pallas_call(pack_kernel, in_specs=[pl.BlockSpec(memory_space=pltpu.HBM...  8.73 us
  transfers between devices with their start and end apart: 12, of which 4 were waited for; matrix products, arithmetic and copies ran while one was open for 0% of the time, Pallas kernels for 0%

profile of v7, /device:TPU:1, one launch (start us, length us, event | category | flops | bytes accessed | tf_op | source)
XLA Modules:
  0.0 137.0 jit_solution(16494664834742034462)
XLA Ops:
  0.7 8.7 %pack_rows.1 = f32[128,8,128]{2,1,0:T(8,128)} custom-call(f32[3,8192]{1,0:T(4,128)} %refs_0_.1, f32[1,8192]{1,0:T(1,128)} %bitcast.55, s32[1,8192]{1,0:T(1,128)} %bitcast.56, s32[1,8192]{1,0:T(1,128)} %bitcast.57, s32[1,8192]{1,0:T(1,128)} %bitcast.58, s32[1,8192]{1,0:T(1,128)} %bitcast.59), custom_call_target="tpu_custom_call" | custom-call | tf_op jit(solution)/shard_map/pack_rows/pallas_call | solution.py:117
  9.4 24.8 %all_to_all.10 = f32[128,8,128]{2,1,0:T(8,128)S(1)} all-to-all(f32[128,8,128]{2,1,0:T(8,128)} %pack_rows.1), channel_id=1, replica_groups=mesh['gx'=8,'gy'=16] {'gx','gy'}, dimensions={0} | all-to-all | bytes 1048576 | tf_op jit(solution)/shard_map/all_to_all | solution.py:490
  34.7 10.0 %sort.33 = (s32[16384]{0:T(1024)S(1)}, f32[16384]{0:T(1024)S(1)}, f32[16384]{0:T(1024)S(1)}, f32[16384]{0:T(1024)S(1)}, f32[16384]{0:T(1024)S(1)}) sort(s32[16384]{0:T(1024)S(1)} %bitcast.50, f32[16384]{0:T(1024)S(1)} %bitcast.54, f32[16384]{0:T(1024)S(1)} %bitcast.53, f32[16384]{0:T(1024)S(1)} %bitcast.52, f32[16384]{0:T(1024)S(1)} %bitcast.51), dimensions={0}, to_apply=%region_0.0 | sort | flops 229376 | bytes 655360 | tf_op jit(solution)/shard_map/sort | solution.py:521
  44.7 1.3 slice_reduce_fusion.1
  46.0 9.8 %scatter_rows.1 = (f32[3,512,256]{2,1,0:T(8,128)S(1)}, f32[6,512,256]{2,1,0:T(8,128)S(1)}, f32[3,512,256]{2,1,0:T(8,128)S(1)}, f32[512,256]{1,0:T(8,128)S(1)}, f...) custom-call(s32[2,32]{1,0:T(2,128)S(1)} %add_shift-right-arithmetic_, ...), custom_call_target="tpu_custom_call" | custom-call | tf_op jit(solution)/shard_map/scatter_rows/pallas_call | solution.py:257
  55.8 1.9 %collective-permute-start.2 = (f32[3,32,256]{2,1,0:T(8,128)S(1)}, f32[3,32,256]{2,1,0:T(8,128)S(1)}, u32[]{:S(2)}, u32[]{:S(2)}) collective-permute-start(f32[3,32,256]{2,1,0:T(8,128)S(1)} %get-tuple-element.37), channel_id=1, source_target_pairs={{0,16},{16,32},{32,48},{48,64},{64,80},{80,96},{96,112},{1,17},{17... | collective-permute-start | bytes 294920 | tf_op jit(solution)/shard_map/ppermute | solution.py:348
  57.7 2.4 %collective-permute-start.3 = (f32[3,32,256]{2,1,0:T(8,128)S(1)}, f32[3,32,256]{2,1,0:T(8,128)S(1)}, u32[]{:S(2)}, u32[]{:S(2)}) collective-permute-start(f32[3,32,256]{2,1,0:T(8,128)S(1)} %get-tuple-element.38), channel_id=1, source_target_pairs={{16,0},{32,16},{48,32},{64,48},{80,64},{96,80},{112,96},{17,1},{33... | collective-permute-start | bytes 294920 | tf_op jit(solution)/shard_map/ppermute | solution.py:348
  60.1 3.2 %collective-permute-start = (f32[3,16,256]{2,1,0:T(8,128)S(1)}, f32[3,16,256]{2,1,0:T(8,128)S(1)}, u32[]{:S(2)}, u32[]{:S(2)}) collective-permute-start(f32[3,16,256]{2,1,0:T(8,128)S(1)} %get-tuple-element.35), channel_id=1, source_target_pairs={{0,1},{1,2},{2,3},{3,4},{4,5},{5,6},{6,7},{7,8},{8,9},{9,10},{10,1... | collective-permute-start | bytes 147464 | tf_op jit(solution)/shard_map/ppermute | solution.py:348
  63.4 1.3 collective-permute-start.1
  64.8 4.7 %collective-permute-done.1.north = f32[3,16,256]{2,1,0:T(8,128)S(1)} collective-permute-done((f32[3,16,256]{2,1,0:T(8,128)S(1)}, f32[3,16,256]{2,1,0:T(8,128)S(1)}, u32[]{:S(2)}, u32[]{:S(2)}) %collective-permute-start.1) | collective-permute-done | bytes 49184 | tf_op jit(solution)/shard_map/ppermute | solution.py:348
  69.5 1.3 sweep_cells.2
  70.9 3.8 %collective-permute-start.6 = (f32[3,32,256]{2,1,0:T(8,128)S(1)}, f32[3,32,256]{2,1,0:T(8,128)S(1)}, u32[]{:S(2)}, u32[]{:S(2)}) collective-permute-start(f32[3,32,256]{2,1,0:T(8,128)S(1)} %get-tuple-element.42), channel_id=1, source_target_pairs={{0,16},{16,32},{32,48},{48,64},{64,80},{80,96},{96,112},{1,17},{17... | collective-permute-start | bytes 294920 | tf_op jit(solution)/shard_map/ppermute | solution.py:348
  74.7 1.9 %collective-permute-start.7 = (f32[3,32,256]{2,1,0:T(8,128)S(1)}, f32[3,32,256]{2,1,0:T(8,128)S(1)}, u32[]{:S(2)}, u32[]{:S(2)}) collective-permute-start(f32[3,32,256]{2,1,0:T(8,128)S(1)} %get-tuple-element.43), channel_id=1, source_target_pairs={{16,0},{32,16},{48,32},{64,48},{80,64},{96,80},{112,96},{17,1},{33... | collective-permute-start | bytes 294920 | tf_op jit(solution)/shard_map/ppermute | solution.py:348
  76.6 3.6 %collective-permute-start.4 = (f32[3,16,256]{2,1,0:T(8,128)S(1)}, f32[3,16,256]{2,1,0:T(8,128)S(1)}, u32[]{:S(2)}, u32[]{:S(2)}) collective-permute-start(f32[3,16,256]{2,1,0:T(8,128)S(1)} %get-tuple-element.40), channel_id=1, source_target_pairs={{0,1},{1,2},{2,3},{3,4},{4,5},{5,6},{6,7},{7,8},{8,9},{9,10},{10,1... | collective-permute-start | bytes 147464 | tf_op jit(solution)/shard_map/ppermute | solution.py:348
  80.2 1.3 collective-permute-start.5
  81.5 3.5 %collective-permute-done.5.north = f32[3,16,256]{2,1,0:T(8,128)S(1)} collective-permute-done((f32[3,16,256]{2,1,0:T(8,128)S(1)}, f32[3,16,256]{2,1,0:T(8,128)S(1)}, u32[]{:S(2)}, u32[]{:S(2)}) %collective-permute-start.5) | collective-permute-done | bytes 49184 | tf_op jit(solution)/shard_map/ppermute | solution.py:348
  85.1 1.4 %sweep_cells.3 = (f32[3,16,32,256]{3,2,1,0:T(8,128)S(1)}, f32[3,32,256]{2,1,0:T(8,128)S(1)}, f32[3,32,256]{2,1,0:T(8,128)S(1)}, f32[3,16,256]{2,1,0:T(8,128)S(1)}, f32[3,16,256]{2,1,0:T(8,128)S(1)}) custom-call(f32[3,16,32,256]{3,2,1,0:T(8,128)S(1)} %bitcast.32, f32[6,16,32,256]{3,2,1,0:T(8,128)S(1)} %bitcast.28, f32[3,16,32,256]{3,2,1,0:T(8,128)S(1)} %bitcast.35, ...), custom_call_target="tpu_custom_call" | custom-call | tf_op jit(solution)/shard_map/sweep_cells/pallas_call | solution.py:336
  86.5 5.1 %collective-permute-start.10 = (f32[3,32,256]{2,1,0:T(8,128)S(1)}, f32[3,32,256]{2,1,0:T(8,128)S(1)}, u32[]{:S(2)}, u32[]{:S(2)}) collective-permute-start(f32[3,32,256]{2,1,0:T(8,128)S(1)} %get-tuple-element.47), channel_id=1, source_target_pairs={{0,16},{16,32},{32,48},{48,64},{64,80},{80,96},{96,112},{1,17},{17... | collective-permute-start | bytes 294920 | tf_op jit(solution)/shard_map/ppermute | solution.py:348
  91.6 1.9 %collective-permute-start.11 = (f32[3,32,256]{2,1,0:T(8,128)S(1)}, f32[3,32,256]{2,1,0:T(8,128)S(1)}, u32[]{:S(2)}, u32[]{:S(2)}) collective-permute-start(f32[3,32,256]{2,1,0:T(8,128)S(1)} %get-tuple-element.48), channel_id=1, source_target_pairs={{16,0},{32,16},{48,32},{64,48},{80,64},{96,80},{112,96},{17,1},{33... | collective-permute-start | bytes 294920 | tf_op jit(solution)/shard_map/ppermute | solution.py:348
  93.5 4.4 %collective-permute-start.8 = (f32[3,16,256]{2,1,0:T(8,128)S(1)}, f32[3,16,256]{2,1,0:T(8,128)S(1)}, u32[]{:S(2)}, u32[]{:S(2)}) collective-permute-start(f32[3,16,256]{2,1,0:T(8,128)S(1)} %get-tuple-element.45), channel_id=1, source_target_pairs={{0,1},{1,2},{2,3},{3,4},{4,5},{5,6},{6,7},{7,8},{8,9},{9,10},{10,1... | collective-permute-start | bytes 147464 | tf_op jit(solution)/shard_map/ppermute | solution.py:348
  97.9 1.3 collective-permute-start.9
  99.2 3.8 %collective-permute-done.9.refs_7_ = f32[3,16,256]{2,1,0:T(8,128)S(1)} collective-permute-done((f32[3,16,256]{2,1,0:T(8,128)S(1)}, f32[3,16,256]{2,1,0:T(8,128)S(1)}, u32[]{:S(2)}, u32[]{:S(2)}) %collective-permute-start.9) | collective-permute-done | bytes 49184 | tf_op jit(solution)/shard_map/ppermute | solution.py:348
  103.1 13.3 %gather_rows.1 = (f32[3,512,256]{2,1,0:T(8,128)}, f32[128,2,128]{2,1,0:T(2,128)S(1)}) custom-call(s32[2,32]{1,0:T(2,128)S(1)} %add_shift-right-arithmetic_fusion.refs_0_, f32[3,16,32,256]{3,2,1,0:T(8,128)S(1)} %bitcast.33, f32[6,16,32,256]{3,2,1,0:T(8,128)S(1)} %bitcast.29, f32[3,16,32,256]{3,2,1,0:T(8,128)S(1)} %bitcast.36, f32[16,32,256]{2,1,0:T(8,128)S(1)} %bitcast.39, ...), custom_call_target="tpu_custom_call" | custom-call | tf_op jit(solution)/shard_map/gather_rows/pallas_call | solution.py:467
  116.3 19.8 %all_to_all.11 = f32[128,2,128]{2,1,0:T(2,128)S(1)} all-to-all(f32[128,2,128]{2,1,0:T(2,128)S(1)} %get-tuple-element.51), channel_id=1, replica_groups=mesh['gx'=8,'gy'=16] {'gx','gy'}, dimensions={0} | all-to-all | bytes 262144 | tf_op jit(solution)/shard_map/all_to_all | solution.py:490
  (18 shorter events, 1.4 us)
Async XLA Ops:
  0.6 45.4 %copy-start = (f32[3,16,32,256]{3,2,1,0:T(8,128)S(1)}, f32[3,16,32,256]{3,2,1,0:T(8,128)}, u32[]{:S(2)}) copy-start(f32[3,16,32,256]{3,2,1,0:T(8,128)} %param.16) | copy-start | bytes 4718596
  0.6 45.4 %copy-start.1 = (f32[16,32,256]{2,1,0:T(8,128)S(1)}, f32[16,32,256]{2,1,0:T(8,128)}, u32[]{:S(2)}) copy-start(f32[16,32,256]{2,1,0:T(8,128)} %param.15) | copy-start | bytes 1572868
  55.8 13.7 %collective-permute-start.2 = (f32[3,32,256]{2,1,0:T(8,128)S(1)}, f32[3,32,256]{2,1,0:T(8,128)S(1)}, u32[]{:S(2)}, u32[]{:S(2)}) collective-permute-start(f32[3,32,256]{2,1,0:T(8,128)S(1)} %get-tuple-element.37), channel_id=1, source_target_pairs={{0,16},{16,32},{32,48},{48,64},{64,80},{80,96},{96,112},{1,17},{17... | collective-permute-start | bytes 294920 | tf_op jit(solution)/shard_map/ppermute | solution.py:348
  57.7 11.8 %collective-permute-start.3 = (f32[3,32,256]{2,1,0:T(8,128)S(1)}, f32[3,32,256]{2,1,0:T(8,128)S(1)}, u32[]{:S(2)}, u32[]{:S(2)}) collective-permute-start(f32[3,32,256]{2,1,0:T(8,128)S(1)} %get-tuple-element.38), channel_id=1, source_target_pairs={{16,0},{32,16},{48,32},{64,48},{80,64},{96,80},{112,96},{17,1},{33... | collective-permute-start | bytes 294920 | tf_op jit(solution)/shard_map/ppermute | solution.py:348
  60.1 4.7 %collective-permute-start = (f32[3,16,256]{2,1,0:T(8,128)S(1)}, f32[3,16,256]{2,1,0:T(8,128)S(1)}, u32[]{:S(2)}, u32[]{:S(2)}) collective-permute-start(f32[3,16,256]{2,1,0:T(8,128)S(1)} %get-tuple-element.35), channel_id=1, source_target_pairs={{0,1},{1,2},{2,3},{3,4},{4,5},{5,6},{6,7},{7,8},{8,9},{9,10},{10,1... | collective-permute-start | bytes 147464 | tf_op jit(solution)/shard_map/ppermute | solution.py:348
  63.4 6.2 %collective-permute-start.1 = (f32[3,16,256]{2,1,0:T(8,128)S(1)}, f32[3,16,256]{2,1,0:T(8,128)S(1)}, u32[]{:S(2)}, u32[]{:S(2)}) collective-permute-start(f32[3,16,256]{2,1,0:T(8,128)S(1)} %get-tuple-element.36), channel_id=1, source_target_pairs={{1,0},{2,1},{3,2},{4,3},{5,4},{6,5},{7,6},{8,7},{9,8},{10,9},{11,1... | collective-permute-start | bytes 147464 | tf_op jit(solution)/shard_map/ppermute | solution.py:348
  70.9 14.2 %collective-permute-start.6 = (f32[3,32,256]{2,1,0:T(8,128)S(1)}, f32[3,32,256]{2,1,0:T(8,128)S(1)}, u32[]{:S(2)}, u32[]{:S(2)}) collective-permute-start(f32[3,32,256]{2,1,0:T(8,128)S(1)} %get-tuple-element.42), channel_id=1, source_target_pairs={{0,16},{16,32},{32,48},{48,64},{64,80},{80,96},{96,112},{1,17},{17... | collective-permute-start | bytes 294920 | tf_op jit(solution)/shard_map/ppermute | solution.py:348
  74.7 10.4 %collective-permute-start.7 = (f32[3,32,256]{2,1,0:T(8,128)S(1)}, f32[3,32,256]{2,1,0:T(8,128)S(1)}, u32[]{:S(2)}, u32[]{:S(2)}) collective-permute-start(f32[3,32,256]{2,1,0:T(8,128)S(1)} %get-tuple-element.43), channel_id=1, source_target_pairs={{16,0},{32,16},{48,32},{64,48},{80,64},{96,80},{112,96},{17,1},{33... | collective-permute-start | bytes 294920 | tf_op jit(solution)/shard_map/ppermute | solution.py:348
  76.6 5.0 %collective-permute-start.4 = (f32[3,16,256]{2,1,0:T(8,128)S(1)}, f32[3,16,256]{2,1,0:T(8,128)S(1)}, u32[]{:S(2)}, u32[]{:S(2)}) collective-permute-start(f32[3,16,256]{2,1,0:T(8,128)S(1)} %get-tuple-element.40), channel_id=1, source_target_pairs={{0,1},{1,2},{2,3},{3,4},{4,5},{5,6},{6,7},{7,8},{8,9},{9,10},{10,1... | collective-permute-start | bytes 147464 | tf_op jit(solution)/shard_map/ppermute | solution.py:348
  80.2 4.8 %collective-permute-start.5 = (f32[3,16,256]{2,1,0:T(8,128)S(1)}, f32[3,16,256]{2,1,0:T(8,128)S(1)}, u32[]{:S(2)}, u32[]{:S(2)}) collective-permute-start(f32[3,16,256]{2,1,0:T(8,128)S(1)} %get-tuple-element.41), channel_id=1, source_target_pairs={{1,0},{2,1},{3,2},{4,3},{5,4},{6,5},{7,6},{8,7},{9,8},{10,9},{11,1... | collective-permute-start | bytes 147464 | tf_op jit(solution)/shard_map/ppermute | solution.py:348
  86.5 16.6 %collective-permute-start.10 = (f32[3,32,256]{2,1,0:T(8,128)S(1)}, f32[3,32,256]{2,1,0:T(8,128)S(1)}, u32[]{:S(2)}, u32[]{:S(2)}) collective-permute-start(f32[3,32,256]{2,1,0:T(8,128)S(1)} %get-tuple-element.47), channel_id=1, source_target_pairs={{0,16},{16,32},{32,48},{48,64},{64,80},{80,96},{96,112},{1,17},{17... | collective-permute-start | bytes 294920 | tf_op jit(solution)/shard_map/ppermute | solution.py:348
  91.6 11.5 %collective-permute-start.11 = (f32[3,32,256]{2,1,0:T(8,128)S(1)}, f32[3,32,256]{2,1,0:T(8,128)S(1)}, u32[]{:S(2)}, u32[]{:S(2)}) collective-permute-start(f32[3,32,256]{2,1,0:T(8,128)S(1)} %get-tuple-element.48), channel_id=1, source_target_pairs={{16,0},{32,16},{48,32},{64,48},{80,64},{96,80},{112,96},{17,1},{33... | collective-permute-start | bytes 294920 | tf_op jit(solution)/shard_map/ppermute | solution.py:348
  93.5 5.7 %collective-permute-start.8 = (f32[3,16,256]{2,1,0:T(8,128)S(1)}, f32[3,16,256]{2,1,0:T(8,128)S(1)}, u32[]{:S(2)}, u32[]{:S(2)}) collective-permute-start(f32[3,16,256]{2,1,0:T(8,128)S(1)} %get-tuple-element.45), channel_id=1, source_target_pairs={{0,1},{1,2},{2,3},{3,4},{4,5},{5,6},{6,7},{7,8},{8,9},{9,10},{10,1... | collective-permute-start | bytes 147464 | tf_op jit(solution)/shard_map/ppermute | solution.py:348
  97.9 5.1 %collective-permute-start.9 = (f32[3,16,256]{2,1,0:T(8,128)S(1)}, f32[3,16,256]{2,1,0:T(8,128)S(1)}, u32[]{:S(2)}, u32[]{:S(2)}) collective-permute-start(f32[3,16,256]{2,1,0:T(8,128)S(1)} %get-tuple-element.46), channel_id=1, source_target_pairs={{1,0},{2,1},{3,2},{4,3},{5,4},{6,5},{7,6},{8,7},{9,8},{10,9},{11,1... | collective-permute-start | bytes 147464 | tf_op jit(solution)/shard_map/ppermute | solution.py:348
